TPU v7x, 512 devices: a whole 4x4x16 slice. The times are simulated.
512 devices in a mesh: video: 16 (over y, z_hi), audio: 8 (over x, core), tp: 4 (over z_lo).
Axes of the slice: x: 4, y: 4, z: 16 (z_hi: 4, z_lo: 4; z = z_hi * 4 + z_lo), core: 2. Of those that a mesh axis runs over, the one named last changes fastest.
Arguments:
- video_query: bfloat16 [81920, 3072], P(('video', 'audio'), 'tp')
- audio_key: bfloat16 [16384, 3072], P(('video', 'audio'), 'tp')
- audio_value: bfloat16 [16384, 3072], P(('video', 'audio'), 'tp'), may hold values from -6 to 6
- cotangent: bfloat16 [81920, 3072], P(('video', 'audio'), 'tp')
- query_gain: float32 [3072], P('tp'), may hold values from 0.5 to 2
- key_gain: float32 [3072], P('tp'), may hold values from 0.5 to 2
- time_lists: int32 [640, 4], P(('video', 'audio')), may hold values from 0 to 127, as said below
Outputs:
- attended: bfloat16 [81920, 3072], P(('video', 'audio'), 'tp')
- video_query_grad: bfloat16 [81920, 3072], P(('video', 'audio'), 'tp')
- audio_key_grad: bfloat16 [16384, 3072], P(('video', 'audio'), 'tp')
- audio_value_grad: bfloat16 [16384, 3072], P(('video', 'audio'), 'tp')
- query_gain_grad: float32 [3072], P('tp')
- key_gain_grad: float32 [3072], P('tp')
Inputs may be any that keep to these rules, and one draw needn't show every extreme that they name: `time_lists`: row b lists audio blocks for video block b. Its first entry is (b) // 5; every entry differs from that value by at most 1, and in every row one entry lies exactly 1 below or above it before clipping to the range.
All inputs are finite; a program needn't handle non-finite values.
Results may differ from a plain program's by a relative error of at most 0.015.
The roundings to bfloat16 on the way count: a program that leaves them out, or rounds other values in their place, can miss the bound.
Values may be sent and summed in bfloat16 or wider, within the bound.
No kernel may reach another device: no remote copies, remote signals or barrier semaphores. Data moves between devices by JAX's collectives and lax.ppermute only.
A program may use at most 64 MiB of HBM per device.

v0:
```python
import jax
import jax.numpy as jnp
from jax import lax
from jax.sharding import PartitionSpec as P

D = 3072
HS = 128
BLOCK = 128


epsilon = 1e-06
excluded = -1e30


def passed_along(value, axis, by):
    size = lax.axis_size(axis)
    pairs = [(i, i + by) for i in range(size) if 0 <= i + by < size]
    return lax.ppermute(value, axis, pairs)


def with_halo(cells, sides, width):
    for axis, dim in sides:
        count = lax.axis_size(axis)
        ends = count - 1
        head = lax.slice_in_dim(cells, 0, width, axis=dim)
        tail = lax.slice_in_dim(cells, cells.shape[dim] - width, cells.shape[dim], axis=dim)
        cells = jnp.concatenate(
            [
                lax.ppermute(tail, axis, [(i, (i + 1) % count) for i in range(ends)]),
                cells,
                lax.ppermute(head, axis, [((i + 1) % count, i) for i in range(ends)]),
            ],
            axis=dim,
        )
    return cells


def contract(left, right):
    return lax.dot_general(
        left, right, (((1,), (1,)), ((), ())), preferred_element_type=jnp.float32
    )


def transposed(left, right):
    return lax.dot_general(
        left, right, (((0,), (0,)), ((), ())), preferred_element_type=jnp.float32
    )


def inverse_rms(total):
    return lax.rsqrt(total / D + epsilon)


def token_mask(allowed):
    count_rows, count_cols = allowed.shape
    spread = jnp.broadcast_to(allowed[:, None, :, None], (count_rows, BLOCK, count_cols, BLOCK))
    return spread.reshape(count_rows * BLOCK, count_cols * BLOCK)


def pass_on(partial_value, offset):
    return passed_along(partial_value.astype(jnp.bfloat16), ("video", "audio"), offset).astype(
        partial_value.dtype
    )


def on_device(video_query, audio_key, audio_value, cotangent, query_gain, key_gain, time_lists):
    factor = HS ** (-0.5)
    width = video_query.shape[1]
    heads = width // HS
    audio_rows = audio_key.shape[0]
    audio_blocks = audio_rows // BLOCK
    place = lax.axis_index(("video", "audio"))
    query_rows = video_query.astype(jnp.float32)
    key_rows = audio_key.astype(jnp.float32)
    query_total, key_total = lax.psum(
        (jnp.sum(query_rows * query_rows, axis=1), jnp.sum(key_rows * key_rows, axis=1)), "tp"
    )
    query_scale = inverse_rms(query_total)
    key_scale = inverse_rms(key_total)
    query_norm = (query_rows * query_scale[:, None] * query_gain).astype(jnp.bfloat16)
    key_norm = (key_rows * key_scale[:, None] * key_gain).astype(jnp.bfloat16)
    window = with_halo(jnp.stack([key_norm, audio_value]), ((("video", "audio"), 1),), audio_rows)
    key_window = window[0]
    value_window = window[1]
    block_ids = (place - 1) * audio_blocks + jnp.arange(3 * audio_blocks, dtype=jnp.int32)
    allowed = jnp.any(time_lists[:, :, None] == block_ids[None, None, :], axis=1)
    mask = token_mask(allowed)
    outputs = []
    query_cols = []
    key_cols = []
    value_cols = []
    for head_index in range(heads):
        columns = slice(head_index * HS, (head_index + 1) * HS)
        query_head = query_norm[:, columns]
        key_head = key_window[:, columns]
        value_head = value_window[:, columns]
        cot_head = cotangent[:, columns]
        scores = jnp.where(mask, contract(query_head, key_head) * factor, excluded)
        highest = jnp.max(scores, axis=1, keepdims=True)
        log_total = highest + jnp.log(jnp.sum(jnp.exp(scores - highest), axis=1, keepdims=True))
        probs = jnp.exp(scores - log_total)
        probs_low = probs.astype(jnp.bfloat16)
        output = jnp.dot(probs_low, value_head, preferred_element_type=jnp.float32).astype(
            jnp.bfloat16
        )
        row_delta = jnp.sum(
            cot_head.astype(jnp.float32) * output.astype(jnp.float32), axis=1, keepdims=True
        )
        grad_probs = contract(cot_head, value_head)
        grad_scores = (probs * (grad_probs - row_delta) * factor).astype(jnp.bfloat16)
        query_cols.append(jnp.dot(grad_scores, key_head, preferred_element_type=jnp.float32))
        key_cols.append(transposed(grad_scores, query_head))
        value_cols.append(transposed(probs_low, cot_head))
        outputs.append(output)
    attended = jnp.concatenate(outputs, axis=1)
    grad_query = jnp.concatenate(query_cols, axis=1)
    partial_value = jnp.stack(
        [jnp.concatenate(key_cols, axis=1), jnp.concatenate(value_cols, axis=1)]
    )
    from_right = pass_on(partial_value[:, :audio_rows], -1)
    from_left = pass_on(partial_value[:, 2 * audio_rows :], 1)
    combined = partial_value[:, audio_rows : 2 * audio_rows] + from_right + from_left
    grad_key = combined[0]
    audio_value_grad = combined[1].astype(jnp.bfloat16)
    scaled_query = grad_query * query_gain
    scaled_key = grad_key * key_gain
    inner_query, inner_key = lax.psum(
        (jnp.sum(query_rows * scaled_query, axis=1), jnp.sum(key_rows * scaled_key, axis=1)), "tp"
    )
    video_query_grad = (
        query_scale[:, None] * scaled_query
        - query_rows * (query_scale * query_scale * query_scale * inner_query / D)[:, None]
    ).astype(jnp.bfloat16)
    audio_key_grad = (
        key_scale[:, None] * scaled_key
        - key_rows * (key_scale * key_scale * key_scale * inner_key / D)[:, None]
    ).astype(jnp.bfloat16)
    query_gain_grad, key_gain_grad = lax.psum(
        (
            jnp.sum(grad_query * query_rows * query_scale[:, None], axis=0),
            jnp.sum(grad_key * key_rows * key_scale[:, None], axis=0),
        ),
        ("video", "audio"),
    )
    return (
        attended,
        video_query_grad,
        audio_key_grad,
        audio_value_grad,
        query_gain_grad,
        key_gain_grad,
    )


def solution(mesh):
    in_specs = (
        P(("video", "audio"), "tp"),
        P(("video", "audio"), "tp"),
        P(("video", "audio"), "tp"),
        P(("video", "audio"), "tp"),
        P("tp"),
        P("tp"),
        P(("video", "audio"), None),
    )
    out_specs = (
        P(("video", "audio"), "tp"),
        P(("video", "audio"), "tp"),
        P(("video", "audio"), "tp"),
        P(("video", "audio"), "tp"),
        P("tp"),
        P("tp"),
    )
    return jax.shard_map(
        on_device, mesh=mesh, in_specs=in_specs, out_specs=out_specs, check_vma=False
    )
```

profile of v0, /device:TPU:32, one launch (start us, length us, event | category | flops | bytes accessed | tf_op | source)
XLA Modules:
  0.0 488.6 jit_solution(13988408186583712272)
XLA Ops:
  0.6 1.2 copy.49
  1.9 1.1 copy.50
  3.0 0.6 copy.48
  4.0 13.9 %all-reduce.2 = (f32[640]{0:T(1024)S(1)}, f32[128]{0:T(128)S(1)}) all-reduce(f32[640]{0:T(1024)S(1)} %fusion.1, f32[128]{0:T(128)S(1)} %fusion.48), channel_id=1, replica_groups=mesh['video'=16,'audio'=8,'tp'=4] {'tp'}, use_global_device_ids=true, to_apply=%region_2.0 | all-reduce | flops 768 | bytes 6144 | tf_op jit(solution)/shard_map/psum | solution.py:75
  18.1 0.8 pad_maximum_fusion.2
  18.9 1.3 collective-permute-start.1
  20.2 3.8 collective-permute-start
  24.5 0.3 copy.51
  24.9 0.9 fusion.124
  25.8 1.7 copy.72
  27.5 1.7 copy.71
  29.3 0.8 copy.70
  30.9 1.3 pad_maximum_fusion.1
  32.3 0.4 fusion.130
  32.7 0.4 fusion.129
  33.0 0.4 fusion.128
  33.4 0.4 fusion.127
  33.8 0.4 fusion.126
  34.2 0.4 fusion.125
  34.7 0.3 convolution_dynamic-update-slice_fusion.11
  35.0 0.3 constant_dynamic-update-slice_fusion.5
  35.4 0.4 fusion.33
  35.8 0.3 convolution_dynamic-update-slice_fusion.17
  37.3 0.3 constant_dynamic-update-slice_fusion.4
  37.6 0.3 constant_dynamic-update-slice_fusion.3
  38.0 0.3 constant_dynamic-update-slice_fusion.2
  38.3 0.3 constant_dynamic-update-slice_fusion.1
  38.7 0.3 constant_dynamic-update-slice_fusion
  39.3 0.6 copy-done.1
  39.9 0.4 fusion.38
  40.3 0.4 fusion.37
  40.7 0.5 copy-done.10
  41.2 0.4 fusion.36
  41.7 0.4 fusion.35
  42.1 0.4 fusion.34
  42.4 0.3 convolution_dynamic-update-slice_fusion.10
  42.8 0.3 convolution_dynamic-update-slice_fusion.9
  43.1 0.3 convolution_dynamic-update-slice_fusion.8
  43.5 0.3 convolution_dynamic-update-slice_fusion.7
  43.8 0.3 convolution_dynamic-update-slice_fusion.6
  44.1 0.3 convolution_dynamic-update-slice_fusion.16
  44.4 0.3 convolution_dynamic-update-slice_fusion.15
  44.7 0.3 convolution_dynamic-update-slice_fusion.14
  45.0 0.3 convolution_dynamic-update-slice_fusion.13
  45.3 0.3 convolution_dynamic-update-slice_fusion.12
  45.8 0.8 copy-done.2
  46.7 0.9 fusion.123
  47.6 1.3 collective-permute-start.2
  48.8 3.8 collective-permute-start.3
  52.6 0.3 convolution_dynamic-update-slice_fusion.4
  53.4 0.3 convolution_dynamic-update-slice_fusion.1
  53.7 0.3 convolution_dynamic-update-slice_fusion
  54.0 2.2 copy.63
  56.2 1.3 fusion.8
  57.5 0.4 copy-done.5
  57.9 1.2 fusion.47
  59.1 0.3 fusion.55
  59.5 0.6 copy-done.6
  60.1 0.8 copy.66
  60.9 8.5 %all-reduce.1 = (f32[640]{0:T(1024)S(1)}, f32[128]{0:T(128)S(1)}) all-reduce(f32[640]{0:T(1024)S(1)} %copy-done.15, f32[128]{0:T(128)S(1)} %get-tuple-element.27), channel_id=1, replica_groups=mesh['video'=16,'audio'=8,'tp'=4] {'tp'}, use_global_device_ids=true, to_apply=%region_24.25 | all-reduce | flops 768 | bytes 6144 | tf_op jit(solution)/shard_map/psum | solution.py:127
  69.4 1.3 fusion.6
  70.8 2.3 copy.64
  73.3 0.8 copy.65
  74.1 414.5 %all-reduce = (f32[768]{0:T(1024)}, f32[768]{0:T(1024)}) all-reduce(f32[768]{0:T(1024)S(1)} %get-tuple-element.24, f32[768]{0:T(1024)S(1)} %get-tuple-element.26), channel_id=1, replica_groups=mesh['video'=16,'audio'=8,'tp'=4] {'video','audio'}, use_global_device_ids=true, to_apply=%region_28.29 | all-reduce | flops 1536 | bytes 12288 | tf_op jit(solution)/shard_map/psum | solution.py:138
  (88 shorter events, 4.9 us)
Async XLA Ops:
  0.6 2.4 copy-start.9
  3.0 14.8 %copy-start.14 = (f32[768]{0:T(1024)S(1)}, f32[768]{0:T(1024)}, u32[]{:S(2)}) copy-start(f32[768]{0:T(1024)} %param.12) | copy-start | bytes 9220
  3.7 20.3 %copy-start.21 = (s32[5,4]{0,1:T(4,128)S(1)}, s32[5,4]{0,1:T(4,128)}, u32[]{:S(2)}) copy-start(s32[5,4]{0,1:T(4,128)} %param.13) | copy-start | bytes 244
  17.8 6.1 %copy-start.22 = (f32[128]{0:T(128)}, f32[128]{0:T(128)S(1)}, u32[]{:S(2)}) copy-start(f32[128]{0:T(128)S(1)} %get-tuple-element.33) | copy-start | bytes 1540
  17.9 12.7 %copy-start.16 = (f32[640]{0:T(1024)}, f32[640]{0:T(1024)S(1)}, u32[]{:S(2)}) copy-start(f32[640]{0:T(1024)S(1)} %get-tuple-element.32) | copy-start | bytes 7684
  17.9 7.0 %copy-start.18 = (f32[128]{0:T(128)}, f32[128]{0:T(128)S(1)}, u32[]{:S(2)}) copy-start(f32[128]{0:T(128)S(1)} %add_rsqrt_fusion.1) | copy-start | bytes 1540
  18.1 6.8 %copy-start = (bf16[640,768]{1,0:T(8,128)(2,1)S(1)}, bf16[640,768]{1,0:T(8,128)(2,1)}, u32[]{:S(2)}) copy-start(bf16[640,768]{1,0:T(8,128)(2,1)} %param.10) | copy-start | bytes 2949124
  18.9 12.0 %collective-permute-start.1 = (bf16[2,128,768]{1,2,0:T(8,128)(2,1)}, bf16[2,128,768]{1,2,0:T(8,128)(2,1)}, u32[]{:S(2)}, u32[]{:S(2)}) collective-permute-start(bf16[2,128,768]{1,2,0:T(8,128)(2,1)} %pad_maximum_fusion.2), channel_id=1, source_target_pairs={{4,0},{8,4},{12,8},{16,12},{20,16},{24,20},{28,24},{32,28},{36,32}... | collective-permute-start | bytes 1179656 | tf_op jit(solution)/shard_map/ppermute | solution.py:31
  20.2 10.7 %collective-permute-start = (bf16[2,128,768]{1,2,0:T(8,128)(2,1)}, bf16[2,128,768]{1,2,0:T(8,128)(2,1)}, u32[]{:S(2)}, u32[]{:S(2)}) collective-permute-start(bf16[2,128,768]{1,2,0:T(8,128)(2,1)} %pad_maximum_fusion.2), channel_id=1, source_target_pairs={{0,4},{4,8},{8,12},{12,16},{16,20},{20,24},{24,28},{28,32},{32,36}... | collective-permute-start | bytes 1179656 | tf_op jit(solution)/shard_map/ppermute | solution.py:29
  25.8 4.8 copy-start.13
  38.3 0.9 copy-start.12
  38.7 1.2 copy-start.1
  39.0 1.3 copy-start.8
  39.0 1.3 copy-start.11
  40.2 0.9 copy-start.10
  44.1 1.5 copy-start.4
  45.6 1.1 copy-start.2
  47.6 9.9 %collective-permute-start.2 = (bf16[2,128,768]{1,2,0:T(8,128)(2,1)}, bf16[2,128,768]{1,2,0:T(8,128)(2,1)}, u32[]{:S(2)}, u32[]{:S(2)}) collective-permute-start(bf16[2,128,768]{1,2,0:T(8,128)(2,1)} %get-tuple-element.34), channel_id=1, source_target_pairs={{4,0},{8,4},{12,8},{16,12},{20,16},{24,20},{28,24},{32,28},{36,32}... | collective-permute-start | bytes 1179656 | tf_op jit(solution)/shard_map/ppermute | solution.py:18
  48.8 8.7 %collective-permute-start.3 = (bf16[2,128,768]{1,2,0:T(8,128)(2,1)S(1)}, bf16[2,128,768]{1,2,0:T(8,128)(2,1)}, u32[]{:S(2)}, u32[]{:S(2)}) collective-permute-start(bf16[2,128,768]{1,2,0:T(8,128)(2,1)S(1)} %get-tuple-element.35), channel_id=1, source_target_pairs={{0,4},{4,8},{8,12},{12,16},{16,20},{20,24},{24,28},{28,32},{32,36}... | collective-permute-start | bytes 1179656 | tf_op jit(solution)/shard_map/ppermute | solution.py:18
  56.2 1.3 copy-start.3
  56.2 1.6 copy-start.5
  57.5 1.6 copy-start.19
  59.1 0.9 copy-start.6
  59.1 1.8 copy-start.15
  59.1 10.2 %copy-start.17 = (f32[640]{0:T(1024)S(1)}, f32[640]{0:T(1024)}, u32[]{:S(2)}) copy-start(f32[640]{0:T(1024)} %copy-done.16) | copy-start | bytes 7684
  70.7 2.3 copy-start.23
  70.7 2.3 copy-start.7
  70.8 2.3 copy-start.20
where the time goes:
time: 490 us; the launch traced here: 489 us
  blocking collectives  437 us (89%)
  local copies, waits for them, and re-layouts  19.7 us (4%)
  matrix products  11.7 us (2%)
  starting transfers between devices  10.1 us (2%)
  other arithmetic  8.91 us (2%)
    psum x1, blocking collectives, on_device(): lax.psum((jnp.sum(grad_query * query_rows * query_scale[:, None], axis=0)...  414 us
    unnamed x63, local copies, waits for them, and re-layouts  18 us
    psum x1, blocking collectives, on_device(): lax.psum((jnp.sum(query_rows * query_rows, axis=1), jnp.sum(key_rows * ke...  13.9 us
  transfers between devices with their start and end apart: 4, of which 0 were waited for; matrix products, arithmetic and copies ran while one was open for 2% of the time, Pallas kernels for 0%

commit v1 on v0

v1 whole, which is shorter than its diff:
```python
import functools
import numpy as np
import jax
import jax.numpy as jnp
from jax import lax
from jax.experimental import pallas as pl
from jax.experimental.pallas import tpu as pltpu
from jax.sharding import Mesh, PartitionSpec as P

D = 3072
HS = 128
BLOCK = 128
FACTOR = HS ** (-0.5)
LOG2E = 1.4426950408889634
EPSILON = 1e-06
EXCLUDED = -1e30
LINE = ("y", "far", "x", "core")


def by_last(left, right):
    return lax.dot_general(
        left, right, (((1,), (1,)), ((), ())), preferred_element_type=jnp.float32
    )


def plain(left, right):
    return jnp.dot(left, right, preferred_element_type=jnp.float32)


def attention_kernel(
    bias, scale, query, cot, gain, key_gain, key_l, key_c, key_r, val_l, val_c, val_r,
    attended, grad_query, inner, query_gain_grad, key_gain_grad, left, right, own,
    scale_cols, inner_sum, probs_low, grad_low,
):
    head = pl.program_id(0)
    rows = query.shape[0]

    @pl.when(head == 0)
    def _():
        scale_cols[...] = jnp.broadcast_to(scale[...], (HS, rows)).T
        inner_sum[...] = jnp.zeros_like(inner_sum)

    raw = query[...].astype(jnp.float32)
    scaled = raw * scale_cols[...]
    normed = (scaled * gain[...]).astype(jnp.bfloat16)
    keys = jnp.concatenate([key_l[...], key_c[...], key_r[...]], axis=0)
    values = jnp.concatenate([val_l[...], val_c[...], val_r[...]], axis=0)
    span = keys.shape[0] // 3
    upstream = cot[...]
    step = 128
    for start in range(0, rows, step):
        part = slice(start, start + step)
        scores = by_last(keys, normed[part]) * (FACTOR * LOG2E)
        scores = jnp.concatenate(
            [
                scores[:span] + bias[0:1, part],
                scores[span : 2 * span],
                scores[2 * span :] + bias[1:2, part],
            ],
            axis=0,
        )
        highest = jnp.max(scores, axis=0, keepdims=True)
        weights = jnp.exp2(scores - highest)
        share = 1.0 / jnp.sum(weights, axis=0, keepdims=True)
        probs_low[:, part] = (weights * share).astype(jnp.bfloat16)
        grad_probs = by_last(values, upstream[part])
        delta = jnp.sum(weights * grad_probs, axis=0, keepdims=True) * share
        grad_low[:, part] = (weights * ((grad_probs - delta) * (share * FACTOR))).astype(
            jnp.bfloat16
        )
    low = probs_low[...]
    grads = grad_low[...]
    attended[...] = plain(values.T, low).T.astype(jnp.bfloat16)
    grad = plain(keys.T, grads).T
    grad_query[...] = grad
    inner_sum[...] += raw * grad * gain[...]
    query_gain_grad[...] = jnp.sum(grad * scaled, axis=0, keepdims=True)
    grad_keys = plain(grads, normed)
    grad_values = plain(low, upstream)
    left[0] = grad_keys[:span].astype(jnp.bfloat16)
    left[1] = grad_values[:span].astype(jnp.bfloat16)
    own[0] = grad_keys[span : 2 * span]
    own[1] = grad_values[span : 2 * span]
    right[0] = grad_keys[2 * span :].astype(jnp.bfloat16)
    right[1] = grad_values[2 * span :].astype(jnp.bfloat16)
    key_gain_grad[...] = (
        jnp.sum(grad_keys * keys.astype(jnp.float32), axis=0, keepdims=True) / key_gain[...]
    )

    @pl.when(head == pl.num_programs(0) - 1)
    def _():
        inner[...] = jnp.sum(inner_sum[...].T, axis=0, keepdims=True)


def attention(bias, scale, query, cot, gain, key_gain, keys, values):
    rows, width = query.shape
    heads = width // HS
    span = keys[0].shape[0]

    def whole(shape):
        return pl.BlockSpec(shape, lambda h: (0,) * len(shape))

    def of_head(*lead):
        return pl.BlockSpec((*lead, HS), lambda h: (0,) * len(lead) + (h,))

    f32, bf16 = jnp.float32, jnp.bfloat16
    shape = jax.ShapeDtypeStruct
    return pl.pallas_call(
        attention_kernel,
        grid=(heads,),
        in_specs=[
            whole((2, rows)),
            whole((1, rows)),
            of_head(rows),
            of_head(rows),
            of_head(1),
            of_head(1),
        ]
        + [of_head(span)] * 6,
        out_specs=[
            of_head(rows),
            of_head(rows),
            whole((1, rows)),
            of_head(1),
            of_head(1),
            of_head(2, span),
            of_head(2, span),
            of_head(2, span),
        ],
        out_shape=[
            shape((rows, width), bf16),
            shape((rows, width), f32),
            shape((1, rows), f32),
            shape((1, width), f32),
            shape((1, width), f32),
            shape((2, span, width), bf16),
            shape((2, span, width), bf16),
            shape((2, span, width), f32),
        ],
        scratch_shapes=[
            pltpu.VMEM((rows, HS), f32),
            pltpu.VMEM((rows, HS), f32),
            pltpu.VMEM((3 * span, rows), bf16),
            pltpu.VMEM((3 * span, rows), bf16),
        ],
        compiler_params=pltpu.CompilerParams(vmem_limit_bytes=40 * 1024 * 1024),
        cost_estimate=pl.CostEstimate(
            flops=12 * rows * 3 * span * width, bytes_accessed=10 * rows * width, transcendentals=0
        ),
        name="attention",
    )(bias, scale, query, cot, gain, key_gain, *keys, *values)


def inverse_rms(total):
    return lax.rsqrt(total / D + EPSILON)


def shift(value, by):
    size = 1
    for axis in LINE:
        size *= lax.axis_size(axis)
    pairs = [(i, i + by) for i in range(size) if 0 <= i + by < size]
    return lax.ppermute(value, LINE, pairs)


def on_device(video_query, audio_key, audio_value, cotangent, query_gain, key_gain, time_lists):
    place = lax.axis_index(LINE)
    query_rows = video_query.astype(jnp.float32)
    key_rows = audio_key.astype(jnp.float32)
    rows = video_query.shape[0]
    value_l = shift(audio_value, 1)
    value_r = shift(audio_value, -1)
    totals = lax.psum(
        jnp.concatenate(
            [jnp.sum(query_rows * query_rows, axis=1), jnp.sum(key_rows * key_rows, axis=1)]
        ),
        "tp",
    )
    scales = inverse_rms(totals)
    query_scale = scales[:rows]
    key_scale = scales[rows:]
    key_norm = (key_rows * key_scale[:, None] * key_gain).astype(jnp.bfloat16)
    key_l = shift(key_norm, 1)
    key_r = shift(key_norm, -1)
    listed = jnp.stack(
        [jnp.any(time_lists == place - 1, axis=1), jnp.any(time_lists == place + 1, axis=1)]
    )
    bias = jnp.repeat(jnp.where(listed, 0.0, EXCLUDED).astype(jnp.float32), BLOCK, axis=1)
    (attended, grad_query, inner_query, gain_q, gain_k, to_left, to_right, own) = attention(
        bias,
        query_scale[None],
        video_query,
        cotangent,
        query_gain[None],
        key_gain[None],
        (key_l, key_norm, key_r),
        (value_l, audio_value, value_r),
    )
    from_right = shift(to_left, -1)
    from_left = shift(to_right, 1)
    gains = jnp.concatenate([gain_q, gain_k], axis=0)
    for axis in ("core", "x", "y"):
        gains = lax.psum(gains, axis)
    combined = own + from_right + from_left
    grad_key = combined[0]
    audio_value_grad = combined[1].astype(jnp.bfloat16)
    scaled_key = grad_key * key_gain
    inner = lax.psum(
        jnp.concatenate([inner_query[0], jnp.sum(key_rows * scaled_key, axis=1)]), "tp"
    )
    gains = lax.psum(gains, "far")
    shrink = scales * scales * scales * inner / D
    video_query_grad = (
        query_scale[:, None] * (grad_query * query_gain) - query_rows * shrink[:rows, None]
    ).astype(jnp.bfloat16)
    audio_key_grad = (key_scale[:, None] * scaled_key - key_rows * shrink[rows:, None]).astype(
        jnp.bfloat16
    )
    return attended, video_query_grad, audio_key_grad, audio_value_grad, gains[0], gains[1]


def solution(mesh):
    far = 4
    video, audio, tp = (mesh.shape[name] for name in ("video", "audio", "tp"))
    fine = Mesh(
        np.asarray(mesh.devices).reshape(video // far, far, audio // 2, 2, tp), (*LINE, "tp")
    )
    tokens = P(LINE, "tp")
    per_feature = P("tp")
    return jax.shard_map(
        on_device,
        mesh=fine,
        in_specs=(tokens, tokens, tokens, tokens, per_feature, per_feature, P(LINE, None)),
        out_specs=(tokens, tokens, tokens, tokens, per_feature, per_feature),
        check_vma=False,
    )
```

time: 490 us -> 139 us (0.28)
  the two profiles are of different devices: /device:TPU:32 before, /device:TPU:8 now
where the time goes in v1:
time: 139 us; the launch traced here: 138 us
  blocking collectives  64.3 us (46%)
  starting transfers between devices  31.7 us (23%)
  other arithmetic  12.2 us (9%)
  Pallas kernels  10.6 us (8%)
  local copies, waits for them, and re-layouts  9.62 us (7%)
  waiting for transfers between devices  9.08 us (7%)
    ppermute x6, starting transfers between devices, shift(): return lax.ppermute(value, LINE, pairs)  31.7 us
    psum x3, blocking collectives, on_device(): gains = lax.psum(gains, axis)  21.1 us
    psum x1, blocking collectives, on_device(): gains = lax.psum(gains, 'far')  18.3 us
    psum x1, blocking collectives, on_device(): lax.psum(jnp.concatenate([jnp.sum(query_rows * query_rows, axis=1), jnp.s...  13 us
    psum x1, blocking collectives, on_device(): lax.psum(jnp.concatenate([inner_query[0], jnp.sum(key_rows * scaled_key,...  11.8 us
    pallas_call x1, Pallas kernels, attention(): pl.pallas_call(attention_kernel, grid=(heads,), in_specs=[whole((2, rows)...  10.6 us
    ppermute x6, waiting for transfers between devices, shift(): return lax.ppermute(value, LINE, pairs)  9.08 us
    unnamed x30, local copies, waits for them, and re-layouts  5.92 us
  transfers between devices with their start and end apart: 6, of which 2 were waited for; matrix products, arithmetic and copies ran while one was open for 2% of the time, Pallas kernels for 0%

profile of v1, /device:TPU:8, one launch (start us, length us, event | category | flops | bytes accessed | tf_op | source)
XLA Modules:
  0.0 138.3 jit_solution(15299639126843507711)
XLA Ops:
  0.6 1.0 fusion.3
  1.7 1.5 %fusion = f32[640]{0:T(1024)S(1)} fusion(bf16[640,768]{1,0:T(8,128)(2,1)} %query.1), kind=kLoop, calls=%fused_computation.2 | loop fusion | flops 1473920 | bytes 985600 | tf_op jit(solution)/shard_map/reduce_sum | solution.py:175
  3.2 13.0 %psum.42 = f32[768]{0:T(1024)S(1)} all-reduce(f32[768]{0:T(1024)S(1)} %pad_maximum_fusion.1), channel_id=1, replica_groups=mesh['y'=4,'far'=4,'x'=4,'core'=2,'tp'=4] {'tp'}, use_global_device_ids=true, to_apply=%region_4.0 | all-reduce | flops 768 | bytes 6144 | tf_op jit(solution)/shard_map/psum | solution.py:173
  16.2 0.0 copy-start.10
  16.2 0.0 copy-start.8
  16.2 0.0 copy-start.13
  16.2 1.0 fusion.5.key_c
  17.2 9.5 %collective-permute-start.1 = (bf16[128,768]{1,0:T(8,128)(2,1)S(1)}, bf16[128,768]{1,0:T(8,128)(2,1)S(1)}, u32[]{:S(2)}, u32[]{:S(2)}) collective-permute-start(bf16[128,768]{1,0:T(8,128)(2,1)S(1)} %fusion.5.key_c), channel_id=1, source_target_pairs={{4,0},{8,4},{12,8},{16,12},{20,16},{24,20},{28,24},{32,28},{36,32}... | collective-permute-start | bytes 589832 | tf_op jit(solution)/shard_map/ppermute | solution.py:163
  26.8 1.9 %collective-permute-start = (bf16[128,768]{1,0:T(8,128)(2,1)S(1)}, bf16[128,768]{1,0:T(8,128)(2,1)S(1)}, u32[]{:S(2)}, u32[]{:S(2)}) collective-permute-start(bf16[128,768]{1,0:T(8,128)(2,1)S(1)} %fusion.5.key_c), channel_id=1, source_target_pairs={{0,4},{4,8},{8,12},{12,16},{16,20},{20,24},{24,28},{28,32},{32,36}... | collective-permute-start | bytes 589832 | tf_op jit(solution)/shard_map/ppermute | solution.py:163
  28.7 1.9 %collective-permute-start.2 = (bf16[128,768]{1,0:T(8,128)(2,1)}, bf16[128,768]{1,0:T(8,128)(2,1)S(1)}, u32[]{:S(2)}, u32[]{:S(2)}) collective-permute-start(bf16[128,768]{1,0:T(8,128)(2,1)} %val_c.1), channel_id=1, source_target_pairs={{0,4},{4,8},{8,12},{12,16},{16,20},{20,24},{24,28},{28,32},{32,36}... | collective-permute-start | bytes 589832 | tf_op jit(solution)/shard_map/ppermute | solution.py:163
  30.6 10.6 %collective-permute-start.3 = (bf16[128,768]{1,0:T(8,128)(2,1)}, bf16[128,768]{1,0:T(8,128)(2,1)S(1)}, u32[]{:S(2)}, u32[]{:S(2)}) collective-permute-start(bf16[128,768]{1,0:T(8,128)(2,1)} %val_c.1), channel_id=1, source_target_pairs={{4,0},{8,4},{12,8},{16,12},{20,16},{24,20},{28,24},{32,28},{36,32}... | collective-permute-start | bytes 589832 | tf_op jit(solution)/shard_map/ppermute | solution.py:163
  41.2 0.0 copy-done.13
  41.2 0.7 broadcast_in_dim.33.key_gain
  41.9 0.7 broadcast_in_dim.32.gain
  42.6 0.7 compare_reduce_fusion.1
  43.3 0.1 broadcast_bitcast_fusion
  43.4 0.0 collective-permute-done.1.key_r
  43.4 0.6 collective-permute-done.key_l
  44.0 8.5 %collective-permute-done.2.val_l = bf16[128,768]{1,0:T(8,128)(2,1)S(1)} collective-permute-done((bf16[128,768]{1,0:T(8,128)(2,1)}, bf16[128,768]{1,0:T(8,128)(2,1)S(1)}, u32[]{:S(2)}, u32[]{:S(2)}) %collective-permute-start.2) | collective-permute-done | bytes 196640 | tf_op jit(solution)/shard_map/ppermute | solution.py:163
  52.5 0.0 collective-permute-done.3.val_r
  52.5 0.0 copy-done.10
  52.5 0.0 copy-done.8
  52.5 0.0 copy-start.5
  52.5 0.7 copy-done.5
  53.2 0.0 copy-start
  53.2 1.2 copy-done
  54.4 0.0 copy-start.3
  54.4 1.2 copy-done.3
  55.6 0.0 copy-start.4
  55.6 0.9 copy-done.4
  56.5 0.0 copy-start.6
  56.5 0.9 copy-done.6
  57.4 10.6 %attention.1 = (bf16[640,768]{1,0:T(8,128)(2,1)}, f32[640,768]{1,0:T(8,128)S(1)}, f32[1,640]{1,0:T(1,128)S(1)}, f32[1,768]{1,0:T(1,128)S(1)}, f32[1,768]{1,0:T(1...) custom-call(f32[2,640]{1,0:T(2,128)S(1)} %bitcast.19, ...), custom_call_target="tpu_custom_call" | custom-call | flops 2264924160 | bytes 4915200 | tf_op jit(solution)/shard_map/attention/pallas_call | solution.py:108
  68.0 0.0 copy-start.2
  68.0 0.9 copy-done.2
  68.9 0.0 copy-start.7
  68.9 5.8 %collective-permute-start.4 = (bf16[2,128,768]{2,1,0:T(8,128)(2,1)S(1)}, bf16[2,128,768]{2,1,0:T(8,128)(2,1)S(1)}, u32[]{:S(2)}, u32[]{:S(2)}) collective-permute-start(bf16[2,128,768]{2,1,0:T(8,128)(2,1)S(1)} %get-tuple-element.18), channel_id=1, source_target_pairs={{4,0},{8,4},{12,8},{16,12},{20,16},{24,20},{28,24},{32,28},{36,32}... | collective-permute-start | bytes 1179656 | tf_op jit(solution)/shard_map/ppermute | solution.py:163
  74.8 1.9 %collective-permute-start.5 = (bf16[2,128,768]{2,1,0:T(8,128)(2,1)S(1)}, bf16[2,128,768]{2,1,0:T(8,128)(2,1)}, u32[]{:S(2)}, u32[]{:S(2)}) collective-permute-start(bf16[2,128,768]{2,1,0:T(8,128)(2,1)S(1)} %get-tuple-element.19), channel_id=1, source_target_pairs={{0,4},{4,8},{8,12},{12,16},{16,20},{20,24},{24,28},{28,32},{32,36}... | collective-permute-start | bytes 1179656 | tf_op jit(solution)/shard_map/ppermute | solution.py:163
  76.7 0.6 reduce
  77.3 2.5 %psum.44 = f32[2,768]{1,0:T(2,128)S(1)} all-reduce(f32[2,768]{1,0:T(2,128)S(1)} %pad_maximum_fusion), channel_id=1, replica_groups=mesh['y'=4,'far'=4,'x'=4,'core'=2,'tp'=4] {'core'}, use_global_device_ids=true, to_apply=%region_7.8 | all-reduce | flops 1536 | bytes 12288 | tf_op jit(solution)/shard_map/psum | solution.py:203
  79.8 9.8 %psum.45 = f32[2,768]{1,0:T(2,128)S(1)} all-reduce(f32[2,768]{1,0:T(2,128)S(1)} %psum.44), channel_id=1, replica_groups=mesh['y'=4,'far'=4,'x'=4,'core'=2,'tp'=4] {'x'}, use_global_device_ids=true, to_apply=%region_8.9 | all-reduce | flops 1536 | bytes 12288 | tf_op jit(solution)/shard_map/psum | solution.py:203
  89.7 8.8 %psum.46 = f32[2,768]{1,0:T(2,128)S(1)} all-reduce(f32[2,768]{1,0:T(2,128)S(1)} %psum.45), channel_id=1, replica_groups=mesh['y'=4,'far'=4,'x'=4,'core'=2,'tp'=4] {'y'}, use_global_device_ids=true, to_apply=%region_9.10 | all-reduce | flops 1536 | bytes 12288 | tf_op jit(solution)/shard_map/psum | solution.py:203
  98.5 18.3 %psum.47 = f32[2,768]{1,0:T(2,128)S(1)} all-reduce(f32[2,768]{1,0:T(2,128)S(1)} %psum.46), channel_id=1, replica_groups=mesh['y'=4,'far'=4,'x'=4,'core'=2,'tp'=4] {'far'}, use_global_device_ids=true, to_apply=%region_10.11 | all-reduce | flops 1536 | bytes 12288 | tf_op jit(solution)/shard_map/psum | solution.py:211
  116.8 0.0 copy-start.12
  116.8 0.6 slice_reduce_fusion
  117.5 0.0 collective-permute-done.4
  117.5 0.0 collective-permute-done.5
  117.5 0.0 copy-start.1
  117.5 0.0 copy-start.9
  117.5 0.0 copy-start.11
  117.5 2.3 %convert_add_fusion = f32[2,128,768]{2,1,0:T(8,128)} fusion(bf16[2,128,768]{2,1,0:T(8,128)(2,1)} %collective-permute-done.5, f32[2,128,768]{2,1,0:T(8,128)} %copy-done.2, bf16[2,128,768]{2,1,0:T(8,128)(2,1)S(1)} %collective-permute-done.4), kind=kLoop, calls=%fused_computation.5 | loop fusion | flops 786432 | bytes 2359296 | tf_op jit(solution)/shard_map/add | solution.py:204
  119.8 0.0 copy-done.7
  119.8 1.1 fusion.6
  120.9 1.7 %fusion.10 = bf16[128,768]{1,0:T(8,128)(2,1)} fusion(f32[2,128,768]{2,1,0:T(8,128)} %convert_add_fusion), kind=kLoop, calls=%fused_computation.19 | loop fusion | bytes 393216 | tf_op jit(solution)/shard_map/convert_element_type | solution.py:206
  122.6 0.0 copy-done.12
  122.6 11.8 %psum.43 = f32[768]{0:T(1024)S(1)} all-reduce(f32[768]{0:T(1024)S(1)} %pad_maximum_fusion.2), channel_id=1, replica_groups=mesh['y'=4,'far'=4,'x'=4,'core'=2,'tp'=4] {'tp'}, use_global_device_ids=true, to_apply=%region_6.7 | all-reduce | flops 768 | bytes 6144 | tf_op jit(solution)/shard_map/psum | solution.py:208
  134.4 0.7 fusion.12
  135.1 1.8 %fusion.8 = bf16[128,768]{1,0:T(8,128)(2,1)} fusion(bf16[128,768]{1,0:T(8,128)(2,1)S(1)} %copy-done.7, f32[2,128,768]{2,1,0:T(8,128)} %convert_add_fusion, f32[128]{0:T(128)S(1)} %slice.29, f32[768]{0:T(1024)} %param.12, f32[128]{0:T(128)} %copy-done.13), kind=kLoop, calls=%fused_computation.15 | loop fusion | flops 589824 | bytes 790528 | tf_op jit(solution)/shard_map/convert_element_type | solution.py:216
  137.0 0.0 copy-done.1
  137.0 0.0 copy-done.9
  137.0 0.0 copy-done.11
  137.0 1.3 fusion.2
  (9 shorter events, 0.1 us)
Async XLA Ops:
  16.2 36.3 %copy-start.10 = (f32[768]{0:T(1024)}, f32[768]{0:T(1024)S(1)}, u32[]{:S(2)}) copy-start(f32[768]{0:T(1024)S(1)} %psum.42) | copy-start | bytes 9220
  16.2 36.3 %copy-start.8 = (f32[768]{0:T(1024)}, f32[768]{0:T(1024)S(1)}, u32[]{:S(2)}) copy-start(f32[768]{0:T(1024)S(1)} %add_rsqrt_fusion) | copy-start | bytes 9220
  16.2 25.0 %copy-start.13 = (f32[128]{0:T(128)}, f32[128]{0:T(128)S(1)}, u32[]{:S(2)}) copy-start(f32[128]{0:T(128)S(1)} %slice.26) | copy-start | bytes 1540
  17.2 26.2 %collective-permute-start.1 = (bf16[128,768]{1,0:T(8,128)(2,1)S(1)}, bf16[128,768]{1,0:T(8,128)(2,1)S(1)}, u32[]{:S(2)}, u32[]{:S(2)}) collective-permute-start(bf16[128,768]{1,0:T(8,128)(2,1)S(1)} %fusion.5.key_c), channel_id=1, source_target_pairs={{4,0},{8,4},{12,8},{16,12},{20,16},{24,20},{28,24},{32,28},{36,32}... | collective-permute-start | bytes 589832 | tf_op jit(solution)/shard_map/ppermute | solution.py:163
  26.8 17.2 %collective-permute-start = (bf16[128,768]{1,0:T(8,128)(2,1)S(1)}, bf16[128,768]{1,0:T(8,128)(2,1)S(1)}, u32[]{:S(2)}, u32[]{:S(2)}) collective-permute-start(bf16[128,768]{1,0:T(8,128)(2,1)S(1)} %fusion.5.key_c), channel_id=1, source_target_pairs={{0,4},{4,8},{8,12},{12,16},{16,20},{20,24},{24,28},{28,32},{32,36}... | collective-permute-start | bytes 589832 | tf_op jit(solution)/shard_map/ppermute | solution.py:163
  28.7 23.8 %collective-permute-start.2 = (bf16[128,768]{1,0:T(8,128)(2,1)}, bf16[128,768]{1,0:T(8,128)(2,1)S(1)}, u32[]{:S(2)}, u32[]{:S(2)}) collective-permute-start(bf16[128,768]{1,0:T(8,128)(2,1)} %val_c.1), channel_id=1, source_target_pairs={{0,4},{4,8},{8,12},{12,16},{16,20},{20,24},{24,28},{28,32},{32,36}... | collective-permute-start | bytes 589832 | tf_op jit(solution)/shard_map/ppermute | solution.py:163
  30.6 21.8 %collective-permute-start.3 = (bf16[128,768]{1,0:T(8,128)(2,1)}, bf16[128,768]{1,0:T(8,128)(2,1)S(1)}, u32[]{:S(2)}, u32[]{:S(2)}) collective-permute-start(bf16[128,768]{1,0:T(8,128)(2,1)} %val_c.1), channel_id=1, source_target_pairs={{4,0},{8,4},{12,8},{16,12},{20,16},{24,20},{28,24},{32,28},{36,32}... | collective-permute-start | bytes 589832 | tf_op jit(solution)/shard_map/ppermute | solution.py:163
  52.5 0.7 copy-start.5
  53.2 1.2 copy-start
  54.4 1.2 copy-start.3
  55.6 0.9 copy-start.4
  56.5 0.9 copy-start.6
  68.0 0.9 copy-start.2
  68.9 50.9 %copy-start.7 = (bf16[128,768]{1,0:T(8,128)(2,1)S(1)}, bf16[128,768]{1,0:T(8,128)(2,1)}, u32[]{:S(2)}) copy-start(bf16[128,768]{1,0:T(8,128)(2,1)} %param.8) | copy-start | bytes 589828
  68.9 48.5 %collective-permute-start.4 = (bf16[2,128,768]{2,1,0:T(8,128)(2,1)S(1)}, bf16[2,128,768]{2,1,0:T(8,128)(2,1)S(1)}, u32[]{:S(2)}, u32[]{:S(2)}) collective-permute-start(bf16[2,128,768]{2,1,0:T(8,128)(2,1)S(1)} %get-tuple-element.18), channel_id=1, source_target_pairs={{4,0},{8,4},{12,8},{16,12},{20,16},{24,20},{28,24},{32,28},{36,32}... | collective-permute-start | bytes 1179656 | tf_op jit(solution)/shard_map/ppermute | solution.py:163
  74.8 42.7 %collective-permute-start.5 = (bf16[2,128,768]{2,1,0:T(8,128)(2,1)S(1)}, bf16[2,128,768]{2,1,0:T(8,128)(2,1)}, u32[]{:S(2)}, u32[]{:S(2)}) collective-permute-start(bf16[2,128,768]{2,1,0:T(8,128)(2,1)S(1)} %get-tuple-element.19), channel_id=1, source_target_pairs={{0,4},{4,8},{8,12},{12,16},{16,20},{20,24},{24,28},{28,32},{32,36}... | collective-permute-start | bytes 1179656 | tf_op jit(solution)/shard_map/ppermute | solution.py:163
  116.8 5.8 %copy-start.12 = (f32[640]{0:T(1024)S(1)}, f32[640]{0:T(1024)}, u32[]{:S(2)}) copy-start(f32[640]{0:T(1024)} %reduce) | copy-start | bytes 7684
  117.5 19.5 %copy-start.1 = (bf16[640,768]{1,0:T(8,128)(2,1)S(1)}, bf16[640,768]{1,0:T(8,128)(2,1)}, u32[]{:S(2)}) copy-start(bf16[640,768]{1,0:T(8,128)(2,1)} %query.1) | copy-start | bytes 2949124
  117.5 19.5 %copy-start.9 = (f32[768]{0:T(1024)S(1)}, f32[768]{0:T(1024)}, u32[]{:S(2)}) copy-start(f32[768]{0:T(1024)} %copy-done.8) | copy-start | bytes 9220
  117.5 19.5 %copy-start.11 = (f32[768]{0:T(1024)S(1)}, f32[768]{0:T(1024)}, u32[]{:S(2)}) copy-start(f32[768]{0:T(1024)} %param.11) | copy-start | bytes 9220

commit v2 on v1

v2 whole, which is shorter than its diff:
```python
import numpy as np
import jax
import jax.numpy as jnp
from jax import lax
from jax.experimental import pallas as pl
from jax.experimental.pallas import tpu as pltpu
from jax.sharding import Mesh, PartitionSpec as P

D = 3072
HS = 128
BLOCK = 128
FACTOR = HS ** (-0.5)
LOG2E = 1.4426950408889634
EPSILON = 1e-06
EXCLUDED = -1e30
VMEM_BYTES = 58 * 1024 * 1024
LINE = ("y", "far", "x", "core")


def by_last(left, right):
    return lax.dot_general(
        left, right, (((1,), (1,)), ((), ())), preferred_element_type=jnp.float32
    )


def plain(left, right):
    return jnp.dot(left, right, preferred_element_type=jnp.float32)


def across_rows(values):
    rows, width = values.shape
    total = values[:, :HS]
    for start in range(HS, width, HS):
        total = total + values[:, start : start + HS]
    return jnp.sum(total.T, axis=0, keepdims=True)


def as_columns(row):
    return jnp.broadcast_to(row, (HS, row.shape[1])).T


def squares_kernel(query, key, totals):
    rows = query.shape[0]
    for start in range(0, rows, BLOCK):
        part = query[start : start + BLOCK].astype(jnp.float32)
        totals[:, start : start + BLOCK] = across_rows(part * part)
    part = key[...].astype(jnp.float32)
    totals[:, rows:] = across_rows(part * part)


def squares(query, key):
    return pl.pallas_call(
        squares_kernel,
        out_shape=jax.ShapeDtypeStruct((1, query.shape[0] + key.shape[0]), jnp.float32),
        compiler_params=pltpu.CompilerParams(vmem_limit_bytes=VMEM_BYTES),
        name="squares",
    )(query, key)


def attention_kernel(
    lists, places, scale, query, cot, gain, key_gain,
    key_n, key_o, key_a, val_n, val_o, val_a,
    attended, grad_query, inner, query_gain_grad, key_gain_grad, near, across, own,
    scale_cols, inner_sum, probs_low, grad_low,
):
    head = pl.program_id(0)
    rows = query.shape[0]

    @pl.when(head == 0)
    def _():
        scale_cols[...] = as_columns(scale[...])
        inner_sum[...] = jnp.zeros_like(inner_sum)

    def closed(block, place):
        found = lists[block, 0] == place
        for entry in range(1, lists.shape[1]):
            found = jnp.logical_or(found, lists[block, entry] == place)
        return jnp.where(found, 0.0, EXCLUDED)

    raw = query[...].astype(jnp.float32)
    scaled = raw * scale_cols[...]
    normed = (scaled * gain[...]).astype(jnp.bfloat16)
    keys = jnp.concatenate([key_n[...], key_o[...], key_a[...]], axis=0)
    values = jnp.concatenate([val_n[...], val_o[...], val_a[...]], axis=0)
    span = keys.shape[0] // 3
    upstream = cot[...]
    for block in range(rows // BLOCK):
        part = slice(block * BLOCK, (block + 1) * BLOCK)
        scores = by_last(keys, normed[part]) * (FACTOR * LOG2E)
        scores = jnp.concatenate(
            [
                scores[:span] + closed(block, places[0]),
                scores[span : 2 * span],
                scores[2 * span :] + closed(block, places[1]),
            ],
            axis=0,
        )
        highest = jnp.max(scores, axis=0, keepdims=True)
        weights = jnp.exp2(scores - highest)
        share = 1.0 / jnp.sum(weights, axis=0, keepdims=True)
        probs_low[:, part] = (weights * share).astype(jnp.bfloat16)
        grad_probs = by_last(values, upstream[part])
        delta = jnp.sum(weights * grad_probs, axis=0, keepdims=True) * share
        grad_low[:, part] = (weights * ((grad_probs - delta) * (share * FACTOR))).astype(
            jnp.bfloat16
        )
    low = probs_low[...]
    grads = grad_low[...]
    attended[...] = plain(values.T, low).T.astype(jnp.bfloat16)
    grad = plain(keys.T, grads).T
    grad_query[...] = grad
    inner_sum[...] += raw * grad * gain[...]
    query_gain_grad[...] = jnp.sum(grad * scaled, axis=0, keepdims=True)
    grad_keys = plain(grads, normed)
    grad_values = plain(low, upstream)
    near[0] = grad_keys[:span].astype(jnp.bfloat16)
    near[1] = grad_values[:span].astype(jnp.bfloat16)
    own[0] = grad_keys[span : 2 * span]
    own[1] = grad_values[span : 2 * span]
    across[0] = grad_keys[2 * span :].astype(jnp.bfloat16)
    across[1] = grad_values[2 * span :].astype(jnp.bfloat16)
    key_gain_grad[...] = (
        jnp.sum(grad_keys * keys.astype(jnp.float32), axis=0, keepdims=True) / key_gain[...]
    )

    @pl.when(head == pl.num_programs(0) - 1)
    def _():
        inner[...] = across_rows(inner_sum[...])


def attention(lists, places, scale, query, cot, gain, key_gain, keys, values):
    rows, width = query.shape
    heads = width // HS
    span = keys[0].shape[0]

    def whole(shape):
        return pl.BlockSpec(shape, lambda h: (0,) * len(shape))

    def of_head(*lead):
        return pl.BlockSpec((*lead, HS), lambda h: (0,) * len(lead) + (h,))

    f32, bf16 = jnp.float32, jnp.bfloat16
    shape = jax.ShapeDtypeStruct
    scalars = pl.BlockSpec(memory_space=pltpu.SMEM)
    return pl.pallas_call(
        attention_kernel,
        grid=(heads,),
        in_specs=[scalars, scalars, whole((1, rows)), of_head(rows), of_head(rows)]
        + [of_head(1)] * 2
        + [of_head(span)] * 6,
        out_specs=[
            of_head(rows),
            of_head(rows),
            whole((1, rows)),
            of_head(1),
            of_head(1),
            of_head(2, span),
            of_head(2, span),
            of_head(2, span),
        ],
        out_shape=[
            shape((rows, width), bf16),
            shape((rows, width), f32),
            shape((1, rows), f32),
            shape((1, width), f32),
            shape((1, width), f32),
            shape((2, span, width), bf16),
            shape((2, span, width), bf16),
            shape((2, span, width), f32),
        ],
        scratch_shapes=[
            pltpu.VMEM((rows, HS), f32),
            pltpu.VMEM((rows, HS), f32),
            pltpu.VMEM((3 * span, rows), bf16),
            pltpu.VMEM((3 * span, rows), bf16),
        ],
        compiler_params=pltpu.CompilerParams(vmem_limit_bytes=VMEM_BYTES),
        cost_estimate=pl.CostEstimate(
            flops=12 * rows * 3 * span * width, bytes_accessed=10 * rows * width, transcendentals=0
        ),
        name="attention",
    )(lists, places, scale, query, cot, gain, key_gain, *keys, *values)


def combine_kernel(own, from_near, from_across, key, key_gain, grad_key, value_grad, inner):
    total = own[0] + from_near[0].astype(jnp.float32) + from_across[0].astype(jnp.float32)
    grad_key[...] = total
    value_grad[...] = (
        own[1] + from_near[1].astype(jnp.float32) + from_across[1].astype(jnp.float32)
    ).astype(jnp.bfloat16)
    inner[...] = across_rows(key[...].astype(jnp.float32) * (total * key_gain[...]))


def combine(own, from_near, from_across, key, key_gain):
    _, rows, width = own.shape
    shape = jax.ShapeDtypeStruct
    return pl.pallas_call(
        combine_kernel,
        out_shape=[
            shape((rows, width), jnp.float32),
            shape((rows, width), jnp.bfloat16),
            shape((1, rows), jnp.float32),
        ],
        compiler_params=pltpu.CompilerParams(vmem_limit_bytes=VMEM_BYTES),
        name="combine",
    )(own, from_near, from_across, key, key_gain)


def norms_backward_kernel(
    scales, inner, query, grad_query, query_gain, key, grad_key, key_gain, query_out, key_out
):
    step = pl.program_id(0)
    rows = query.shape[0]

    def one(part, raw, grad, gain):
        scale = scales[:, part]
        shrink = scale * scale * scale * inner[:, part] * (1.0 / D)
        scale, shrink = as_columns(scale), as_columns(shrink)
        pieces = []
        for start in range(0, raw.shape[1], HS):
            lanes = slice(start, start + HS)
            pieces.append(
                scale * (grad[:, lanes] * gain[:, lanes])
                - raw[:, lanes].astype(jnp.float32) * shrink
            )
        return jnp.concatenate(pieces, axis=1).astype(jnp.bfloat16)

    here = pl.ds(pl.multiple_of(step * rows, rows), rows)
    query_out[...] = one(here, query, grad_query, query_gain)

    @pl.when(step == 0)
    def _():
        first = scales.shape[1] - key.shape[0]
        key_out[...] = one(slice(first, scales.shape[1]), key, grad_key, key_gain)


def norms_backward(scales, inner, query, grad_query, query_gain, key, grad_key, key_gain):
    rows, width = query.shape

    def whole(shape):
        return pl.BlockSpec(shape, lambda i: (0,) * len(shape))

    block = pl.BlockSpec((BLOCK, width), lambda i: (i, 0))
    shape = jax.ShapeDtypeStruct
    return pl.pallas_call(
        norms_backward_kernel,
        grid=(rows // BLOCK,),
        in_specs=[
            whole(scales.shape),
            whole(inner.shape),
            block,
            block,
            whole(query_gain.shape),
            whole(key.shape),
            whole(grad_key.shape),
            whole(key_gain.shape),
        ],
        out_specs=[block, whole(key.shape)],
        out_shape=[shape(query.shape, jnp.bfloat16), shape(key.shape, jnp.bfloat16)],
        compiler_params=pltpu.CompilerParams(vmem_limit_bytes=VMEM_BYTES),
        name="norms_backward",
    )(scales, inner, query, grad_query, query_gain, key, grad_key, key_gain)


def inverse_rms(total):
    return lax.rsqrt(total / D + EPSILON)


def swap_near(value):
    return lax.ppermute(value, "core", [(0, 1), (1, 0)])


def swap_across(value):
    size = 1
    for axis in LINE:
        size *= lax.axis_size(axis)
    pairs = []
    for i in range(1, size - 1, 2):
        pairs += [(i, i + 1), (i + 1, i)]
    return lax.ppermute(value, LINE, pairs)


def on_device(video_query, audio_key, audio_value, cotangent, query_gain, key_gain, time_lists):
    place = lax.axis_index(LINE)
    core = lax.axis_index("core")
    places = jnp.stack([place + 1 - 2 * core, place - 1 + 2 * core]).astype(jnp.int32)
    rows = video_query.shape[0]
    query_gain = query_gain[None]
    key_gain = key_gain[None]
    value_n = swap_near(audio_value)
    value_a = swap_across(audio_value)
    totals = lax.psum(squares(video_query, audio_key), "tp")
    scales = inverse_rms(totals)
    key_norm = (audio_key.astype(jnp.float32) * scales[0, rows:, None] * key_gain).astype(
        jnp.bfloat16
    )
    key_norm, value_n, value_a = lax.optimization_barrier((key_norm, value_n, value_a))
    key_n = swap_near(key_norm)
    key_a = swap_across(key_norm)
    (attended, grad_query, inner_query, gain_q, gain_k, to_near, to_across, own) = attention(
        time_lists,
        places,
        scales[:, :rows],
        video_query,
        cotangent,
        query_gain,
        key_gain,
        (key_n, key_norm, key_a),
        (value_n, audio_value, value_a),
    )
    from_across = swap_across(to_across)
    from_near = swap_near(to_near)
    gains = jnp.concatenate([gain_q, gain_k], axis=0)
    for axis in ("core", "x", "y", "far"):
        gains = lax.psum(gains, axis)
    grad_key, audio_value_grad, inner_key = combine(
        own, from_near, from_across, audio_key, key_gain
    )
    inner = lax.psum(jnp.concatenate([inner_query, inner_key], axis=1), "tp")
    video_query_grad, audio_key_grad = norms_backward(
        scales, inner, video_query, grad_query, query_gain, audio_key, grad_key, key_gain
    )
    return attended, video_query_grad, audio_key_grad, audio_value_grad, gains[0], gains[1]


def solution(mesh):
    far = 4
    video, audio, tp = (mesh.shape[name] for name in ("video", "audio", "tp"))
    fine = Mesh(
        np.asarray(mesh.devices).reshape(video // far, far, audio // 2, 2, tp), (*LINE, "tp")
    )
    tokens = P(LINE, "tp")
    per_feature = P("tp")
    return jax.shard_map(
        on_device,
        mesh=fine,
        in_specs=(tokens, tokens, tokens, tokens, per_feature, per_feature, P(LINE, None)),
        out_specs=(tokens, tokens, tokens, tokens, per_feature, per_feature),
        check_vma=False,
    )
```

time: 139 us -> 128 us (0.921)
  Pallas kernels: 10.6 us -> 20.5 us
  other arithmetic: 12.2 us -> 3.12 us
  blocking collectives: 64.3 us -> 58.1 us
  waiting for transfers between devices: 9.08 us -> 5.15 us
  local copies, waits for them, and re-layouts: 9.62 us -> 7.34 us
    psum x3 -> x2, blocking collectives: 43.1 us -> 22.8 us  [the longest x1 12.4 us: on_device(): inner = lax.psum(jnp.concatenate([inner_query, inner_key], axis=1), 'tp')]
    psum x3 -> x4, blocking collectives: 21.1 us -> 35.3 us  [on_device(): gains = lax.psum(gains, axis)]
    pallas_call x1 -> x4, Pallas kernels: 10.6 us -> 20.5 us  [the longest x1 11 us: attention(): pl.pallas_call(attention_kernel, grid=(heads,), in_specs=[scalars, scalar...]
    ppermute x6, waiting for transfers between devices: 9.08 us -> 5.15 us  [the longest x3 5.14 us: swap_across(): return lax.ppermute(value, LINE, pairs)]
    reduce_sum x3 -> x0, other arithmetic: 3.65 us -> none  [the longest x1 1.47 us: on_device(): jnp.sum(query_rows * query_rows, axis=1)]
    convert_element_type x3 -> x1, other arithmetic: 4.21 us -> 1.04 us  [on_device(): (audio_key.astype(jnp.float32) * scales[0, rows:, None] * key_gain).astyp...]
    unnamed x30 -> x17, local copies, waits for them, and re-layouts: 5.92 us -> 3.59 us
    add x1 -> x0, other arithmetic: 2.32 us -> none  [on_device(): combined = own + from_right + from_left]
  transfers between devices with their start and end apart: 6 -> 6, of which waited for: 2 -> 1; matrix products, arithmetic and copies ran while one was open for 2% -> 6% of each run, Pallas kernels for 0% -> 2%
where the time goes in v2:
time: 128 us
  blocking collectives  58.1 us (45%)
  starting transfers between devices  32.8 us (26%)
  Pallas kernels  20.5 us (16%)
  local copies, waits for them, and re-layouts  7.34 us (6%)
  waiting for transfers between devices  5.15 us (4%)
  other arithmetic  3.12 us (2%)
    psum x4, blocking collectives, on_device(): gains = lax.psum(gains, axis)  35.3 us
    ppermute x3, starting transfers between devices, swap_across(): return lax.ppermute(value, LINE, pairs)  27 us
    psum x1, blocking collectives, on_device(): inner = lax.psum(jnp.concatenate([inner_query, inner_key], axis=1), 'tp')  12.4 us
    pallas_call x1, Pallas kernels, attention(): pl.pallas_call(attention_kernel, grid=(heads,), in_specs=[scalars, scalar...  11 us
    psum x1, blocking collectives, on_device(): totals = lax.psum(squares(video_query, audio_key), 'tp')  10.4 us
    ppermute x3, starting transfers between devices, swap_near(): return lax.ppermute(value, 'core', [(0, 1), (1, 0)])  5.76 us
    ppermute x3, waiting for transfers between devices, swap_across(): return lax.ppermute(value, LINE, pairs)  5.14 us
    pallas_call x1, Pallas kernels, norms_backward(): pl.pallas_call(norms_backward_kernel, grid=(rows // BLOCK,), in_specs=[wh...  5.01 us
  transfers between devices with their start and end apart: 6, of which 1 were waited for; matrix products, arithmetic and copies ran while one was open for 6% of the time, Pallas kernels for 2%

profile of v2, /device:TPU:8, one launch (start us, length us, event | category | flops | bytes accessed | tf_op | source)
XLA Modules:
  0.0 127.8 jit_solution(12539456364672184423)
XLA Ops:
  0.6 1.9 %collective-permute-start = (bf16[128,768]{1,0:T(8,128)(2,1)}, bf16[128,768]{1,0:T(8,128)(2,1)S(1)}, u32[]{:S(2)}, u32[]{:S(2)}) collective-permute-start(bf16[128,768]{1,0:T(8,128)(2,1)} %val_o.1), channel_id=1, source_target_pairs={{0,4},{4,0},{1,5},{5,1},{2,6},{6,2},{3,7},{7,3},{8,12},{12,8},{9,1... | collective-permute-start | bytes 589832 | tf_op jit(solution)/shard_map/ppermute | solution.py:270
  2.6 14.9 %collective-permute-start.1 = (bf16[128,768]{1,0:T(8,128)(2,1)}, bf16[128,768]{1,0:T(8,128)(2,1)S(1)}, u32[]{:S(2)}, u32[]{:S(2)}) collective-permute-start(bf16[128,768]{1,0:T(8,128)(2,1)} %val_o.1), channel_id=1, source_target_pairs={{4,8},{8,4},{12,16},{16,12},{20,24},{24,20},{28,32},{32,28},{36,40... | collective-permute-start | bytes 589832 | tf_op jit(solution)/shard_map/ppermute | solution.py:280
  17.5 2.1 %squares.1 = f32[1,768]{1,0:T(1,128)} custom-call(bf16[640,768]{1,0:T(8,128)(2,1)} %query.5, bf16[128,768]{1,0:T(8,128)(2,1)} %key.5), custom_call_target="tpu_custom_call" | custom-call | tf_op jit(solution)/shard_map/squares/pallas_call | solution.py:52
  19.6 10.4 %psum.42 = f32[1,768]{1,0:T(1,128)S(1)} all-reduce(f32[1,768]{1,0:T(1,128)} %squares.1), channel_id=1, replica_groups=mesh['y'=4,'far'=4,'x'=4,'core'=2,'tp'=4] {'tp'}, use_global_device_ids=true, to_apply=%region_0.0 | all-reduce | flops 768 | bytes 6144 | tf_op jit(solution)/shard_map/psum | solution.py:292
  30.0 0.0 copy-start.3
  30.0 1.0 multiply_convert_fusion.key_o
  31.1 0.0 copy-start.2
  31.1 0.0 collective-permute-done.val_n
  31.1 0.0 copy-start.4
  31.1 0.0 collective-permute-done.1.val_a
  31.1 0.0 copy-start.5
  31.1 6.8 %collective-permute-start.3 = (bf16[128,768]{1,0:T(8,128)(2,1)S(1)}, bf16[128,768]{1,0:T(8,128)(2,1)S(1)}, u32[]{:S(2)}, u32[]{:S(2)}) collective-permute-start(bf16[128,768]{1,0:T(8,128)(2,1)S(1)} %multiply_convert_fusion.key_o), channel_id=1, source_target_pairs={{4,8},{8,4},{12,16},{16,12},{20,24},{24,20},{28,32},{32,28},{36,40... | collective-permute-start | bytes 589832 | tf_op jit(solution)/shard_map/ppermute | solution.py:280
  37.9 1.9 %collective-permute-start.2 = (bf16[128,768]{1,0:T(8,128)(2,1)S(1)}, bf16[128,768]{1,0:T(8,128)(2,1)S(1)}, u32[]{:S(2)}, u32[]{:S(2)}) collective-permute-start(bf16[128,768]{1,0:T(8,128)(2,1)S(1)} %multiply_convert_fusion.key_o), channel_id=1, source_target_pairs={{0,4},{4,0},{1,5},{5,1},{2,6},{6,2},{3,7},{7,3},{8,12},{12,8},{9,1... | collective-permute-start | bytes 589832 | tf_op jit(solution)/shard_map/ppermute | solution.py:270
  39.9 1.3 %broadcast_in_dim.7.key_gain = f32[1,768]{1,0:T(1,128)} reshape(f32[768]{0:T(1024)} %param.12) | data formatting | bytes 6144 | tf_op jit(solution)/shard_map/broadcast_in_dim | solution.py:289
  41.1 0.6 slice.16.scale
  41.7 1.3 broadcast_in_dim.6.gain.query_gain
  43.0 1.4 %copy.13.lists = s32[5,4]{1,0:T(8,128)} copy(s32[5,4]{0,1:T(4,128)} %param.13) | data formatting | bytes 160 | tf_op args[6]
  44.3 0.7 pad_add_fusion.places
  45.0 5.1 %collective-permute-done.3.key_a = bf16[128,768]{1,0:T(8,128)(2,1)S(1)} collective-permute-done((bf16[128,768]{1,0:T(8,128)(2,1)S(1)}, bf16[128,768]{1,0:T(8,128)(2,1)S(1)}, u32[]{:S(2)}, u32[]{:S(2)}) %collective-permute-start.3) | collective-permute-done | bytes 196640 | tf_op jit(solution)/shard_map/ppermute | solution.py:280
  50.1 0.0 copy-start.6
  50.1 0.0 collective-permute-done.2.key_n
  50.2 0.0 copy-done.2
  50.2 0.0 copy-done.4
  50.2 0.0 copy-done.5
  50.2 0.7 copy-done.6
  50.8 0.0 copy-start.7
  50.8 0.7 copy-done.7
  51.5 11.0 %attention.1 = (bf16[640,768]{1,0:T(8,128)(2,1)}, f32[640,768]{1,0:T(8,128)}, f32[1,640]{1,0:T(1,128)}, f32[1,768]{1,0:T(1,128)}, f32[1,768]{1,0:T(1,128)}, /*in...) custom-call(s32[5,4]{1,0:T(8,128)} %copy.13.lists, s32[2]{0:T(128)} %pad_add_fusion.places, ...), custom_call_target="tpu_custom_call" | custom-call | flops 2264924160 | bytes 4915200 | tf_op jit(solution)/shard_map/attention/pallas_call | solution.py:145
  62.6 0.0 copy-done.3
  62.6 1.9 %collective-permute-start.4 = (bf16[2,128,768]{2,1,0:T(8,128)(2,1)}, bf16[2,128,768]{2,1,0:T(8,128)(2,1)S(1)}, u32[]{:S(2)}, u32[]{:S(2)}) collective-permute-start(bf16[2,128,768]{2,1,0:T(8,128)(2,1)} %get-tuple-element.28), channel_id=1, source_target_pairs={{0,4},{4,0},{1,5},{5,1},{2,6},{6,2},{3,7},{7,3},{8,12},{12,8},{9,1... | collective-permute-start | bytes 1179656 | tf_op jit(solution)/shard_map/ppermute | solution.py:270
  64.5 5.3 %collective-permute-start.5 = (bf16[2,128,768]{2,1,0:T(8,128)(2,1)}, bf16[2,128,768]{2,1,0:T(8,128)(2,1)S(1)}, u32[]{:S(2)}, u32[]{:S(2)}) collective-permute-start(bf16[2,128,768]{2,1,0:T(8,128)(2,1)} %get-tuple-element.29), channel_id=1, source_target_pairs={{4,8},{8,4},{12,16},{16,12},{20,24},{24,20},{28,32},{32,28},{36,40... | collective-permute-start | bytes 1179656 | tf_op jit(solution)/shard_map/ppermute | solution.py:280
  69.8 0.7 pad_maximum_fusion
  70.5 2.5 %psum.44 = f32[2,768]{1,0:T(2,128)S(1)} all-reduce(f32[2,768]{1,0:T(2,128)S(1)} %pad_maximum_fusion), channel_id=1, replica_groups=mesh['y'=4,'far'=4,'x'=4,'core'=2,'tp'=4] {'core'}, use_global_device_ids=true, to_apply=%region_2.0 | all-reduce | flops 1536 | bytes 12288 | tf_op jit(solution)/shard_map/psum | solution.py:315
  73.0 8.6 %psum.45 = f32[2,768]{1,0:T(2,128)S(1)} all-reduce(f32[2,768]{1,0:T(2,128)S(1)} %psum.44), channel_id=1, replica_groups=mesh['y'=4,'far'=4,'x'=4,'core'=2,'tp'=4] {'x'}, use_global_device_ids=true, to_apply=%region_3.0 | all-reduce | flops 1536 | bytes 12288 | tf_op jit(solution)/shard_map/psum | solution.py:315
  81.5 8.8 %psum.46 = f32[2,768]{1,0:T(2,128)S(1)} all-reduce(f32[2,768]{1,0:T(2,128)S(1)} %psum.45), channel_id=1, replica_groups=mesh['y'=4,'far'=4,'x'=4,'core'=2,'tp'=4] {'y'}, use_global_device_ids=true, to_apply=%region_4.0 | all-reduce | flops 1536 | bytes 12288 | tf_op jit(solution)/shard_map/psum | solution.py:315
  90.4 15.4 %psum.47 = f32[2,768]{1,0:T(2,128)S(1)} all-reduce(f32[2,768]{1,0:T(2,128)S(1)} %psum.46), channel_id=1, replica_groups=mesh['y'=4,'far'=4,'x'=4,'core'=2,'tp'=4] {'far'}, use_global_device_ids=true, to_apply=%region_5.0 | all-reduce | flops 1536 | bytes 12288 | tf_op jit(solution)/shard_map/psum | solution.py:315
  105.8 0.6 slice_reduce_fusion
  106.4 0.0 collective-permute-done.4.from_near
  106.4 0.0 copy-start
  106.4 0.0 collective-permute-done.5.from_across
  106.4 0.0 copy-start.1
  106.4 0.7 copy-done
  107.1 0.2 copy-done.1
  107.3 2.4 %combine.1 = (f32[128,768]{1,0:T(8,128)}, bf16[128,768]{1,0:T(8,128)(2,1)}, f32[1,128]{1,0:T(1,128)}) custom-call(f32[2,128,768]{2,1,0:T(8,128)} %get-tuple-element.27.own, bf16[2,128,768]{2,1,0:T(8,128)(2,1)} %copy-done, bf16[2,128,768]{2,1,0:T(8,128)(2,1)} %copy-done.1, bf16[128,768]{1,0:T(8,128)(2,1)} %key.5, f32[1,768]{1,0:T(1,128)} %broadcast_in_dim.7.key_gain), custom_call_target="tpu_custom_call" | custom-call | tf_op jit(solution)/shard_map/combine/pallas_call | solution.py:197
  109.6 0.7 pad_maximum_fusion.1
  110.3 12.4 %psum.43.inner = f32[1,768]{1,0:T(1,128)} all-reduce(f32[1,768]{1,0:T(1,128)S(1)} %pad_maximum_fusion.1), channel_id=1, replica_groups=mesh['y'=4,'far'=4,'x'=4,'core'=2,'tp'=4] {'tp'}, use_global_device_ids=true, to_apply=%region_1.0 | all-reduce | flops 768 | bytes 6144 | tf_op jit(solution)/shard_map/psum | solution.py:319
  122.8 5.0 %norms_backward.1 = (bf16[640,768]{1,0:T(8,128)(2,1)}, bf16[128,768]{1,0:T(8,128)(2,1)}) custom-call(f32[1,768]{1,0:T(1,128)} %copy-done.3, f32[1,768]{1,0:T(1,128)} %psum.43.inner, bf16[640,768]{1,0:T(8,128)(2,1)} %query.5, f32[640,768]{1,0:T(8,128)} %get-tuple-element.31.grad_query, f32[1,768]{1,0:T(1,128)} %broadcast_in_dim.6.gain.query_gain, ...), custom_call_target="tpu_custom_call" | custom-call | tf_op jit(solution)/shard_map/norms_backward/pallas_call | solution.py:245
  (2 shorter events, 0.0 us)
Async XLA Ops:
  0.6 30.4 %collective-permute-start = (bf16[128,768]{1,0:T(8,128)(2,1)}, bf16[128,768]{1,0:T(8,128)(2,1)S(1)}, u32[]{:S(2)}, u32[]{:S(2)}) collective-permute-start(bf16[128,768]{1,0:T(8,128)(2,1)} %val_o.1), channel_id=1, source_target_pairs={{0,4},{4,0},{1,5},{5,1},{2,6},{6,2},{3,7},{7,3},{8,12},{12,8},{9,1... | collective-permute-start | bytes 589832 | tf_op jit(solution)/shard_map/ppermute | solution.py:270
  2.6 28.5 %collective-permute-start.1 = (bf16[128,768]{1,0:T(8,128)(2,1)}, bf16[128,768]{1,0:T(8,128)(2,1)S(1)}, u32[]{:S(2)}, u32[]{:S(2)}) collective-permute-start(bf16[128,768]{1,0:T(8,128)(2,1)} %val_o.1), channel_id=1, source_target_pairs={{4,8},{8,4},{12,16},{16,12},{20,24},{24,20},{28,32},{32,28},{36,40... | collective-permute-start | bytes 589832 | tf_op jit(solution)/shard_map/ppermute | solution.py:280
  30.0 32.6 %copy-start.3 = (f32[1,768]{1,0:T(1,128)}, f32[1,768]{1,0:T(1,128)S(1)}, u32[]{:S(2)}) copy-start(f32[1,768]{1,0:T(1,128)S(1)} %add_rsqrt_fusion.scales) | copy-start | bytes 9220
  31.1 19.1 %copy-start.2 = (bf16[128,768]{1,0:T(8,128)(2,1)}, bf16[128,768]{1,0:T(8,128)(2,1)S(1)}, u32[]{:S(2)}) copy-start(bf16[128,768]{1,0:T(8,128)(2,1)S(1)} %multiply_convert_fusion.key_o) | copy-start | bytes 589828
  31.1 19.1 %copy-start.4 = (bf16[128,768]{1,0:T(8,128)(2,1)}, bf16[128,768]{1,0:T(8,128)(2,1)S(1)}, u32[]{:S(2)}) copy-start(bf16[128,768]{1,0:T(8,128)(2,1)S(1)} %collective-permute-done.val_n) | copy-start | bytes 589828
  31.1 19.1 %copy-start.5 = (bf16[128,768]{1,0:T(8,128)(2,1)}, bf16[128,768]{1,0:T(8,128)(2,1)S(1)}, u32[]{:S(2)}) copy-start(bf16[128,768]{1,0:T(8,128)(2,1)S(1)} %collective-permute-done.1.val_a) | copy-start | bytes 589828
  31.1 19.0 %collective-permute-start.3 = (bf16[128,768]{1,0:T(8,128)(2,1)S(1)}, bf16[128,768]{1,0:T(8,128)(2,1)S(1)}, u32[]{:S(2)}, u32[]{:S(2)}) collective-permute-start(bf16[128,768]{1,0:T(8,128)(2,1)S(1)} %multiply_convert_fusion.key_o), channel_id=1, source_target_pairs={{4,8},{8,4},{12,16},{16,12},{20,24},{24,20},{28,32},{32,28},{36,40... | collective-permute-start | bytes 589832 | tf_op jit(solution)/shard_map/ppermute | solution.py:280
  37.9 12.2 %collective-permute-start.2 = (bf16[128,768]{1,0:T(8,128)(2,1)S(1)}, bf16[128,768]{1,0:T(8,128)(2,1)S(1)}, u32[]{:S(2)}, u32[]{:S(2)}) collective-permute-start(bf16[128,768]{1,0:T(8,128)(2,1)S(1)} %multiply_convert_fusion.key_o), channel_id=1, source_target_pairs={{0,4},{4,0},{1,5},{5,1},{2,6},{6,2},{3,7},{7,3},{8,12},{12,8},{9,1... | collective-permute-start | bytes 589832 | tf_op jit(solution)/shard_map/ppermute | solution.py:270
  50.1 0.7 copy-start.6
  50.8 0.7 copy-start.7
  62.6 43.8 %collective-permute-start.4 = (bf16[2,128,768]{2,1,0:T(8,128)(2,1)}, bf16[2,128,768]{2,1,0:T(8,128)(2,1)S(1)}, u32[]{:S(2)}, u32[]{:S(2)}) collective-permute-start(bf16[2,128,768]{2,1,0:T(8,128)(2,1)} %get-tuple-element.28), channel_id=1, source_target_pairs={{0,4},{4,0},{1,5},{5,1},{2,6},{6,2},{3,7},{7,3},{8,12},{12,8},{9,1... | collective-permute-start | bytes 1179656 | tf_op jit(solution)/shard_map/ppermute | solution.py:270
  64.5 41.9 %collective-permute-start.5 = (bf16[2,128,768]{2,1,0:T(8,128)(2,1)}, bf16[2,128,768]{2,1,0:T(8,128)(2,1)S(1)}, u32[]{:S(2)}, u32[]{:S(2)}) collective-permute-start(bf16[2,128,768]{2,1,0:T(8,128)(2,1)} %get-tuple-element.29), channel_id=1, source_target_pairs={{4,8},{8,4},{12,16},{16,12},{20,24},{24,20},{28,32},{32,28},{36,40... | collective-permute-start | bytes 1179656 | tf_op jit(solution)/shard_map/ppermute | solution.py:280
  106.4 0.7 copy-start
  106.4 0.9 copy-start.1

commit v3 on v2

v3 whole, which is shorter than its diff:
```python
import numpy as np
import jax
import jax.numpy as jnp
from jax import lax
from jax.experimental import pallas as pl
from jax.experimental.pallas import tpu as pltpu
from jax.sharding import Mesh, PartitionSpec as P

D = 3072
HS = 128
BLOCK = 128
FACTOR = HS ** (-0.5)
LOG2E = 1.4426950408889634
EPSILON = 1e-06
EXCLUDED = -1e30
VMEM_BYTES = 58 * 1024 * 1024
LINE = ("y", "far", "x", "core")


def by_last(left, right):
    return lax.dot_general(
        left, right, (((1,), (1,)), ((), ())), preferred_element_type=jnp.float32
    )


def plain(left, right):
    return jnp.dot(left, right, preferred_element_type=jnp.float32)


def across_rows(values):
    rows, width = values.shape
    total = values[:, :HS]
    for start in range(HS, width, HS):
        total = total + values[:, start : start + HS]
    return jnp.sum(total.T, axis=0, keepdims=True)


def as_columns(row):
    return jnp.broadcast_to(row, (HS, row.shape[1])).T


def inverse_rms(total):
    return lax.rsqrt(total * (1.0 / D) + EPSILON)


def squares_kernel(query, key, totals):
    rows = query.shape[0]
    for start in range(0, rows, BLOCK):
        part = query[start : start + BLOCK].astype(jnp.float32)
        totals[:, start : start + BLOCK] = across_rows(part * part)
    part = key[...].astype(jnp.float32)
    totals[:, rows:] = across_rows(part * part)


def squares(query, key):
    return pl.pallas_call(
        squares_kernel,
        out_shape=jax.ShapeDtypeStruct((1, query.shape[0] + key.shape[0]), jnp.float32),
        compiler_params=pltpu.CompilerParams(vmem_limit_bytes=VMEM_BYTES),
        name="squares",
    )(query, key)


def attention_kernel(
    lists, places, totals, totals_n, totals_a, query, cot, gain, key_gain, own_key, own_value,
    halo_n, halo_a,
    attended, grad_query, inner, gains, near, across, own,
    scale_cols, key_cols, inner_sum, probs_low, grad_low,
):
    head = pl.program_id(0)
    rows = query.shape[0]
    span = own_key.shape[0]

    @pl.when(head == 0)
    def _():
        scale_cols[...] = as_columns(inverse_rms(totals[:, :rows]))
        for index, source in enumerate((totals_n, totals, totals_a)):
            key_cols[index * span : (index + 1) * span] = as_columns(
                inverse_rms(source[:, rows:])
            )
        inner_sum[...] = jnp.zeros_like(inner_sum)

    def closed(block, place):
        found = lists[block, 0] == place
        for entry in range(1, lists.shape[1]):
            found = jnp.logical_or(found, lists[block, entry] == place)
        return jnp.where(found, 0.0, EXCLUDED)

    raw = query[...].astype(jnp.float32)
    scaled = raw * scale_cols[...]
    normed = (scaled * gain[...]).astype(jnp.bfloat16)
    key_raw = jnp.concatenate([halo_n[0], own_key[...], halo_a[0]], axis=0)
    values = jnp.concatenate([halo_n[1], own_value[...], halo_a[1]], axis=0)
    key_scaled = key_raw.astype(jnp.float32) * key_cols[...]
    keys = (key_scaled * key_gain[...]).astype(jnp.bfloat16)
    upstream = cot[...]
    for block in range(rows // BLOCK):
        part = slice(block * BLOCK, (block + 1) * BLOCK)
        scores = by_last(keys, normed[part]) * (FACTOR * LOG2E)
        scores = jnp.concatenate(
            [
                scores[:span] + closed(block, places[0]),
                scores[span : 2 * span],
                scores[2 * span :] + closed(block, places[1]),
            ],
            axis=0,
        )
        highest = jnp.max(scores, axis=0, keepdims=True)
        weights = jnp.exp2(scores - highest)
        share = 1.0 / jnp.sum(weights, axis=0, keepdims=True)
        probs_low[:, part] = (weights * share).astype(jnp.bfloat16)
        grad_probs = by_last(values, upstream[part])
        delta = jnp.sum(weights * grad_probs, axis=0, keepdims=True) * share
        grad_low[:, part] = (weights * ((grad_probs - delta) * (share * FACTOR))).astype(
            jnp.bfloat16
        )
    low = probs_low[...]
    grads = grad_low[...]
    attended[...] = plain(values.T, low).T.astype(jnp.bfloat16)
    grad = plain(keys.T, grads).T
    grad_query[...] = grad
    inner_sum[...] += raw * grad * gain[...]
    grad_keys = plain(grads, normed)
    grad_values = plain(low, upstream)
    gains[0:1] = jnp.sum(grad * scaled, axis=0, keepdims=True)
    gains[1:2] = jnp.sum(grad_keys * key_scaled, axis=0, keepdims=True)
    near[0] = grad_keys[:span].astype(jnp.bfloat16)
    near[1] = grad_values[:span].astype(jnp.bfloat16)
    own[0] = grad_keys[span : 2 * span]
    own[1] = grad_values[span : 2 * span]
    across[0] = grad_keys[2 * span :].astype(jnp.bfloat16)
    across[1] = grad_values[2 * span :].astype(jnp.bfloat16)

    @pl.when(head == pl.num_programs(0) - 1)
    def _():
        inner[...] = across_rows(inner_sum[...])


def attention(
    lists, places, totals, totals_n, totals_a, query, cot, gain, key_gain, key, value, halo_n, halo_a
):
    rows, width = query.shape
    heads = width // HS
    span = key.shape[0]

    def whole(shape):
        return pl.BlockSpec(shape, lambda h: (0,) * len(shape))

    def of_head(*lead):
        return pl.BlockSpec((*lead, HS), lambda h: (0,) * len(lead) + (h,))

    f32, bf16 = jnp.float32, jnp.bfloat16
    shape = jax.ShapeDtypeStruct
    scalars = pl.BlockSpec(memory_space=pltpu.SMEM)
    return pl.pallas_call(
        attention_kernel,
        grid=(heads,),
        in_specs=[scalars] * 2
        + [whole(totals.shape)] * 3
        + [of_head(rows)] * 2
        + [of_head(1)] * 2
        + [of_head(span)] * 2
        + [of_head(2, span)] * 2,
        out_specs=[
            of_head(rows),
            of_head(rows),
            whole((1, rows)),
            of_head(2),
            of_head(2, span),
            of_head(2, span),
            of_head(2, span),
        ],
        out_shape=[
            shape((rows, width), bf16),
            shape((rows, width), f32),
            shape((1, rows), f32),
            shape((2, width), f32),
            shape((2, span, width), bf16),
            shape((2, span, width), bf16),
            shape((2, span, width), f32),
        ],
        scratch_shapes=[
            pltpu.VMEM((rows, HS), f32),
            pltpu.VMEM((3 * span, HS), f32),
            pltpu.VMEM((rows, HS), f32),
            pltpu.VMEM((3 * span, rows), bf16),
            pltpu.VMEM((3 * span, rows), bf16),
        ],
        compiler_params=pltpu.CompilerParams(vmem_limit_bytes=VMEM_BYTES),
        cost_estimate=pl.CostEstimate(
            flops=12 * rows * 3 * span * width, bytes_accessed=10 * rows * width, transcendentals=0
        ),
        name="attention",
    )(lists, places, totals, totals_n, totals_a, query, cot, gain, key_gain, key, value, halo_n, halo_a)


def combine_kernel(
    own, from_near, from_across, key, key_gain, inner_query, grad_key, value_grad, inner
):
    total = own[0] + from_near[0].astype(jnp.float32) + from_across[0].astype(jnp.float32)
    grad_key[...] = total
    value_grad[...] = (
        own[1] + from_near[1].astype(jnp.float32) + from_across[1].astype(jnp.float32)
    ).astype(jnp.bfloat16)
    rows = inner_query.shape[1]
    inner[:, :rows] = inner_query[...]
    inner[:, rows:] = across_rows(key[...].astype(jnp.float32) * (total * key_gain[...]))


def combine(own, from_near, from_across, key, key_gain, inner_query):
    _, rows, width = own.shape
    shape = jax.ShapeDtypeStruct
    return pl.pallas_call(
        combine_kernel,
        out_shape=[
            shape((rows, width), jnp.float32),
            shape((rows, width), jnp.bfloat16),
            shape((1, inner_query.shape[1] + rows), jnp.float32),
        ],
        compiler_params=pltpu.CompilerParams(vmem_limit_bytes=VMEM_BYTES),
        name="combine",
    )(own, from_near, from_across, key, key_gain, inner_query)


def norms_backward_kernel(
    totals, inner_parts, gains, query, grad_query, query_gain, key, grad_key, key_gain,
    query_out, key_out, query_gain_grad, key_gain_grad,
):
    rows = query.shape[0]
    inner = inner_parts[0]
    for index in range(1, len(inner_parts)):
        inner = inner + inner_parts[index]
    scale = inverse_rms(totals[...])
    shrink = scale * scale * scale * inner * (1.0 / D)

    def one(start, out, raw, grad, gain):
        here = slice(start, start + BLOCK)
        wide, less = as_columns(scale[:, here]), as_columns(shrink[:, here])
        first = start % rows
        there = slice(first, first + BLOCK)
        for lane in range(0, raw.shape[1], HS):
            lanes = slice(lane, lane + HS)
            out[there, lanes] = (
                wide * (grad[there, lanes] * gain[:, lanes])
                - raw[there, lanes].astype(jnp.float32) * less
            ).astype(jnp.bfloat16)

    for start in range(0, rows, BLOCK):
        one(start, query_out, query, grad_query, query_gain)
    one(rows, key_out, key, grad_key, key_gain)
    query_gain_grad[...] = gains[0:1]
    key_gain_grad[...] = gains[1:2]


def norms_backward(totals, inner_parts, gains, *rest):
    query, key = rest[0], rest[3]
    count = len(inner_parts)

    def kernel(totals, *refs):
        parts = [ref[...] for ref in refs[:count]]
        norms_backward_kernel(totals, parts, *refs[count:])

    shape = jax.ShapeDtypeStruct
    width = query.shape[1]
    return pl.pallas_call(
        kernel,
        out_shape=[
            shape(query.shape, jnp.bfloat16),
            shape(key.shape, jnp.bfloat16),
            shape((1, width), jnp.float32),
            shape((1, width), jnp.float32),
        ],
        compiler_params=pltpu.CompilerParams(vmem_limit_bytes=VMEM_BYTES),
        name="norms_backward",
    )(totals, *inner_parts, gains, *rest)


def swap_near(value):
    return lax.ppermute(value, "core", [(0, 1), (1, 0)])


def swap_across(value):
    size = 1
    for axis in LINE:
        size *= lax.axis_size(axis)
    pairs = []
    for i in range(1, size - 1, 2):
        pairs += [(i, i + 1), (i + 1, i)]
    return lax.ppermute(value, LINE, pairs)


def on_device(video_query, audio_key, audio_value, cotangent, query_gain, key_gain, time_lists):
    place = lax.axis_index(LINE)
    core = lax.axis_index("core")
    places = jnp.stack([place + 1 - 2 * core, place - 1 + 2 * core]).astype(jnp.int32)
    query_gain = query_gain[None]
    key_gain = key_gain[None]
    held = jnp.stack([audio_key, audio_value])
    halo_a = swap_across(held)
    halo_n = swap_near(held)
    totals = lax.psum(squares(video_query, audio_key), "tp")
    totals_a = swap_across(totals)
    totals_n = swap_near(totals)
    (attended, grad_query, inner_query, gains, to_near, to_across, own) = attention(
        time_lists,
        places,
        totals,
        totals_n,
        totals_a,
        video_query,
        cotangent,
        query_gain,
        key_gain,
        audio_key,
        audio_value,
        halo_n,
        halo_a,
    )
    from_across = swap_across(to_across)
    from_near = swap_near(to_near)
    for axis in ("core", "x", "y"):
        gains = lax.psum(gains, axis)
    grad_key, audio_value_grad, inner = combine(
        own, from_near, from_across, audio_key, key_gain, inner_query
    )
    inner, gains = lax.optimization_barrier((inner, gains))
    size = lax.axis_size("tp")
    inner_parts = [inner] + [
        lax.ppermute(inner, "tp", [(i, (i + by) % size) for i in range(size)])
        for by in range(1, size)
    ]
    gains = lax.psum(gains, "far")
    video_query_grad, audio_key_grad, query_gain_grad, key_gain_grad = norms_backward(
        totals,
        inner_parts,
        gains,
        video_query,
        grad_query,
        query_gain,
        audio_key,
        grad_key,
        key_gain,
    )
    return (
        attended,
        video_query_grad,
        audio_key_grad,
        audio_value_grad,
        query_gain_grad[0],
        key_gain_grad[0],
    )


def solution(mesh):
    far = 4
    video, audio, tp = (mesh.shape[name] for name in ("video", "audio", "tp"))
    fine = Mesh(
        np.asarray(mesh.devices).reshape(video // far, far, audio // 2, 2, tp), (*LINE, "tp")
    )
    tokens = P(LINE, "tp")
    per_feature = P("tp")
    return jax.shard_map(
        on_device,
        mesh=fine,
        in_specs=(tokens, tokens, tokens, tokens, per_feature, per_feature, P(LINE, None)),
        out_specs=(tokens, tokens, tokens, tokens, per_feature, per_feature),
        check_vma=False,
    )
```

time: 128 us -> 126 us (0.984)
  the two profiles are of different devices: /device:TPU:8 before, /device:TPU:32 now
where the time goes in v3:
time: 126 us
  blocking collectives  77.2 us (61%)
  starting transfers between devices  19.5 us (15%)
  Pallas kernels  19.1 us (15%)
  local copies, waits for them, and re-layouts  4.8 us (4%)
  other arithmetic  4.29 us (3%)
    psum x3, blocking collectives, on_device(): gains = lax.psum(gains, axis)  49.6 us
    psum x1, blocking collectives, on_device(): gains = lax.psum(gains, 'far')  16.5 us
    pallas_call x1, Pallas kernels, attention(): pl.pallas_call(attention_kernel, grid=(heads,), in_specs=[scalars] * 2 +...  11.2 us
    psum x1, blocking collectives, on_device(): totals = lax.psum(squares(video_query, audio_key), 'tp')  11.1 us
    ppermute x3, starting transfers between devices, swap_near(): return lax.ppermute(value, 'core', [(0, 1), (1, 0)])  9.78 us
    ppermute x3, starting transfers between devices, on_device(): lax.ppermute(inner, 'tp', [(i, (i + by) % size) for i in range(size)])  7.75 us
    unnamed x27, local copies, waits for them, and re-layouts  3.63 us
    pallas_call x1, Pallas kernels, norms_backward(): pl.pallas_call(kernel, out_shape=[shape(query.shape, jnp.bfloat16), shape...  3.46 us
  transfers between devices with their start and end apart: 9, of which 0 were waited for; matrix products, arithmetic and copies ran while one was open for 2% of the time, Pallas kernels for 2%

profile of v3, /device:TPU:32, one launch (start us, length us, event | category | flops | bytes accessed | tf_op | source)
XLA Modules:
  0.0 125.8 jit_solution(14997849562462666462)
XLA Ops:
  0.6 0.0 copy-start.3
  0.6 0.0 copy-start.4
  0.7 0.0 copy-start.8
  0.7 1.1 pad_maximum_fusion
  1.7 0.7 collective-permute-start.3
  2.4 4.7 %collective-permute-start.2 = (bf16[2,128,768]{2,1,0:T(8,128)(2,1)S(1)}, bf16[2,128,768]{2,1,0:T(8,128)(2,1)S(1)}, u32[]{:S(2)}, u32[]{:S(2)}) collective-permute-start(bf16[2,128,768]{2,1,0:T(8,128)(2,1)S(1)} %pad_maximum_fusion), channel_id=1, source_target_pairs={{0,4},{4,0},{1,5},{5,1},{2,6},{6,2},{3,7},{7,3},{8,12},{12,8},{9,1... | collective-permute-start | bytes 1179656 | tf_op jit(solution)/shard_map/ppermute | solution.py:279
  7.2 2.1 %squares.1 = f32[1,768]{1,0:T(1,128)} custom-call(bf16[640,768]{1,0:T(8,128)(2,1)} %refs_5_.1, bf16[128,768]{1,0:T(8,128)(2,1)} %refs_8_.1), custom_call_target="tpu_custom_call" | custom-call | tf_op jit(solution)/shard_map/squares/pallas_call | solution.py:56
  9.3 11.1 %psum.35.totals = f32[1,768]{1,0:T(1,128)S(1)} all-reduce(f32[1,768]{1,0:T(1,128)} %squares.1), channel_id=1, replica_groups=mesh['y'=4,'far'=4,'x'=4,'core'=2,'tp'=4] {'tp'}, use_global_device_ids=true, to_apply=%region_0.0 | all-reduce | flops 768 | bytes 6144 | tf_op jit(solution)/shard_map/psum | solution.py:301
  20.4 0.0 copy-start.2
  20.4 0.7 collective-permute-start.1
  21.0 3.1 %collective-permute-start = (f32[1,768]{1,0:T(1,128)S(1)}, f32[1,768]{1,0:T(1,128)S(1)}, u32[]{:S(2)}, u32[]{:S(2)}) collective-permute-start(f32[1,768]{1,0:T(1,128)S(1)} %psum.35.totals), channel_id=1, source_target_pairs={{0,4},{4,0},{1,5},{5,1},{2,6},{6,2},{3,7},{7,3},{8,12},{12,8},{9,1... | collective-permute-start | bytes 9224 | tf_op jit(solution)/shard_map/ppermute | solution.py:279
  24.2 0.7 pad_add_fusion.places
  24.8 0.0 copy-done.3
  24.8 0.6 broadcast_in_dim.7.key_gain.refs_10_
  25.4 0.0 copy-done.4
  25.4 0.6 broadcast_in_dim.6.gain.refs_7_
  26.0 0.0 copy-done.8
  26.0 0.7 copy.13.lists
  26.7 0.0 collective-permute-done.1.totals_a
  26.7 0.0 copy-start.11
  26.7 0.0 collective-permute-done.totals_n
  26.7 0.0 copy-start.12
  26.7 0.0 collective-permute-done.3.halo_a
  26.7 0.0 copy-start.9
  26.7 0.0 collective-permute-done.2.halo_n
  26.7 0.0 copy-done.2
  26.8 0.5 copy-done.11
  27.3 0.0 copy-done.12
  27.3 0.2 copy-done.9
  27.5 0.0 copy-start.10
  27.5 0.8 copy-done.10
  28.3 11.2 %attention.1 = (bf16[640,768]{1,0:T(8,128)(2,1)}, f32[640,768]{1,0:T(8,128)}, f32[1,640]{1,0:T(1,128)}, f32[2,768]{1,0:T(2,128)}, bf16[2,128,768]{2,1,0:T(8,128)...) custom-call(s32[5,4]{1,0:T(8,128)} %copy.13.lists, s32[2]{0:T(128)} %pad_add_fusion.places, ...), custom_call_target="tpu_custom_call" | custom-call | flops 2264924160 | bytes 4915200 | tf_op jit(solution)/shard_map/attention/pallas_call | solution.py:155
  39.4 1.9 %collective-permute-start.4 = (bf16[2,128,768]{2,1,0:T(8,128)(2,1)}, bf16[2,128,768]{2,1,0:T(8,128)(2,1)S(1)}, u32[]{:S(2)}, u32[]{:S(2)}) collective-permute-start(bf16[2,128,768]{2,1,0:T(8,128)(2,1)} %get-tuple-element.24), channel_id=1, source_target_pairs={{0,4},{4,0},{1,5},{5,1},{2,6},{6,2},{3,7},{7,3},{8,12},{12,8},{9,1... | collective-permute-start | bytes 1179656 | tf_op jit(solution)/shard_map/ppermute | solution.py:279
  41.3 0.7 collective-permute-start.5
  42.0 4.8 %psum.36 = f32[2,768]{1,0:T(2,128)S(1)} all-reduce(f32[2,768]{1,0:T(2,128)} %get-tuple-element.28), channel_id=1, replica_groups=mesh['y'=4,'far'=4,'x'=4,'core'=2,'tp'=4] {'core'}, use_global_device_ids=true, to_apply=%region_1.0 | all-reduce | flops 1536 | bytes 12288 | tf_op jit(solution)/shard_map/psum | solution.py:322
  46.8 27.8 %psum.37 = f32[2,768]{1,0:T(2,128)S(1)} all-reduce(f32[2,768]{1,0:T(2,128)S(1)} %psum.36), channel_id=1, replica_groups=mesh['y'=4,'far'=4,'x'=4,'core'=2,'tp'=4] {'x'}, use_global_device_ids=true, to_apply=%region_2.0 | all-reduce | flops 1536 | bytes 12288 | tf_op jit(solution)/shard_map/psum | solution.py:322
  74.6 17.1 %psum.38 = f32[2,768]{1,0:T(2,128)S(1)} all-reduce(f32[2,768]{1,0:T(2,128)S(1)} %psum.37), channel_id=1, replica_groups=mesh['y'=4,'far'=4,'x'=4,'core'=2,'tp'=4] {'y'}, use_global_device_ids=true, to_apply=%region_3.0 | all-reduce | flops 1536 | bytes 12288 | tf_op jit(solution)/shard_map/psum | solution.py:322
  91.7 0.0 collective-permute-done.4.from_near
  91.7 0.0 copy-start
  91.7 0.0 collective-permute-done.5.from_across
  91.7 0.0 copy-start.1
  91.7 0.7 copy-done
  92.5 0.1 copy-done.1
  92.6 2.4 %combine.1 = (f32[128,768]{1,0:T(8,128)}, bf16[128,768]{1,0:T(8,128)(2,1)}, f32[1,768]{1,0:T(1,128)}) custom-call(f32[2,128,768]{2,1,0:T(8,128)} %get-tuple-element.23.own, bf16[2,128,768]{2,1,0:T(8,128)(2,1)} %copy-done, bf16[2,128,768]{2,1,0:T(8,128)(2,1)} %copy-done.1, bf16[128,768]{1,0:T(8,128)(2,1)} %refs_8_.1, ...), custom_call_target="tpu_custom_call" | custom-call | tf_op jit(solution)/shard_map/combine/pallas_call | solution.py:213
  94.9 1.9 %collective-permute-start.8 = (f32[1,768]{1,0:T(1,128)}, f32[1,768]{1,0:T(1,128)S(1)}, u32[]{:S(2)}, u32[]{:S(2)}) collective-permute-start(f32[1,768]{1,0:T(1,128)} %get-tuple-element.29.refs_0_), channel_id=1, source_target_pairs={{0,3},{1,0},{2,1},{3,2},{4,7},{5,4},{6,5},{7,6},{8,11},{9,8},{10,9... | collective-permute-start | bytes 9224 | tf_op jit(solution)/shard_map/ppermute | solution.py:329
  96.9 1.9 %collective-permute-start.7 = (f32[1,768]{1,0:T(1,128)}, f32[1,768]{1,0:T(1,128)S(1)}, u32[]{:S(2)}, u32[]{:S(2)}) collective-permute-start(f32[1,768]{1,0:T(1,128)} %get-tuple-element.29.refs_0_), channel_id=1, source_target_pairs={{0,2},{1,3},{2,0},{3,1},{4,6},{5,7},{6,4},{7,5},{8,10},{9,11},{10,... | collective-permute-start | bytes 9224 | tf_op jit(solution)/shard_map/ppermute | solution.py:329
  98.8 3.9 %collective-permute-start.6 = (f32[1,768]{1,0:T(1,128)}, f32[1,768]{1,0:T(1,128)S(1)}, u32[]{:S(2)}, u32[]{:S(2)}) collective-permute-start(f32[1,768]{1,0:T(1,128)} %get-tuple-element.29.refs_0_), channel_id=1, source_target_pairs={{0,1},{1,2},{2,3},{3,0},{4,5},{5,6},{6,7},{7,4},{8,9},{9,10},{10,1... | collective-permute-start | bytes 9224 | tf_op jit(solution)/shard_map/ppermute | solution.py:329
  102.7 16.5 %psum.39.refs_4_ = f32[2,768]{1,0:T(2,128)} all-reduce(f32[2,768]{1,0:T(2,128)S(1)} %psum.38), channel_id=1, replica_groups=mesh['y'=4,'far'=4,'x'=4,'core'=2,'tp'=4] {'far'}, use_global_device_ids=true, to_apply=%region_4.0 | all-reduce | flops 1536 | bytes 12288 | tf_op jit(solution)/shard_map/psum | solution.py:332
  119.2 0.0 collective-permute-done.8.refs_3_
  119.2 0.0 copy-start.5
  119.2 0.0 collective-permute-done.7.refs_2_
  119.2 0.0 copy-start.6
  119.2 0.0 collective-permute-done.6.refs_1_
  119.2 0.0 copy-start.7
  119.2 0.6 copy-done.5
  119.8 0.0 copy-done.6
  119.8 0.0 copy-done.7
  119.8 3.5 %norms_backward.1 = (bf16[640,768]{1,0:T(8,128)(2,1)}, bf16[128,768]{1,0:T(8,128)(2,1)}, f32[1,768]{1,0:T(1,128)}, f32[1,768]{1,0:T(1,128)}) custom-call(f32[1,768]{1,0:T(1,128)} %copy-done.2, f32[1,768]{1,0:T(1,128)} %get-tuple-element.29.refs_0_, f32[1,768]{1,0:T(1,128)} %copy-done.7, f32[1,768]{1,0:T(1,128)} %copy-done.6, f32[1,768]{1,0:T(1,128)} %copy-done.5, ...), custom_call_target="tpu_custom_call" | custom-call | tf_op jit(solution)/shard_map/norms_backward/pallas_call | solution.py:265
  123.3 1.3 %reduce = f32[768]{0:T(1024)} reduce(f32[1,768]{1,0:T(1,128)} %get-tuple-element.36, f32[]{:T(128)} %constant.29), dimensions={0}, to_apply=%get-tuple-element.36.reduce_sub_computation | reduce | bytes 6148 | tf_op jit(solution)/shard_map/norms_backward/pallas_call | solution.py:265
  124.6 1.3 %reduce.1 = f32[768]{0:T(1024)} reduce(f32[1,768]{1,0:T(1,128)} %get-tuple-element.37, f32[]{:T(128)} %constant.29), dimensions={0}, to_apply=%get-tuple-element.37.reduce_sub_computation | reduce | bytes 6148 | tf_op jit(solution)/shard_map/norms_backward/pallas_call | solution.py:265
Async XLA Ops:
  0.6 24.2 %copy-start.3 = (f32[768]{0:T(1024)S(1)}, f32[768]{0:T(1024)}, u32[]{:S(2)}) copy-start(f32[768]{0:T(1024)} %param.12) | copy-start | bytes 9220
  0.6 24.8 %copy-start.4 = (f32[768]{0:T(1024)S(1)}, f32[768]{0:T(1024)}, u32[]{:S(2)}) copy-start(f32[768]{0:T(1024)} %param.11) | copy-start | bytes 9220
  0.7 25.4 %copy-start.8 = (s32[5,4]{0,1:T(4,128)S(1)}, s32[5,4]{0,1:T(4,128)}, u32[]{:S(2)}) copy-start(s32[5,4]{0,1:T(4,128)} %param.13) | copy-start | bytes 244
  1.7 25.0 %collective-permute-start.3 = (bf16[2,128,768]{2,1,0:T(8,128)(2,1)S(1)}, bf16[2,128,768]{2,1,0:T(8,128)(2,1)S(1)}, u32[]{:S(2)}, u32[]{:S(2)}) collective-permute-start(bf16[2,128,768]{2,1,0:T(8,128)(2,1)S(1)} %pad_maximum_fusion), channel_id=1, source_target_pairs={{4,8},{8,4},{12,16},{16,12},{20,24},{24,20},{28,32},{32,28},{36,40... | collective-permute-start | bytes 1179656 | tf_op jit(solution)/shard_map/ppermute | solution.py:289
  2.4 24.3 %collective-permute-start.2 = (bf16[2,128,768]{2,1,0:T(8,128)(2,1)S(1)}, bf16[2,128,768]{2,1,0:T(8,128)(2,1)S(1)}, u32[]{:S(2)}, u32[]{:S(2)}) collective-permute-start(bf16[2,128,768]{2,1,0:T(8,128)(2,1)S(1)} %pad_maximum_fusion), channel_id=1, source_target_pairs={{0,4},{4,0},{1,5},{5,1},{2,6},{6,2},{3,7},{7,3},{8,12},{12,8},{9,1... | collective-permute-start | bytes 1179656 | tf_op jit(solution)/shard_map/ppermute | solution.py:279
  20.4 6.4 %copy-start.2 = (f32[1,768]{1,0:T(1,128)}, f32[1,768]{1,0:T(1,128)S(1)}, u32[]{:S(2)}) copy-start(f32[1,768]{1,0:T(1,128)S(1)} %psum.35.totals) | copy-start | bytes 9220
  20.4 6.3 %collective-permute-start.1 = (f32[1,768]{1,0:T(1,128)S(1)}, f32[1,768]{1,0:T(1,128)S(1)}, u32[]{:S(2)}, u32[]{:S(2)}) collective-permute-start(f32[1,768]{1,0:T(1,128)S(1)} %psum.35.totals), channel_id=1, source_target_pairs={{4,8},{8,4},{12,16},{16,12},{20,24},{24,20},{28,32},{32,28},{36,40... | collective-permute-start | bytes 9224 | tf_op jit(solution)/shard_map/ppermute | solution.py:289
  21.0 5.7 %collective-permute-start = (f32[1,768]{1,0:T(1,128)S(1)}, f32[1,768]{1,0:T(1,128)S(1)}, u32[]{:S(2)}, u32[]{:S(2)}) collective-permute-start(f32[1,768]{1,0:T(1,128)S(1)} %psum.35.totals), channel_id=1, source_target_pairs={{0,4},{4,0},{1,5},{5,1},{2,6},{6,2},{3,7},{7,3},{8,12},{12,8},{9,1... | collective-permute-start | bytes 9224 | tf_op jit(solution)/shard_map/ppermute | solution.py:279
  26.7 0.6 copy-start.11
  26.7 0.6 copy-start.12
  26.7 0.8 copy-start.9
  27.5 0.8 copy-start.10
  39.4 52.3 %collective-permute-start.4 = (bf16[2,128,768]{2,1,0:T(8,128)(2,1)}, bf16[2,128,768]{2,1,0:T(8,128)(2,1)S(1)}, u32[]{:S(2)}, u32[]{:S(2)}) collective-permute-start(bf16[2,128,768]{2,1,0:T(8,128)(2,1)} %get-tuple-element.24), channel_id=1, source_target_pairs={{0,4},{4,0},{1,5},{5,1},{2,6},{6,2},{3,7},{7,3},{8,12},{12,8},{9,1... | collective-permute-start | bytes 1179656 | tf_op jit(solution)/shard_map/ppermute | solution.py:279
  41.3 50.4 %collective-permute-start.5 = (bf16[2,128,768]{2,1,0:T(8,128)(2,1)}, bf16[2,128,768]{2,1,0:T(8,128)(2,1)S(1)}, u32[]{:S(2)}, u32[]{:S(2)}) collective-permute-start(bf16[2,128,768]{2,1,0:T(8,128)(2,1)} %get-tuple-element.25), channel_id=1, source_target_pairs={{4,8},{8,4},{12,16},{16,12},{20,24},{24,20},{28,32},{32,28},{36,40... | collective-permute-start | bytes 1179656 | tf_op jit(solution)/shard_map/ppermute | solution.py:289
  91.7 0.8 copy-start
  91.7 0.9 copy-start.1
  94.9 24.3 %collective-permute-start.8 = (f32[1,768]{1,0:T(1,128)}, f32[1,768]{1,0:T(1,128)S(1)}, u32[]{:S(2)}, u32[]{:S(2)}) collective-permute-start(f32[1,768]{1,0:T(1,128)} %get-tuple-element.29.refs_0_), channel_id=1, source_target_pairs={{0,3},{1,0},{2,1},{3,2},{4,7},{5,4},{6,5},{7,6},{8,11},{9,8},{10,9... | collective-permute-start | bytes 9224 | tf_op jit(solution)/shard_map/ppermute | solution.py:329
  96.9 22.4 %collective-permute-start.7 = (f32[1,768]{1,0:T(1,128)}, f32[1,768]{1,0:T(1,128)S(1)}, u32[]{:S(2)}, u32[]{:S(2)}) collective-permute-start(f32[1,768]{1,0:T(1,128)} %get-tuple-element.29.refs_0_), channel_id=1, source_target_pairs={{0,2},{1,3},{2,0},{3,1},{4,6},{5,7},{6,4},{7,5},{8,10},{9,11},{10,... | collective-permute-start | bytes 9224 | tf_op jit(solution)/shard_map/ppermute | solution.py:329
  98.8 20.4 %collective-permute-start.6 = (f32[1,768]{1,0:T(1,128)}, f32[1,768]{1,0:T(1,128)S(1)}, u32[]{:S(2)}, u32[]{:S(2)}) collective-permute-start(f32[1,768]{1,0:T(1,128)} %get-tuple-element.29.refs_0_), channel_id=1, source_target_pairs={{0,1},{1,2},{2,3},{3,0},{4,5},{5,6},{6,7},{7,4},{8,9},{9,10},{10,1... | collective-permute-start | bytes 9224 | tf_op jit(solution)/shard_map/ppermute | solution.py:329
  119.2 0.6 copy-start.5
  119.2 0.6 copy-start.6
  119.2 0.6 copy-start.7

commit v4 on v3

--- a/solution.py
+++ b/solution.py
@@ -13,7 +13,7 @@
 LOG2E = 1.4426950408889634
 EPSILON = 1e-06
 EXCLUDED = -1e30
-VMEM_BYTES = 58 * 1024 * 1024
+VMEM_BYTES = 24 * 1024 * 1024
 LINE = ("y", "far", "x", "core")
 
 
@@ -86,50 +86,70 @@
             found = jnp.logical_or(found, lists[block, entry] == place)
         return jnp.where(found, 0.0, EXCLUDED)
 
-    raw = query[...].astype(jnp.float32)
-    scaled = raw * scale_cols[...]
-    normed = (scaled * gain[...]).astype(jnp.bfloat16)
-    key_raw = jnp.concatenate([halo_n[0], own_key[...], halo_a[0]], axis=0)
-    values = jnp.concatenate([halo_n[1], own_value[...], halo_a[1]], axis=0)
-    key_scaled = key_raw.astype(jnp.float32) * key_cols[...]
-    keys = (key_scaled * key_gain[...]).astype(jnp.bfloat16)
-    upstream = cot[...]
-    for block in range(rows // BLOCK):
-        part = slice(block * BLOCK, (block + 1) * BLOCK)
-        scores = by_last(keys, normed[part]) * (FACTOR * LOG2E)
+    def soften(lanes, slot, keys, values, normed, upstream, blocks):
+        part = slice(blocks[0] * BLOCK, (blocks[-1] + 1) * BLOCK)
+        scores = by_last(keys, normed[part])
         scores = jnp.concatenate(
-            [
-                scores[:span] + closed(block, places[0]),
-                scores[span : 2 * span],
-                scores[2 * span :] + closed(block, places[1]),
-            ],
+            [scores[:span] + shut(blocks, 0), scores[span : 2 * span], scores[2 * span :] + shut(blocks, 1)],
             axis=0,
         )
         highest = jnp.max(scores, axis=0, keepdims=True)
-        weights = jnp.exp2(scores - highest)
+        weights = jnp.exp2((scores - highest) * (FACTOR * LOG2E))
         share = 1.0 / jnp.sum(weights, axis=0, keepdims=True)
-        probs_low[:, part] = (weights * share).astype(jnp.bfloat16)
+        probs_low[slot, :, part] = (weights * share).astype(jnp.bfloat16)
         grad_probs = by_last(values, upstream[part])
         delta = jnp.sum(weights * grad_probs, axis=0, keepdims=True) * share
-        grad_low[:, part] = (weights * ((grad_probs - delta) * (share * FACTOR))).astype(
+        grad_low[slot, :, part] = (weights * ((grad_probs - delta) * (share * FACTOR))).astype(
             jnp.bfloat16
         )
-    low = probs_low[...]
-    grads = grad_low[...]
-    attended[...] = plain(values.T, low).T.astype(jnp.bfloat16)
-    grad = plain(keys.T, grads).T
-    grad_query[...] = grad
-    inner_sum[...] += raw * grad * gain[...]
-    grad_keys = plain(grads, normed)
-    grad_values = plain(low, upstream)
-    gains[0:1] = jnp.sum(grad * scaled, axis=0, keepdims=True)
-    gains[1:2] = jnp.sum(grad_keys * key_scaled, axis=0, keepdims=True)
-    near[0] = grad_keys[:span].astype(jnp.bfloat16)
-    near[1] = grad_values[:span].astype(jnp.bfloat16)
-    own[0] = grad_keys[span : 2 * span]
-    own[1] = grad_values[span : 2 * span]
-    across[0] = grad_keys[2 * span :].astype(jnp.bfloat16)
-    across[1] = grad_values[2 * span :].astype(jnp.bfloat16)
+
+    def shut(blocks, side):
+        if len(blocks) == 1:
+            return closed(blocks[0], places[side])
+        return jnp.concatenate([jnp.full((1, BLOCK), closed(b, places[side])) for b in blocks], axis=1)
+
+    def prepare(slot):
+        lanes = slice(slot * HS, (slot + 1) * HS)
+        raw = query[:, lanes].astype(jnp.float32)
+        scaled = raw * scale_cols[...]
+        normed = (scaled * gain[:, lanes]).astype(jnp.bfloat16)
+        key_raw = jnp.concatenate([halo_n[0, :, lanes], own_key[:, lanes], halo_a[0, :, lanes]], axis=0)
+        values = jnp.concatenate([halo_n[1, :, lanes], own_value[:, lanes], halo_a[1, :, lanes]], axis=0)
+        key_scaled = key_raw.astype(jnp.float32) * key_cols[...]
+        keys = (key_scaled * key_gain[:, lanes]).astype(jnp.bfloat16)
+        return lanes, raw, scaled, normed, values, key_scaled, keys, cot[:, lanes]
+
+    def finish(slot, lanes, raw, scaled, normed, values, key_scaled, keys, upstream):
+        low = probs_low[slot]
+        grads = grad_low[slot]
+        attended[:, lanes] = plain(values.T, low).T.astype(jnp.bfloat16)
+        grad = plain(keys.T, grads).T
+        grad_query[:, lanes] = grad
+        inner_sum[...] += raw * grad * gain[:, lanes]
+        grad_keys = plain(grads, normed)
+        grad_values = plain(low, upstream)
+        gains[0:1, lanes] = jnp.sum(grad * scaled, axis=0, keepdims=True)
+        gains[1:2, lanes] = jnp.sum(grad_keys * key_scaled, axis=0, keepdims=True)
+        near[0, :, lanes] = grad_keys[:span].astype(jnp.bfloat16)
+        near[1, :, lanes] = grad_values[:span].astype(jnp.bfloat16)
+        own[0, :, lanes] = grad_keys[span : 2 * span]
+        own[1, :, lanes] = grad_values[span : 2 * span]
+        across[0, :, lanes] = grad_keys[2 * span :].astype(jnp.bfloat16)
+        across[1, :, lanes] = grad_values[2 * span :].astype(jnp.bfloat16)
+
+    total = rows // BLOCK
+    groups = [list(range(i, min(i + 2, total))) for i in range(0, total, 2)]
+    held = [prepare(slot) for slot in range(2)]
+    for slot in range(2):
+        lanes, raw, scaled, normed, values, key_scaled, keys, upstream = held[slot]
+        for blocks in groups:
+            soften(lanes, slot, keys, values, normed, upstream, blocks)
+        if slot and 1 == 1:
+            finish(slot - 1, *held[slot - 1])
+        if 1 == 0:
+            finish(slot, *held[slot])
+    if 1 == 1:
+        finish(2 - 1, *held[-1])
 
     @pl.when(head == pl.num_programs(0) - 1)
     def _():
@@ -140,14 +160,14 @@
     lists, places, totals, totals_n, totals_a, query, cot, gain, key_gain, key, value, halo_n, halo_a
 ):
     rows, width = query.shape
-    heads = width // HS
+    heads = width // (2 * HS)
     span = key.shape[0]
 
     def whole(shape):
         return pl.BlockSpec(shape, lambda h: (0,) * len(shape))
 
     def of_head(*lead):
-        return pl.BlockSpec((*lead, HS), lambda h: (0,) * len(lead) + (h,))
+        return pl.BlockSpec((*lead, 2 * HS), lambda h: (0,) * len(lead) + (h,))
 
     f32, bf16 = jnp.float32, jnp.bfloat16
     shape = jax.ShapeDtypeStruct
@@ -183,8 +203,8 @@
             pltpu.VMEM((rows, HS), f32),
             pltpu.VMEM((3 * span, HS), f32),
             pltpu.VMEM((rows, HS), f32),
-            pltpu.VMEM((3 * span, rows), bf16),
-            pltpu.VMEM((3 * span, rows), bf16),
+            pltpu.VMEM((2, 3 * span, rows), bf16),
+            pltpu.VMEM((2, 3 * span, rows), bf16),
         ],
         compiler_params=pltpu.CompilerParams(vmem_limit_bytes=VMEM_BYTES),
         cost_estimate=pl.CostEstimate(
@@ -248,8 +268,8 @@
     for start in range(0, rows, BLOCK):
         one(start, query_out, query, grad_query, query_gain)
     one(rows, key_out, key, grad_key, key_gain)
-    query_gain_grad[...] = gains[0:1]
-    key_gain_grad[...] = gains[1:2]
+    query_gain_grad[...] = gains[0]
+    key_gain_grad[...] = gains[1]
 
 
 def norms_backward(totals, inner_parts, gains, *rest):
@@ -267,8 +287,8 @@
         out_shape=[
             shape(query.shape, jnp.bfloat16),
             shape(key.shape, jnp.bfloat16),
-            shape((1, width), jnp.float32),
-            shape((1, width), jnp.float32),
+            shape((width,), jnp.float32),
+            shape((width,), jnp.float32),
         ],
         compiler_params=pltpu.CompilerParams(vmem_limit_bytes=VMEM_BYTES),
         name="norms_backward",
@@ -295,12 +315,14 @@
     places = jnp.stack([place + 1 - 2 * core, place - 1 + 2 * core]).astype(jnp.int32)
     query_gain = query_gain[None]
     key_gain = key_gain[None]
+    own_parts = squares(video_query, audio_key)
+    parts_a = swap_across(own_parts)
+    parts_n = swap_near(own_parts)
     held = jnp.stack([audio_key, audio_value])
+    held, parts_a, parts_n = lax.optimization_barrier((held, parts_a, parts_n))
     halo_a = swap_across(held)
     halo_n = swap_near(held)
-    totals = lax.psum(squares(video_query, audio_key), "tp")
-    totals_a = swap_across(totals)
-    totals_n = swap_near(totals)
+    totals, totals_n, totals_a = lax.psum((own_parts, parts_n, parts_a), "tp")
     (attended, grad_query, inner_query, gains, to_near, to_across, own) = attention(
         time_lists,
         places,
@@ -346,8 +368,8 @@
         video_query_grad,
         audio_key_grad,
         audio_value_grad,
-        query_gain_grad[0],
-        key_gain_grad[0],
+        query_gain_grad,
+        key_gain_grad,
     )
 
 

time: 126 us -> 133 us (1.056)
  the two profiles are of different devices: /device:TPU:32 before, /device:TPU:8 now
where the time goes in v4:
time: 133 us; the launch traced here: 132 us
  blocking collectives  55.6 us (42%)
  starting transfers between devices  48.3 us (36%)
  Pallas kernels  13.5 us (10%)
  local copies, waits for them, and re-layouts  12.6 us (9%)
    ppermute x3, starting transfers between devices, swap_across(): return lax.ppermute(value, LINE, pairs)  33.9 us
    psum x3, blocking collectives, on_device(): gains = lax.psum(gains, axis)  21.5 us
    psum x1, blocking collectives, on_device(): totals, totals_n, totals_a = lax.psum((own_parts, parts_n, parts_a), 'tp')  18 us
    psum x1, blocking collectives, on_device(): gains = lax.psum(gains, 'far')  16.1 us
    unnamed x43, local copies, waits for them, and re-layouts  12.6 us
    pallas_call x1, Pallas kernels, attention(): pl.pallas_call(attention_kernel, grid=(heads,), in_specs=[scalars] * 2 +...  9.2 us
    ppermute x3, starting transfers between devices, on_device(): lax.ppermute(inner, 'tp', [(i, (i + by) % size) for i in range(size)])  8.49 us
    ppermute x3, starting transfers between devices, swap_near(): return lax.ppermute(value, 'core', [(0, 1), (1, 0)])  5.88 us
  transfers between devices with their start and end apart: 9, of which 1 were waited for; matrix products, arithmetic and copies ran while one was open for 1% of the time, Pallas kernels for 0%

profile of v4, /device:TPU:8, one launch (start us, length us, event | category | flops | bytes accessed | tf_op | source)
XLA Modules:
  0.0 132.4 jit_solution(10970589559589481166)
XLA Ops:
  0.6 0.0 copy-start
  0.6 1.2 copy-done
  1.8 0.0 copy-start.2
  1.8 0.9 copy-done.2
  2.8 0.0 copy-start.18
  2.8 0.0 copy-start.19
  2.8 0.0 copy-start.20
  2.8 0.0 copy-start.1
  2.8 0.0 copy-start.3
  2.8 0.0 copy-start.8
  2.8 0.3 squares.1
  3.1 2.1 %collective-permute-start.1 = (f32[1,768]{1,0:T(1,128)S(1)}, f32[1,768]{1,0:T(1,128)S(1)}, u32[]{:S(2)}, u32[]{:S(2)}) collective-permute-start(f32[1,768]{1,0:T(1,128)S(1)} %squares.1), channel_id=1, source_target_pairs={{0,4},{4,0},{1,5},{5,1},{2,6},{6,2},{3,7},{7,3},{8,12},{12,8},{9,1... | collective-permute-start | bytes 9224 | tf_op jit(solution)/shard_map/ppermute | solution.py:299
  5.2 14.9 %collective-permute-start = (f32[1,768]{1,0:T(1,128)S(1)}, f32[1,768]{1,0:T(1,128)S(1)}, u32[]{:S(2)}, u32[]{:S(2)}) collective-permute-start(f32[1,768]{1,0:T(1,128)S(1)} %squares.1), channel_id=1, source_target_pairs={{4,8},{8,4},{12,16},{16,12},{20,24},{24,20},{28,32},{32,28},{36,40... | collective-permute-start | bytes 9224 | tf_op jit(solution)/shard_map/ppermute | solution.py:309
  20.1 1.0 pad_maximum_fusion
  21.1 0.0 collective-permute-done.1
  21.1 0.3 collective-permute-done
  21.4 10.5 %collective-permute-start.3 = (bf16[2,128,768]{2,1,0:T(8,128)(2,1)S(1)}, bf16[2,128,768]{2,1,0:T(8,128)(2,1)S(1)}, u32[]{:S(2)}, u32[]{:S(2)}) collective-permute-start(bf16[2,128,768]{2,1,0:T(8,128)(2,1)S(1)} %pad_maximum_fusion), channel_id=1, source_target_pairs={{4,8},{8,4},{12,16},{16,12},{20,24},{24,20},{28,32},{32,28},{36,40... | collective-permute-start | bytes 1179656 | tf_op jit(solution)/shard_map/ppermute | solution.py:309
  31.9 1.9 %collective-permute-start.2 = (bf16[2,128,768]{2,1,0:T(8,128)(2,1)S(1)}, bf16[2,128,768]{2,1,0:T(8,128)(2,1)S(1)}, u32[]{:S(2)}, u32[]{:S(2)}) collective-permute-start(bf16[2,128,768]{2,1,0:T(8,128)(2,1)S(1)} %pad_maximum_fusion), channel_id=1, source_target_pairs={{0,4},{4,0},{1,5},{5,1},{2,6},{6,2},{3,7},{7,3},{8,12},{12,8},{9,1... | collective-permute-start | bytes 1179656 | tf_op jit(solution)/shard_map/ppermute | solution.py:299
  33.8 0.0 copy-done.18
  33.9 0.0 copy-done.19
  33.9 0.0 copy-done.20
  33.9 0.1 copy.13.lists
  34.0 0.1 pad_add_fusion.places
  34.1 18.0 %all-reduce = (f32[1,768]{1,0:T(1,128)S(1)}, f32[1,768]{1,0:T(1,128)S(1)}, f32[1,768]{1,0:T(1,128)S(1)}) all-reduce(f32[1,768]{1,0:T(1,128)S(1)} %squares.1, f32[1,768]{1,0:T(1,128)S(1)} %collective-permute-done.1, f32[1,768]{1,0:T(1,128)S(1)} %collective-permute-done), channel_id=1, replica_groups=mesh['y'=4,'far'=4,'x'=4,'core'=2,'tp'=4] {'tp'}, use_global_device_ids=true, to_apply=%region_0.0 | all-reduce | flops 2304 | bytes 18432 | tf_op jit(solution)/shard_map/psum | solution.py:325
  52.1 0.0 copy-start.9
  52.1 0.0 collective-permute-done.3.halo_a
  52.1 0.0 copy-start.14
  52.1 0.7 copy-done.14
  52.9 0.0 collective-permute-done.2.halo_n
  52.9 0.0 copy-start.16
  52.9 0.7 copy-done.16
  53.6 0.0 copy-done.1
  53.6 0.0 copy-done.3
  53.6 0.0 copy-done.8
  53.6 0.0 copy-start.13
  53.6 1.2 copy-done.13
  54.8 1.0 copy-done.15
  55.8 1.0 copy-done.17
  56.8 9.2 %attention.1 = (bf16[640,768]{1,0:T(8,128)(2,1)}, f32[640,768]{1,0:T(8,128)S(1)}, f32[1,640]{1,0:T(1,128)S(1)}, f32[2,768]{1,0:T(2,128)S(1)}, bf16[2,128,768]{2,...) custom-call(s32[5,4]{1,0:T(8,128)S(1)} %copy.13.lists, s32[2]{0:T(128)S(1)} %pad_add_fusion.places, ...), custom_call_target="tpu_custom_call" | custom-call | flops 2264924160 | bytes 4915200 | tf_op jit(solution)/shard_map/attention/pallas_call | solution.py:175
  66.0 0.0 copy-done.9
  66.0 0.9 copy-done.4
  66.9 0.6 copy-done.11
  67.5 1.9 %collective-permute-start.4 = (bf16[2,128,768]{2,1,0:T(8,128)(2,1)}, bf16[2,128,768]{2,1,0:T(8,128)(2,1)S(1)}, u32[]{:S(2)}, u32[]{:S(2)}) collective-permute-start(bf16[2,128,768]{2,1,0:T(8,128)(2,1)} %get-tuple-element.30), channel_id=1, source_target_pairs={{0,4},{4,0},{1,5},{5,1},{2,6},{6,2},{3,7},{7,3},{8,12},{12,8},{9,1... | collective-permute-start | bytes 1179656 | tf_op jit(solution)/shard_map/ppermute | solution.py:299
  69.4 8.5 %collective-permute-start.5 = (bf16[2,128,768]{2,1,0:T(8,128)(2,1)}, bf16[2,128,768]{2,1,0:T(8,128)(2,1)}, u32[]{:S(2)}, u32[]{:S(2)}) collective-permute-start(bf16[2,128,768]{2,1,0:T(8,128)(2,1)} %get-tuple-element.31), channel_id=1, source_target_pairs={{4,8},{8,4},{12,16},{16,12},{20,24},{24,20},{28,32},{32,28},{36,40... | collective-permute-start | bytes 1179656 | tf_op jit(solution)/shard_map/ppermute | solution.py:309
  77.9 3.1 %psum.52 = f32[2,768]{1,0:T(2,128)} all-reduce(f32[2,768]{1,0:T(2,128)S(1)} %get-tuple-element.34), channel_id=1, replica_groups=mesh['y'=4,'far'=4,'x'=4,'core'=2,'tp'=4] {'core'}, use_global_device_ids=true, to_apply=%region_3.0 | all-reduce | flops 1536 | bytes 12288 | tf_op jit(solution)/shard_map/psum | solution.py:344
  80.9 7.9 %psum.53 = f32[2,768]{1,0:T(2,128)S(1)} all-reduce(f32[2,768]{1,0:T(2,128)} %psum.52), channel_id=1, replica_groups=mesh['y'=4,'far'=4,'x'=4,'core'=2,'tp'=4] {'x'}, use_global_device_ids=true, to_apply=%region_4.0 | all-reduce | flops 1536 | bytes 12288 | tf_op jit(solution)/shard_map/psum | solution.py:344
  88.9 10.5 %psum.54 = f32[2,768]{1,0:T(2,128)} all-reduce(f32[2,768]{1,0:T(2,128)S(1)} %psum.53), channel_id=1, replica_groups=mesh['y'=4,'far'=4,'x'=4,'core'=2,'tp'=4] {'y'}, use_global_device_ids=true, to_apply=%region_5.0 | all-reduce | flops 1536 | bytes 12288 | tf_op jit(solution)/shard_map/psum | solution.py:344
  99.4 0.0 collective-permute-done.4.from_near
  99.4 0.8 copy-done.6
  100.1 0.0 collective-permute-done.5.from_across
  100.1 1.1 copy-done.5
  101.3 1.0 copy-done.7
  102.3 0.7 copy-done.12
  102.9 1.9 %combine.1 = (f32[128,768]{1,0:T(8,128)S(1)}, bf16[128,768]{1,0:T(8,128)(2,1)}, f32[1,768]{1,0:T(1,128)}) custom-call(f32[2,128,768]{2,1,0:T(8,128)S(1)} %copy-done.5, bf16[2,128,768]{2,1,0:T(8,128)(2,1)S(1)} %copy-done.7, bf16[2,128,768]{2,1,0:T(8,128)(2,1)} %collective-permute-done.5.from_across, bf16[128,768]{1,0:T(8,128)(2,1)S(1)} %copy-done.3, ...), custom_call_target="tpu_custom_call" | custom-call | tf_op jit(solution)/shard_map/combine/pallas_call | solution.py:233
  104.8 1.9 %collective-permute-start.8 = (f32[1,768]{1,0:T(1,128)}, f32[1,768]{1,0:T(1,128)}, u32[]{:S(2)}, u32[]{:S(2)}) collective-permute-start(f32[1,768]{1,0:T(1,128)} %get-tuple-element.35.refs_0_), channel_id=1, source_target_pairs={{0,3},{1,0},{2,1},{3,2},{4,7},{5,4},{6,5},{7,6},{8,11},{9,8},{10,9... | collective-permute-start | bytes 9224 | tf_op jit(solution)/shard_map/ppermute | solution.py:351
  106.8 4.7 %collective-permute-start.7 = (f32[1,768]{1,0:T(1,128)}, f32[1,768]{1,0:T(1,128)}, u32[]{:S(2)}, u32[]{:S(2)}) collective-permute-start(f32[1,768]{1,0:T(1,128)} %get-tuple-element.35.refs_0_), channel_id=1, source_target_pairs={{0,2},{1,3},{2,0},{3,1},{4,6},{5,7},{6,4},{7,5},{8,10},{9,11},{10,... | collective-permute-start | bytes 9224 | tf_op jit(solution)/shard_map/ppermute | solution.py:351
  111.4 1.9 %collective-permute-start.6 = (f32[1,768]{1,0:T(1,128)}, f32[1,768]{1,0:T(1,128)}, u32[]{:S(2)}, u32[]{:S(2)}) collective-permute-start(f32[1,768]{1,0:T(1,128)} %get-tuple-element.35.refs_0_), channel_id=1, source_target_pairs={{0,1},{1,2},{2,3},{3,0},{4,5},{5,6},{6,7},{7,4},{8,9},{9,10},{10,1... | collective-permute-start | bytes 9224 | tf_op jit(solution)/shard_map/ppermute | solution.py:351
  113.4 16.1 %psum.55.refs_4_ = f32[2,768]{1,0:T(2,128)S(1)} all-reduce(f32[2,768]{1,0:T(2,128)} %psum.54), channel_id=1, replica_groups=mesh['y'=4,'far'=4,'x'=4,'core'=2,'tp'=4] {'far'}, use_global_device_ids=true, to_apply=%region_6.0 | all-reduce | flops 1536 | bytes 12288 | tf_op jit(solution)/shard_map/psum | solution.py:354
  129.5 0.0 collective-permute-done.8.refs_3_
  129.5 0.0 collective-permute-done.7.refs_2_
  129.5 0.0 collective-permute-done.6.refs_1_
  129.5 0.0 copy-start.10
  129.6 0.7 copy-done.10
  130.2 2.1 %norms_backward.1 = (bf16[640,768]{1,0:T(8,128)(2,1)}, bf16[128,768]{1,0:T(8,128)(2,1)}, f32[768]{0:T(1024)}, f32[768]{0:T(1024)}) custom-call(f32[1,768]{1,0:T(1,128)S(1)} %copy-done.10, f32[1,768]{1,0:T(1,128)} %get-tuple-element.35.refs_0_, f32[1,768]{1,0:T(1,128)} %collective-permute-done.6.refs_1_, f32[1,768]{1,0:T(1,128)} %collective-permute-done.7.refs_2_, ...), custom_call_target="tpu_custom_call" | custom-call | tf_op jit(solution)/shard_map/norms_backward/pallas_call | solution.py:285
  (10 shorter events, 0.0 us)
Async XLA Ops:
  0.6 1.2 copy-start
  1.8 0.9 copy-start.2
  2.8 31.1 %copy-start.18 = (f32[768]{0:T(1024)S(1)}, f32[768]{0:T(1024)}, u32[]{:S(2)}) copy-start(f32[768]{0:T(1024)} %param.12) | copy-start | bytes 9220
  2.8 31.1 %copy-start.19 = (f32[768]{0:T(1024)S(1)}, f32[768]{0:T(1024)}, u32[]{:S(2)}) copy-start(f32[768]{0:T(1024)} %param.11) | copy-start | bytes 9220
  2.8 31.1 %copy-start.20 = (s32[5,4]{0,1:T(4,128)S(1)}, s32[5,4]{0,1:T(4,128)}, u32[]{:S(2)}) copy-start(s32[5,4]{0,1:T(4,128)} %param.13) | copy-start | bytes 244
  2.8 50.8 %copy-start.1 = (bf16[640,768]{1,0:T(8,128)(2,1)S(1)}, bf16[640,768]{1,0:T(8,128)(2,1)}, u32[]{:S(2)}) copy-start(bf16[640,768]{1,0:T(8,128)(2,1)} %refs_5_.1) | copy-start | bytes 2949124
  2.8 50.8 %copy-start.3 = (bf16[128,768]{1,0:T(8,128)(2,1)S(1)}, bf16[128,768]{1,0:T(8,128)(2,1)}, u32[]{:S(2)}) copy-start(bf16[128,768]{1,0:T(8,128)(2,1)} %refs_8_.1) | copy-start | bytes 589828
  2.8 50.8 %copy-start.8 = (bf16[128,768]{1,0:T(8,128)(2,1)S(1)}, bf16[128,768]{1,0:T(8,128)(2,1)}, u32[]{:S(2)}) copy-start(bf16[128,768]{1,0:T(8,128)(2,1)} %own_value.1) | copy-start | bytes 589828
  3.1 18.0 %collective-permute-start.1 = (f32[1,768]{1,0:T(1,128)S(1)}, f32[1,768]{1,0:T(1,128)S(1)}, u32[]{:S(2)}, u32[]{:S(2)}) collective-permute-start(f32[1,768]{1,0:T(1,128)S(1)} %squares.1), channel_id=1, source_target_pairs={{0,4},{4,0},{1,5},{5,1},{2,6},{6,2},{3,7},{7,3},{8,12},{12,8},{9,1... | collective-permute-start | bytes 9224 | tf_op jit(solution)/shard_map/ppermute | solution.py:299
  5.2 16.2 %collective-permute-start = (f32[1,768]{1,0:T(1,128)S(1)}, f32[1,768]{1,0:T(1,128)S(1)}, u32[]{:S(2)}, u32[]{:S(2)}) collective-permute-start(f32[1,768]{1,0:T(1,128)S(1)} %squares.1), channel_id=1, source_target_pairs={{4,8},{8,4},{12,16},{16,12},{20,24},{24,20},{28,32},{32,28},{36,40... | collective-permute-start | bytes 9224 | tf_op jit(solution)/shard_map/ppermute | solution.py:309
  21.4 30.7 %collective-permute-start.3 = (bf16[2,128,768]{2,1,0:T(8,128)(2,1)S(1)}, bf16[2,128,768]{2,1,0:T(8,128)(2,1)S(1)}, u32[]{:S(2)}, u32[]{:S(2)}) collective-permute-start(bf16[2,128,768]{2,1,0:T(8,128)(2,1)S(1)} %pad_maximum_fusion), channel_id=1, source_target_pairs={{4,8},{8,4},{12,16},{16,12},{20,24},{24,20},{28,32},{32,28},{36,40... | collective-permute-start | bytes 1179656 | tf_op jit(solution)/shard_map/ppermute | solution.py:309
  31.9 21.0 %collective-permute-start.2 = (bf16[2,128,768]{2,1,0:T(8,128)(2,1)S(1)}, bf16[2,128,768]{2,1,0:T(8,128)(2,1)S(1)}, u32[]{:S(2)}, u32[]{:S(2)}) collective-permute-start(bf16[2,128,768]{2,1,0:T(8,128)(2,1)S(1)} %pad_maximum_fusion), channel_id=1, source_target_pairs={{0,4},{4,0},{1,5},{5,1},{2,6},{6,2},{3,7},{7,3},{8,12},{12,8},{9,1... | collective-permute-start | bytes 1179656 | tf_op jit(solution)/shard_map/ppermute | solution.py:299
  52.1 13.9 %copy-start.9 = (f32[1,768]{1,0:T(1,128)}, f32[1,768]{1,0:T(1,128)S(1)}, u32[]{:S(2)}) copy-start(f32[1,768]{1,0:T(1,128)S(1)} %get-tuple-element.44.totals) | copy-start | bytes 9220
  52.1 0.7 copy-start.14
  52.9 0.7 copy-start.16
  53.6 1.2 copy-start.13
  54.8 1.0 copy-start.15
  55.8 1.0 copy-start.17
  66.0 0.9 copy-start.4
  66.9 0.6 copy-start.11
  67.5 31.9 %collective-permute-start.4 = (bf16[2,128,768]{2,1,0:T(8,128)(2,1)}, bf16[2,128,768]{2,1,0:T(8,128)(2,1)S(1)}, u32[]{:S(2)}, u32[]{:S(2)}) collective-permute-start(bf16[2,128,768]{2,1,0:T(8,128)(2,1)} %get-tuple-element.30), channel_id=1, source_target_pairs={{0,4},{4,0},{1,5},{5,1},{2,6},{6,2},{3,7},{7,3},{8,12},{12,8},{9,1... | collective-permute-start | bytes 1179656 | tf_op jit(solution)/shard_map/ppermute | solution.py:299
  69.4 30.7 %collective-permute-start.5 = (bf16[2,128,768]{2,1,0:T(8,128)(2,1)}, bf16[2,128,768]{2,1,0:T(8,128)(2,1)}, u32[]{:S(2)}, u32[]{:S(2)}) collective-permute-start(bf16[2,128,768]{2,1,0:T(8,128)(2,1)} %get-tuple-element.31), channel_id=1, source_target_pairs={{4,8},{8,4},{12,16},{16,12},{20,24},{24,20},{28,32},{32,28},{36,40... | collective-permute-start | bytes 1179656 | tf_op jit(solution)/shard_map/ppermute | solution.py:309
  99.4 0.8 copy-start.6
  100.1 1.1 copy-start.5
  101.3 1.0 copy-start.7
  102.3 0.7 copy-start.12
  104.8 24.7 %collective-permute-start.8 = (f32[1,768]{1,0:T(1,128)}, f32[1,768]{1,0:T(1,128)}, u32[]{:S(2)}, u32[]{:S(2)}) collective-permute-start(f32[1,768]{1,0:T(1,128)} %get-tuple-element.35.refs_0_), channel_id=1, source_target_pairs={{0,3},{1,0},{2,1},{3,2},{4,7},{5,4},{6,5},{7,6},{8,11},{9,8},{10,9... | collective-permute-start | bytes 9224 | tf_op jit(solution)/shard_map/ppermute | solution.py:351
  106.8 22.8 %collective-permute-start.7 = (f32[1,768]{1,0:T(1,128)}, f32[1,768]{1,0:T(1,128)}, u32[]{:S(2)}, u32[]{:S(2)}) collective-permute-start(f32[1,768]{1,0:T(1,128)} %get-tuple-element.35.refs_0_), channel_id=1, source_target_pairs={{0,2},{1,3},{2,0},{3,1},{4,6},{5,7},{6,4},{7,5},{8,10},{9,11},{10,... | collective-permute-start | bytes 9224 | tf_op jit(solution)/shard_map/ppermute | solution.py:351
  111.4 18.1 %collective-permute-start.6 = (f32[1,768]{1,0:T(1,128)}, f32[1,768]{1,0:T(1,128)}, u32[]{:S(2)}, u32[]{:S(2)}) collective-permute-start(f32[1,768]{1,0:T(1,128)} %get-tuple-element.35.refs_0_), channel_id=1, source_target_pairs={{0,1},{1,2},{2,3},{3,0},{4,5},{5,6},{6,7},{7,4},{8,9},{9,10},{10,1... | collective-permute-start | bytes 9224 | tf_op jit(solution)/shard_map/ppermute | solution.py:351
  129.5 0.7 copy-start.10

commit v5 on v4

--- a/solution.py
+++ b/solution.py
@@ -61,23 +61,38 @@
     )(query, key)
 
 
+def norm_keys_kernel(totals, key, value, gain, held):
+    first = totals.shape[1] - key.shape[0]
+    scale = as_columns(inverse_rms(totals[:, first:]))
+    for start in range(0, key.shape[1], HS):
+        lanes = slice(start, start + HS)
+        held[0, :, lanes] = (key[:, lanes].astype(jnp.float32) * scale * gain[:, lanes]).astype(
+            jnp.bfloat16
+        )
+    held[1] = value[...]
+
+
+def norm_keys(totals, key, value, gain):
+    return pl.pallas_call(
+        norm_keys_kernel,
+        out_shape=jax.ShapeDtypeStruct((2, *key.shape), jnp.bfloat16),
+        compiler_params=pltpu.CompilerParams(vmem_limit_bytes=VMEM_BYTES),
+        name="norm_keys",
+    )(totals, key, value, gain)
+
+
 def attention_kernel(
-    lists, places, totals, totals_n, totals_a, query, cot, gain, key_gain, own_key, own_value,
-    halo_n, halo_a,
+    lists, places, totals, query, cot, gain, key_gain, held, halo_n, halo_a,
     attended, grad_query, inner, gains, near, across, own,
-    scale_cols, key_cols, inner_sum, probs_low, grad_low,
+    scale_cols, inner_sum, probs_low, grad_low,
 ):
     head = pl.program_id(0)
     rows = query.shape[0]
-    span = own_key.shape[0]
+    span = held.shape[1]
 
     @pl.when(head == 0)
     def _():
         scale_cols[...] = as_columns(inverse_rms(totals[:, :rows]))
-        for index, source in enumerate((totals_n, totals, totals_a)):
-            key_cols[index * span : (index + 1) * span] = as_columns(
-                inverse_rms(source[:, rows:])
-            )
         inner_sum[...] = jnp.zeros_like(inner_sum)
 
     def closed(block, place):
@@ -113,13 +128,11 @@
         raw = query[:, lanes].astype(jnp.float32)
         scaled = raw * scale_cols[...]
         normed = (scaled * gain[:, lanes]).astype(jnp.bfloat16)
-        key_raw = jnp.concatenate([halo_n[0, :, lanes], own_key[:, lanes], halo_a[0, :, lanes]], axis=0)
-        values = jnp.concatenate([halo_n[1, :, lanes], own_value[:, lanes], halo_a[1, :, lanes]], axis=0)
-        key_scaled = key_raw.astype(jnp.float32) * key_cols[...]
-        keys = (key_scaled * key_gain[:, lanes]).astype(jnp.bfloat16)
-        return lanes, raw, scaled, normed, values, key_scaled, keys, cot[:, lanes]
-
-    def finish(slot, lanes, raw, scaled, normed, values, key_scaled, keys, upstream):
+        keys = jnp.concatenate([halo_n[0, :, lanes], held[0, :, lanes], halo_a[0, :, lanes]], axis=0)
+        values = jnp.concatenate([halo_n[1, :, lanes], held[1, :, lanes], halo_a[1, :, lanes]], axis=0)
+        return lanes, raw, scaled, normed, values, keys, cot[:, lanes]
+
+    def finish(slot, lanes, raw, scaled, normed, values, keys, upstream):
         low = probs_low[slot]
         grads = grad_low[slot]
         attended[:, lanes] = plain(values.T, low).T.astype(jnp.bfloat16)
@@ -129,7 +142,10 @@
         grad_keys = plain(grads, normed)
         grad_values = plain(low, upstream)
         gains[0:1, lanes] = jnp.sum(grad * scaled, axis=0, keepdims=True)
-        gains[1:2, lanes] = jnp.sum(grad_keys * key_scaled, axis=0, keepdims=True)
+        gains[1:2, lanes] = (
+            jnp.sum(grad_keys * keys.astype(jnp.float32), axis=0, keepdims=True)
+            / key_gain[:, lanes]
+        )
         near[0, :, lanes] = grad_keys[:span].astype(jnp.bfloat16)
         near[1, :, lanes] = grad_values[:span].astype(jnp.bfloat16)
         own[0, :, lanes] = grad_keys[span : 2 * span]
@@ -139,29 +155,27 @@
 
     total = rows // BLOCK
     groups = [list(range(i, min(i + 2, total))) for i in range(0, total, 2)]
-    held = [prepare(slot) for slot in range(2)]
+    ready = [prepare(slot) for slot in range(2)]
     for slot in range(2):
-        lanes, raw, scaled, normed, values, key_scaled, keys, upstream = held[slot]
+        lanes, raw, scaled, normed, values, keys, upstream = ready[slot]
         for blocks in groups:
             soften(lanes, slot, keys, values, normed, upstream, blocks)
         if slot and 1 == 1:
-            finish(slot - 1, *held[slot - 1])
+            finish(slot - 1, *ready[slot - 1])
         if 1 == 0:
-            finish(slot, *held[slot])
+            finish(slot, *ready[slot])
     if 1 == 1:
-        finish(2 - 1, *held[-1])
+        finish(2 - 1, *ready[-1])
 
     @pl.when(head == pl.num_programs(0) - 1)
     def _():
         inner[...] = across_rows(inner_sum[...])
 
 
-def attention(
-    lists, places, totals, totals_n, totals_a, query, cot, gain, key_gain, key, value, halo_n, halo_a
-):
+def attention(lists, places, totals, query, cot, gain, key_gain, held, halo_n, halo_a):
     rows, width = query.shape
     heads = width // (2 * HS)
-    span = key.shape[0]
+    span = held.shape[1]
 
     def whole(shape):
         return pl.BlockSpec(shape, lambda h: (0,) * len(shape))
@@ -176,11 +190,10 @@
         attention_kernel,
         grid=(heads,),
         in_specs=[scalars] * 2
-        + [whole(totals.shape)] * 3
+        + [whole(totals.shape)]
         + [of_head(rows)] * 2
         + [of_head(1)] * 2
-        + [of_head(span)] * 2
-        + [of_head(2, span)] * 2,
+        + [of_head(2, span)] * 3,
         out_specs=[
             of_head(rows),
             of_head(rows),
@@ -201,7 +214,6 @@
         ],
         scratch_shapes=[
             pltpu.VMEM((rows, HS), f32),
-            pltpu.VMEM((3 * span, HS), f32),
             pltpu.VMEM((rows, HS), f32),
             pltpu.VMEM((2, 3 * span, rows), bf16),
             pltpu.VMEM((2, 3 * span, rows), bf16),
@@ -211,7 +223,7 @@
             flops=12 * rows * 3 * span * width, bytes_accessed=10 * rows * width, transcendentals=0
         ),
         name="attention",
-    )(lists, places, totals, totals_n, totals_a, query, cot, gain, key_gain, key, value, halo_n, halo_a)
+    )(lists, places, totals, query, cot, gain, key_gain, held, halo_n, halo_a)
 
 
 def combine_kernel(
@@ -312,29 +324,26 @@
 def on_device(video_query, audio_key, audio_value, cotangent, query_gain, key_gain, time_lists):
     place = lax.axis_index(LINE)
     core = lax.axis_index("core")
+    video_query, audio_key, audio_value, cotangent = (
+        pltpu.with_memory_space_constraint(argument, pltpu.HBM)
+        for argument in (video_query, audio_key, audio_value, cotangent)
+    )
     places = jnp.stack([place + 1 - 2 * core, place - 1 + 2 * core]).astype(jnp.int32)
     query_gain = query_gain[None]
     key_gain = key_gain[None]
-    own_parts = squares(video_query, audio_key)
-    parts_a = swap_across(own_parts)
-    parts_n = swap_near(own_parts)
-    held = jnp.stack([audio_key, audio_value])
-    held, parts_a, parts_n = lax.optimization_barrier((held, parts_a, parts_n))
+    totals = lax.psum(squares(video_query, audio_key), "tp")
+    held = norm_keys(totals, audio_key, audio_value, key_gain)
     halo_a = swap_across(held)
     halo_n = swap_near(held)
-    totals, totals_n, totals_a = lax.psum((own_parts, parts_n, parts_a), "tp")
     (attended, grad_query, inner_query, gains, to_near, to_across, own) = attention(
         time_lists,
         places,
         totals,
-        totals_n,
-        totals_a,
         video_query,
         cotangent,
         query_gain,
         key_gain,
-        audio_key,
-        audio_value,
+        held,
         halo_n,
         halo_a,
     )

time: 133 us -> 124 us (0.932)
  the two profiles are of different devices: /device:TPU:8 before, /device:TPU:32 now
where the time goes in v5:
time: 124 us
  blocking collectives  82.9 us (67%)
  Pallas kernels  16.7 us (13%)
  starting transfers between devices  15.6 us (13%)
  local copies, waits for them, and re-layouts  6.14 us (5%)
  waiting for transfers between devices  1.49 us (1%)
    psum x3, blocking collectives, on_device(): gains = lax.psum(gains, axis)  53.6 us
    psum x1, blocking collectives, on_device(): gains = lax.psum(gains, 'far')  15.5 us
    psum x1, blocking collectives, on_device(): totals = lax.psum(squares(video_query, audio_key), 'tp')  13.8 us
    ppermute x3, starting transfers between devices, on_device(): lax.ppermute(inner, 'tp', [(i, (i + by) % size) for i in range(size)])  10.2 us
    pallas_call x1, Pallas kernels, attention(): pl.pallas_call(attention_kernel, grid=(heads,), in_specs=[scalars] * 2 +...  9.52 us
    unnamed x19, local copies, waits for them, and re-layouts  5.44 us
    ppermute x2, starting transfers between devices, swap_near(): return lax.ppermute(value, 'core', [(0, 1), (1, 0)])  4.01 us
    pallas_call x1, Pallas kernels, norms_backward(): pl.pallas_call(kernel, out_shape=[shape(query.shape, jnp.bfloat16), shape...  2.7 us
  transfers between devices with their start and end apart: 7, of which 1 were waited for; matrix products, arithmetic and copies ran while one was open for 0% of the time, Pallas kernels for 0%

profile of v5, /device:TPU:32, one launch (start us, length us, event | category | flops | bytes accessed | tf_op | source)
XLA Modules:
  0.0 123.7 jit_solution(17345744752375286793)
XLA Ops:
  0.6 0.0 copy-start.7
  0.6 0.0 copy-start.8
  0.7 0.7 broadcast_in_dim.7.gain.key_gain.refs_10_
  1.4 1.5 %squares.1 = f32[1,768]{1,0:T(1,128)S(1)} custom-call(bf16[640,768]{1,0:T(8,128)(2,1)} %refs_5_.1, bf16[128,768]{1,0:T(8,128)(2,1)} %refs_8_.1), custom_call_target="tpu_custom_call" | custom-call | tf_op jit(solution)/shard_map/squares/pallas_call | solution.py:56
  2.9 13.8 %psum.35.totals = f32[1,768]{1,0:T(1,128)S(1)} all-reduce(f32[1,768]{1,0:T(1,128)S(1)} %squares.1), channel_id=1, replica_groups=mesh['y'=4,'far'=4,'x'=4,'core'=2,'tp'=4] {'tp'}, use_global_device_ids=true, to_apply=%region_0.0 | all-reduce | flops 768 | bytes 6144 | tf_op jit(solution)/shard_map/psum | solution.py:334
  16.7 1.2 norm_keys.1.held
  17.8 0.7 collective-permute-start.1
  18.5 1.9 %collective-permute-start = (bf16[2,128,768]{2,1,0:T(8,128)(2,1)S(1)}, bf16[2,128,768]{2,1,0:T(8,128)(2,1)S(1)}, u32[]{:S(2)}, u32[]{:S(2)}) collective-permute-start(bf16[2,128,768]{2,1,0:T(8,128)(2,1)S(1)} %norm_keys.1.held), channel_id=1, source_target_pairs={{0,4},{4,0},{1,5},{5,1},{2,6},{6,2},{3,7},{7,3},{8,12},{12,8},{9,1... | collective-permute-start | bytes 1179656 | tf_op jit(solution)/shard_map/ppermute | solution.py:311
  20.5 0.0 copy-done.7
  20.5 0.0 copy-done.8
  20.5 0.1 copy.13.lists
  20.6 0.1 pad_add_fusion.places
  20.7 0.0 collective-permute-done.1.halo_a
  20.7 1.5 %collective-permute-done.halo_n = bf16[2,128,768]{2,1,0:T(8,128)(2,1)S(1)} collective-permute-done((bf16[2,128,768]{2,1,0:T(8,128)(2,1)S(1)}, bf16[2,128,768]{2,1,0:T(8,128)(2,1)S(1)}, u32[]{:S(2)}, u32[]{:S(2)}) %collective-permute-start) | collective-permute-done | bytes 393248 | tf_op jit(solution)/shard_map/ppermute | solution.py:311
  22.2 0.0 copy-start.5
  22.2 0.7 copy-done.5
  22.9 0.0 copy-start.6
  22.9 1.0 copy-done.6
  23.9 9.5 %attention.1 = (bf16[640,768]{1,0:T(8,128)(2,1)}, f32[640,768]{1,0:T(8,128)S(1)}, f32[1,640]{1,0:T(1,128)S(1)}, f32[2,768]{1,0:T(2,128)S(1)}, bf16[2,128,768]{2,...) custom-call(s32[5,4]{1,0:T(8,128)S(1)} %copy.13.lists, s32[2]{0:T(128)S(1)} %pad_add_fusion.places, ...), custom_call_target="tpu_custom_call" | custom-call | flops 2264924160 | bytes 4915200 | tf_op jit(solution)/shard_map/attention/pallas_call | solution.py:189
  33.4 0.0 copy-start.2
  33.4 0.6 copy-done.2
  34.0 0.0 copy-start.3
  34.0 0.6 copy-done.3
  34.6 2.1 %collective-permute-start.2 = (bf16[2,128,768]{2,1,0:T(8,128)(2,1)}, bf16[2,128,768]{2,1,0:T(8,128)(2,1)S(1)}, u32[]{:S(2)}, u32[]{:S(2)}) collective-permute-start(bf16[2,128,768]{2,1,0:T(8,128)(2,1)} %get-tuple-element.24), channel_id=1, source_target_pairs={{0,4},{4,0},{1,5},{5,1},{2,6},{6,2},{3,7},{7,3},{8,12},{12,8},{9,1... | collective-permute-start | bytes 1179656 | tf_op jit(solution)/shard_map/ppermute | solution.py:311
  36.7 0.7 collective-permute-start.3
  37.4 5.9 %psum.36 = f32[2,768]{1,0:T(2,128)} all-reduce(f32[2,768]{1,0:T(2,128)} %copy-done.2), channel_id=1, replica_groups=mesh['y'=4,'far'=4,'x'=4,'core'=2,'tp'=4] {'core'}, use_global_device_ids=true, to_apply=%region_1.0 | all-reduce | flops 1536 | bytes 12288 | tf_op jit(solution)/shard_map/psum | solution.py:353
  43.3 28.1 %psum.37 = f32[2,768]{1,0:T(2,128)} all-reduce(f32[2,768]{1,0:T(2,128)} %psum.36), channel_id=1, replica_groups=mesh['y'=4,'far'=4,'x'=4,'core'=2,'tp'=4] {'x'}, use_global_device_ids=true, to_apply=%region_2.0 | all-reduce | flops 1536 | bytes 12288 | tf_op jit(solution)/shard_map/psum | solution.py:353
  71.4 19.5 %psum.38 = f32[2,768]{1,0:T(2,128)} all-reduce(f32[2,768]{1,0:T(2,128)} %psum.37), channel_id=1, replica_groups=mesh['y'=4,'far'=4,'x'=4,'core'=2,'tp'=4] {'y'}, use_global_device_ids=true, to_apply=%region_3.0 | all-reduce | flops 1536 | bytes 12288 | tf_op jit(solution)/shard_map/psum | solution.py:353
  91.0 0.0 collective-permute-done.2.from_near
  91.0 0.0 collective-permute-done.3.from_across
  91.0 0.0 copy-start
  91.0 0.7 copy-done
  91.7 0.0 copy-start.1
  91.7 1.0 copy-done.1
  92.7 0.0 copy-start.4
  92.7 0.7 copy-done.4
  93.4 1.8 %combine.1 = (f32[128,768]{1,0:T(8,128)S(1)}, bf16[128,768]{1,0:T(8,128)(2,1)}, f32[1,768]{1,0:T(1,128)S(1)}) custom-call(f32[2,128,768]{2,1,0:T(8,128)S(1)} %get-tuple-element.23.own, bf16[2,128,768]{2,1,0:T(8,128)(2,1)S(1)} %collective-permute-done.2.from_near, bf16[2,128,768]{2,1,0:T(8,128)(2,1)S(1)} %copy-done.1, bf16[128,768]{1,0:T(8,128)(2,1)} %refs_8_.1, ...), custom_call_target="tpu_custom_call" | custom-call | tf_op jit(solution)/shard_map/combine/pallas_call | solution.py:245
  95.2 4.3 %collective-permute-start.6 = (f32[1,768]{1,0:T(1,128)S(1)}, f32[1,768]{1,0:T(1,128)S(1)}, u32[]{:S(2)}, u32[]{:S(2)}) collective-permute-start(f32[1,768]{1,0:T(1,128)S(1)} %get-tuple-element.29.refs_0_), channel_id=1, source_target_pairs={{0,3},{1,0},{2,1},{3,2},{4,7},{5,4},{6,5},{7,6},{8,11},{9,8},{10,9... | collective-permute-start | bytes 9224 | tf_op jit(solution)/shard_map/ppermute | solution.py:360
  99.5 1.9 %collective-permute-start.5 = (f32[1,768]{1,0:T(1,128)S(1)}, f32[1,768]{1,0:T(1,128)S(1)}, u32[]{:S(2)}, u32[]{:S(2)}) collective-permute-start(f32[1,768]{1,0:T(1,128)S(1)} %get-tuple-element.29.refs_0_), channel_id=1, source_target_pairs={{0,2},{1,3},{2,0},{3,1},{4,6},{5,7},{6,4},{7,5},{8,10},{9,11},{10,... | collective-permute-start | bytes 9224 | tf_op jit(solution)/shard_map/ppermute | solution.py:360
  101.5 4.0 %collective-permute-start.4 = (f32[1,768]{1,0:T(1,128)S(1)}, f32[1,768]{1,0:T(1,128)S(1)}, u32[]{:S(2)}, u32[]{:S(2)}) collective-permute-start(f32[1,768]{1,0:T(1,128)S(1)} %get-tuple-element.29.refs_0_), channel_id=1, source_target_pairs={{0,1},{1,2},{2,3},{3,0},{4,5},{5,6},{6,7},{7,4},{8,9},{9,10},{10,1... | collective-permute-start | bytes 9224 | tf_op jit(solution)/shard_map/ppermute | solution.py:360
  105.4 15.5 %psum.39.refs_4_ = f32[2,768]{1,0:T(2,128)S(1)} all-reduce(f32[2,768]{1,0:T(2,128)} %psum.38), channel_id=1, replica_groups=mesh['y'=4,'far'=4,'x'=4,'core'=2,'tp'=4] {'far'}, use_global_device_ids=true, to_apply=%region_4.0 | all-reduce | flops 1536 | bytes 12288 | tf_op jit(solution)/shard_map/psum | solution.py:363
  120.9 0.0 collective-permute-done.6.refs_3_
  121.0 0.0 collective-permute-done.5.refs_2_
  121.0 0.0 collective-permute-done.4.refs_1_
  121.0 2.7 %norms_backward.1 = (bf16[640,768]{1,0:T(8,128)(2,1)}, bf16[128,768]{1,0:T(8,128)(2,1)}, f32[768]{0:T(1024)}, f32[768]{0:T(1024)}) custom-call(f32[1,768]{1,0:T(1,128)S(1)} %psum.35.totals, f32[1,768]{1,0:T(1,128)S(1)} %get-tuple-element.29.refs_0_, f32[1,768]{1,0:T(1,128)S(1)} %collective-permute-done.4.refs_1_, ...), custom_call_target="tpu_custom_call" | custom-call | tf_op jit(solution)/shard_map/norms_backward/pallas_call | solution.py:297
  (1 shorter events, 0.0 us)
Async XLA Ops:
  0.6 19.8 %copy-start.7 = (f32[768]{0:T(1024)S(1)}, f32[768]{0:T(1024)}, u32[]{:S(2)}) copy-start(f32[768]{0:T(1024)} %param.11) | copy-start | bytes 9220
  0.6 19.9 %copy-start.8 = (s32[5,4]{0,1:T(4,128)S(1)}, s32[5,4]{0,1:T(4,128)}, u32[]{:S(2)}) copy-start(s32[5,4]{0,1:T(4,128)} %param.13) | copy-start | bytes 244
  17.8 2.8 %collective-permute-start.1 = (bf16[2,128,768]{2,1,0:T(8,128)(2,1)S(1)}, bf16[2,128,768]{2,1,0:T(8,128)(2,1)S(1)}, u32[]{:S(2)}, u32[]{:S(2)}) collective-permute-start(bf16[2,128,768]{2,1,0:T(8,128)(2,1)S(1)} %norm_keys.1.held), channel_id=1, source_target_pairs={{4,8},{8,4},{12,16},{16,12},{20,24},{24,20},{28,32},{32,28},{36,40... | collective-permute-start | bytes 1179656 | tf_op jit(solution)/shard_map/ppermute | solution.py:321
  18.5 3.6 %collective-permute-start = (bf16[2,128,768]{2,1,0:T(8,128)(2,1)S(1)}, bf16[2,128,768]{2,1,0:T(8,128)(2,1)S(1)}, u32[]{:S(2)}, u32[]{:S(2)}) collective-permute-start(bf16[2,128,768]{2,1,0:T(8,128)(2,1)S(1)} %norm_keys.1.held), channel_id=1, source_target_pairs={{0,4},{4,0},{1,5},{5,1},{2,6},{6,2},{3,7},{7,3},{8,12},{12,8},{9,1... | collective-permute-start | bytes 1179656 | tf_op jit(solution)/shard_map/ppermute | solution.py:311
  22.2 0.7 copy-start.5
  22.9 1.0 copy-start.6
  33.4 0.6 copy-start.2
  34.0 0.6 copy-start.3
  34.6 56.4 %collective-permute-start.2 = (bf16[2,128,768]{2,1,0:T(8,128)(2,1)}, bf16[2,128,768]{2,1,0:T(8,128)(2,1)S(1)}, u32[]{:S(2)}, u32[]{:S(2)}) collective-permute-start(bf16[2,128,768]{2,1,0:T(8,128)(2,1)} %get-tuple-element.24), channel_id=1, source_target_pairs={{0,4},{4,0},{1,5},{5,1},{2,6},{6,2},{3,7},{7,3},{8,12},{12,8},{9,1... | collective-permute-start | bytes 1179656 | tf_op jit(solution)/shard_map/ppermute | solution.py:311
  36.7 54.3 %collective-permute-start.3 = (bf16[2,128,768]{2,1,0:T(8,128)(2,1)}, bf16[2,128,768]{2,1,0:T(8,128)(2,1)S(1)}, u32[]{:S(2)}, u32[]{:S(2)}) collective-permute-start(bf16[2,128,768]{2,1,0:T(8,128)(2,1)} %get-tuple-element.25), channel_id=1, source_target_pairs={{4,8},{8,4},{12,16},{16,12},{20,24},{24,20},{28,32},{32,28},{36,40... | collective-permute-start | bytes 1179656 | tf_op jit(solution)/shard_map/ppermute | solution.py:321
  91.0 0.7 copy-start
  91.7 1.0 copy-start.1
  92.7 0.7 copy-start.4
  95.2 25.7 %collective-permute-start.6 = (f32[1,768]{1,0:T(1,128)S(1)}, f32[1,768]{1,0:T(1,128)S(1)}, u32[]{:S(2)}, u32[]{:S(2)}) collective-permute-start(f32[1,768]{1,0:T(1,128)S(1)} %get-tuple-element.29.refs_0_), channel_id=1, source_target_pairs={{0,3},{1,0},{2,1},{3,2},{4,7},{5,4},{6,5},{7,6},{8,11},{9,8},{10,9... | collective-permute-start | bytes 9224 | tf_op jit(solution)/shard_map/ppermute | solution.py:360
  99.5 21.4 %collective-permute-start.5 = (f32[1,768]{1,0:T(1,128)S(1)}, f32[1,768]{1,0:T(1,128)S(1)}, u32[]{:S(2)}, u32[]{:S(2)}) collective-permute-start(f32[1,768]{1,0:T(1,128)S(1)} %get-tuple-element.29.refs_0_), channel_id=1, source_target_pairs={{0,2},{1,3},{2,0},{3,1},{4,6},{5,7},{6,4},{7,5},{8,10},{9,11},{10,... | collective-permute-start | bytes 9224 | tf_op jit(solution)/shard_map/ppermute | solution.py:360
  101.5 19.5 %collective-permute-start.4 = (f32[1,768]{1,0:T(1,128)S(1)}, f32[1,768]{1,0:T(1,128)S(1)}, u32[]{:S(2)}, u32[]{:S(2)}) collective-permute-start(f32[1,768]{1,0:T(1,128)S(1)} %get-tuple-element.29.refs_0_), channel_id=1, source_target_pairs={{0,1},{1,2},{2,3},{3,0},{4,5},{5,6},{6,7},{7,4},{8,9},{9,10},{10,1... | collective-permute-start | bytes 9224 | tf_op jit(solution)/shard_map/ppermute | solution.py:360

commit v6 on v5

--- a/solution.py
+++ b/solution.py
@@ -66,7 +66,7 @@
     scale = as_columns(inverse_rms(totals[:, first:]))
     for start in range(0, key.shape[1], HS):
         lanes = slice(start, start + HS)
-        held[0, :, lanes] = (key[:, lanes].astype(jnp.float32) * scale * gain[:, lanes]).astype(
+        held[0, :, lanes] = (key[:, lanes].astype(jnp.float32) * scale * gain[lanes][None]).astype(
             jnp.bfloat16
         )
     held[1] = value[...]
@@ -84,7 +84,7 @@
 def attention_kernel(
     lists, places, totals, query, cot, gain, key_gain, held, halo_n, halo_a,
     attended, grad_query, inner, gains, near, across, own,
-    scale_cols, inner_sum, probs_low, grad_low,
+    scale_cols, inner_sum, key_sum, probs_low, grad_low,
 ):
     head = pl.program_id(0)
     rows = query.shape[0]
@@ -94,6 +94,7 @@
     def _():
         scale_cols[...] = as_columns(inverse_rms(totals[:, :rows]))
         inner_sum[...] = jnp.zeros_like(inner_sum)
+        key_sum[...] = jnp.zeros_like(key_sum)
 
     def closed(block, place):
         found = lists[block, 0] == place
@@ -142,10 +143,9 @@
         grad_keys = plain(grads, normed)
         grad_values = plain(low, upstream)
         gains[0:1, lanes] = jnp.sum(grad * scaled, axis=0, keepdims=True)
-        gains[1:2, lanes] = (
-            jnp.sum(grad_keys * keys.astype(jnp.float32), axis=0, keepdims=True)
-            / key_gain[:, lanes]
-        )
+        products = grad_keys * keys.astype(jnp.float32)
+        key_sum[...] += products
+        gains[1:2, lanes] = jnp.sum(products, axis=0, keepdims=True) / key_gain[:, lanes]
         near[0, :, lanes] = grad_keys[:span].astype(jnp.bfloat16)
         near[1, :, lanes] = grad_values[:span].astype(jnp.bfloat16)
         own[0, :, lanes] = grad_keys[span : 2 * span]
@@ -169,7 +169,8 @@
 
     @pl.when(head == pl.num_programs(0) - 1)
     def _():
-        inner[...] = across_rows(inner_sum[...])
+        inner[:, :rows] = across_rows(inner_sum[...])
+        inner[:, rows:] = across_rows(key_sum[...])
 
 
 def attention(lists, places, totals, query, cot, gain, key_gain, held, halo_n, halo_a):
@@ -197,7 +198,7 @@
         out_specs=[
             of_head(rows),
             of_head(rows),
-            whole((1, rows)),
+            whole((1, rows + 3 * span)),
             of_head(2),
             of_head(2, span),
             of_head(2, span),
@@ -206,15 +207,16 @@
         out_shape=[
             shape((rows, width), bf16),
             shape((rows, width), f32),
-            shape((1, rows), f32),
-            shape((2, width), f32),
-            shape((2, span, width), bf16),
-            shape((2, span, width), bf16),
+            pltpu.HBM((1, rows + 3 * span), f32),
+            pltpu.HBM((2, width), f32),
+            pltpu.HBM((2, span, width), bf16),
+            pltpu.HBM((2, span, width), bf16),
             shape((2, span, width), f32),
         ],
         scratch_shapes=[
             pltpu.VMEM((rows, HS), f32),
             pltpu.VMEM((rows, HS), f32),
+            pltpu.VMEM((3 * span, HS), f32),
             pltpu.VMEM((2, 3 * span, rows), bf16),
             pltpu.VMEM((2, 3 * span, rows), bf16),
         ],
@@ -226,85 +228,75 @@
     )(lists, places, totals, query, cot, gain, key_gain, held, halo_n, halo_a)
 
 
-def combine_kernel(
-    own, from_near, from_across, key, key_gain, inner_query, grad_key, value_grad, inner
-):
-    total = own[0] + from_near[0].astype(jnp.float32) + from_across[0].astype(jnp.float32)
-    grad_key[...] = total
-    value_grad[...] = (
-        own[1] + from_near[1].astype(jnp.float32) + from_across[1].astype(jnp.float32)
-    ).astype(jnp.bfloat16)
-    rows = inner_query.shape[1]
-    inner[:, :rows] = inner_query[...]
-    inner[:, rows:] = across_rows(key[...].astype(jnp.float32) * (total * key_gain[...]))
-
-
-def combine(own, from_near, from_across, key, key_gain, inner_query):
-    _, rows, width = own.shape
-    shape = jax.ShapeDtypeStruct
-    return pl.pallas_call(
-        combine_kernel,
-        out_shape=[
-            shape((rows, width), jnp.float32),
-            shape((rows, width), jnp.bfloat16),
-            shape((1, inner_query.shape[1] + rows), jnp.float32),
-        ],
-        compiler_params=pltpu.CompilerParams(vmem_limit_bytes=VMEM_BYTES),
-        name="combine",
-    )(own, from_near, from_across, key, key_gain, inner_query)
-
-
 def norms_backward_kernel(
-    totals, inner_parts, gains, query, grad_query, query_gain, key, grad_key, key_gain,
-    query_out, key_out, query_gain_grad, key_gain_grad,
+    totals, inner, inner_n, inner_a, gains, query, grad_query, query_gain, key, key_gain,
+    own, from_near, from_across,
+    query_out, key_out, value_out, query_gain_grad, key_gain_grad,
 ):
     rows = query.shape[0]
-    inner = inner_parts[0]
-    for index in range(1, len(inner_parts)):
-        inner = inner + inner_parts[index]
+    span = key.shape[0]
     scale = inverse_rms(totals[...])
-    shrink = scale * scale * scale * inner * (1.0 / D)
-
-    def one(start, out, raw, grad, gain):
+    query_scale, key_scale = scale[:, :rows], scale[:, rows:]
+    query_less = query_scale * query_scale * query_scale * inner[:, :rows] * (1.0 / D)
+    key_inner = (
+        inner_n[:, rows : rows + span]
+        + inner[:, rows + span : rows + 2 * span]
+        + inner_a[:, rows + 2 * span :]
+    )
+    key_less = key_scale * key_scale * key_inner * (1.0 / D)
+
+    for start in range(0, rows, BLOCK):
         here = slice(start, start + BLOCK)
-        wide, less = as_columns(scale[:, here]), as_columns(shrink[:, here])
-        first = start % rows
-        there = slice(first, first + BLOCK)
-        for lane in range(0, raw.shape[1], HS):
+        wide, less = as_columns(query_scale[:, here]), as_columns(query_less[:, here])
+        for lane in range(0, query.shape[1], HS):
             lanes = slice(lane, lane + HS)
-            out[there, lanes] = (
-                wide * (grad[there, lanes] * gain[:, lanes])
-                - raw[there, lanes].astype(jnp.float32) * less
+            query_out[here, lanes] = (
+                wide * (grad_query[here, lanes] * query_gain[:, lanes])
+                - query[here, lanes].astype(jnp.float32) * less
             ).astype(jnp.bfloat16)
-
-    for start in range(0, rows, BLOCK):
-        one(start, query_out, query, grad_query, query_gain)
-    one(rows, key_out, key, grad_key, key_gain)
+    for start in range(0, span, BLOCK):
+        here = slice(start, start + BLOCK)
+        wide, less = as_columns(key_scale[:, here]), as_columns(key_less[:, here])
+        for lane in range(0, key.shape[1], HS):
+            lanes = slice(lane, lane + HS)
+            grad_key, grad_value = (
+                own[lead, here, lanes]
+                + from_near[lead, here, lanes].astype(jnp.float32)
+                + from_across[lead, here, lanes].astype(jnp.float32)
+                for lead in (0, 1)
+            )
+            key_out[here, lanes] = (
+                wide * (grad_key * key_gain[:, lanes]) - key[here, lanes].astype(jnp.float32) * less
+            ).astype(jnp.bfloat16)
+            value_out[here, lanes] = grad_value.astype(jnp.bfloat16)
     query_gain_grad[...] = gains[0]
     key_gain_grad[...] = gains[1]
 
 
-def norms_backward(totals, inner_parts, gains, *rest):
-    query, key = rest[0], rest[3]
-    count = len(inner_parts)
-
-    def kernel(totals, *refs):
-        parts = [ref[...] for ref in refs[:count]]
-        norms_backward_kernel(totals, parts, *refs[count:])
-
+def norms_backward(*operands):
+    query, key = operands[5], operands[8]
     shape = jax.ShapeDtypeStruct
     width = query.shape[1]
     return pl.pallas_call(
-        kernel,
+        norms_backward_kernel,
         out_shape=[
             shape(query.shape, jnp.bfloat16),
+            shape(key.shape, jnp.bfloat16),
             shape(key.shape, jnp.bfloat16),
             shape((width,), jnp.float32),
             shape((width,), jnp.float32),
         ],
         compiler_params=pltpu.CompilerParams(vmem_limit_bytes=VMEM_BYTES),
         name="norms_backward",
-    )(totals, *inner_parts, gains, *rest)
+    )(*operands)
+
+
+def in_hbm(value):
+    return pltpu.with_memory_space_constraint(value, pltpu.HBM)
+
+
+def in_vmem(value):
+    return pltpu.with_memory_space_constraint(value, pltpu.VMEM)
 
 
 def swap_near(value):
@@ -325,17 +317,17 @@
     place = lax.axis_index(LINE)
     core = lax.axis_index("core")
     video_query, audio_key, audio_value, cotangent = (
-        pltpu.with_memory_space_constraint(argument, pltpu.HBM)
+        in_hbm(argument)
         for argument in (video_query, audio_key, audio_value, cotangent)
     )
     places = jnp.stack([place + 1 - 2 * core, place - 1 + 2 * core]).astype(jnp.int32)
+    totals = lax.psum(squares(video_query, audio_key), "tp")
+    held = norm_keys(totals, audio_key, audio_value, in_hbm(key_gain))
     query_gain = query_gain[None]
     key_gain = key_gain[None]
-    totals = lax.psum(squares(video_query, audio_key), "tp")
-    held = norm_keys(totals, audio_key, audio_value, key_gain)
-    halo_a = swap_across(held)
-    halo_n = swap_near(held)
-    (attended, grad_query, inner_query, gains, to_near, to_across, own) = attention(
+    halo_a = in_vmem(swap_across(held))
+    halo_n = in_vmem(swap_near(held))
+    attended, grad_query, inner, gains, to_near, to_across, own = attention(
         time_lists,
         places,
         totals,
@@ -347,30 +339,34 @@
         halo_n,
         halo_a,
     )
-    from_across = swap_across(to_across)
-    from_near = swap_near(to_near)
-    for axis in ("core", "x", "y"):
+    inner = lax.psum(inner, "tp")
+    inner, gains = lax.optimization_barrier((inner, gains))
+    inner_a = swap_across(inner)
+    inner_n = swap_near(inner)
+    gains = lax.psum(gains, "core")
+    inner_a, inner_n, gains, to_near, to_across = lax.optimization_barrier(
+        (inner_a, inner_n, gains, to_near, to_across)
+    )
+    from_across = in_vmem(swap_across(to_across))
+    from_near = in_vmem(swap_near(to_near))
+    for axis in ("x", "y", "far"):
         gains = lax.psum(gains, axis)
-    grad_key, audio_value_grad, inner = combine(
-        own, from_near, from_across, audio_key, key_gain, inner_query
-    )
-    inner, gains = lax.optimization_barrier((inner, gains))
-    size = lax.axis_size("tp")
-    inner_parts = [inner] + [
-        lax.ppermute(inner, "tp", [(i, (i + by) % size) for i in range(size)])
-        for by in range(1, size)
-    ]
-    gains = lax.psum(gains, "far")
-    video_query_grad, audio_key_grad, query_gain_grad, key_gain_grad = norms_backward(
-        totals,
-        inner_parts,
-        gains,
-        video_query,
-        grad_query,
-        query_gain,
-        audio_key,
-        grad_key,
-        key_gain,
+    video_query_grad, audio_key_grad, audio_value_grad, query_gain_grad, key_gain_grad = (
+        norms_backward(
+            totals,
+            inner,
+            inner_n,
+            inner_a,
+            gains,
+            video_query,
+            grad_query,
+            query_gain,
+            audio_key,
+            key_gain,
+            own,
+            from_near,
+            from_across,
+        )
     )
     return (
         attended,

time: 124 us -> 130 us (1.048)
  the two profiles are of different devices: /device:TPU:32 before, /device:TPU:2 now
where the time goes in v6:
time: 130 us
  blocking collectives  90.2 us (69%)
  Pallas kernels  15 us (12%)
  starting transfers between devices  13.7 us (11%)
  local copies, waits for them, and re-layouts  6.35 us (5%)
  waiting for transfers between devices  3.41 us (3%)
    psum x3, blocking collectives, on_device(): gains = lax.psum(gains, axis)  64.3 us
    psum x1, blocking collectives, on_device(): totals = lax.psum(squares(video_query, audio_key), 'tp')  13 us
    pallas_call x1, Pallas kernels, attention(): pl.pallas_call(attention_kernel, grid=(heads,), in_specs=[scalars] * 2 +...  9.55 us
    psum x1, blocking collectives, on_device(): inner = lax.psum(inner, 'tp')  8.51 us
    ppermute x3, starting transfers between devices, swap_near(): return lax.ppermute(value, 'core', [(0, 1), (1, 0)])  7.66 us
    unnamed x31, local copies, waits for them, and re-layouts  6.34 us
    ppermute x3, starting transfers between devices, swap_across(): return lax.ppermute(value, LINE, pairs)  6.06 us
    psum x1, blocking collectives, on_device(): gains = lax.psum(gains, 'core')  4.47 us
  transfers between devices with their start and end apart: 6, of which 1 were waited for; matrix products, arithmetic and copies ran while one was open for 0% of the time, Pallas kernels for 0%

profile of v6, /device:TPU:2, one launch (start us, length us, event | category | flops | bytes accessed | tf_op | source)
XLA Modules:
  0.0 129.6 jit_solution(16016050643799886870)
XLA Ops:
  0.6 0.0 copy-start.12
  0.6 0.0 copy-start.13
  0.7 0.0 copy-start.14
  0.7 1.5 %squares.1 = f32[1,768]{1,0:T(1,128)S(1)} custom-call(bf16[640,768]{1,0:T(8,128)(2,1)} %query.5, bf16[128,768]{1,0:T(8,128)(2,1)} %key.5), custom_call_target="tpu_custom_call" | custom-call | tf_op jit(solution)/shard_map/squares/pallas_call | solution.py:56
  2.2 13.0 %psum.42.totals = f32[1,768]{1,0:T(1,128)S(1)} all-reduce(f32[1,768]{1,0:T(1,128)S(1)} %squares.1), channel_id=1, replica_groups=mesh['y'=4,'far'=4,'x'=4,'core'=2,'tp'=4] {'tp'}, use_global_device_ids=true, to_apply=%region_0.0 | all-reduce | flops 768 | bytes 6144 | tf_op jit(solution)/shard_map/psum | solution.py:324
  15.2 1.2 norm_keys.1.held
  16.4 1.9 %collective-permute-start.1 = (bf16[2,128,768]{2,1,0:T(8,128)(2,1)S(1)}, bf16[2,128,768]{2,1,0:T(8,128)(2,1)S(1)}, u32[]{:S(2)}, u32[]{:S(2)}) collective-permute-start(bf16[2,128,768]{2,1,0:T(8,128)(2,1)S(1)} %norm_keys.1.held), channel_id=1, source_target_pairs={{4,8},{8,4},{12,16},{16,12},{20,24},{24,20},{28,32},{32,28},{36,40... | collective-permute-start | bytes 1179656 | tf_op jit(solution)/shard_map/ppermute | solution.py:313
  18.3 3.5 %collective-permute-start = (bf16[2,128,768]{2,1,0:T(8,128)(2,1)S(1)}, bf16[2,128,768]{2,1,0:T(8,128)(2,1)S(1)}, u32[]{:S(2)}, u32[]{:S(2)}) collective-permute-start(bf16[2,128,768]{2,1,0:T(8,128)(2,1)S(1)} %norm_keys.1.held), channel_id=1, source_target_pairs={{0,4},{4,0},{1,5},{5,1},{2,6},{6,2},{3,7},{7,3},{8,12},{12,8},{9,1... | collective-permute-start | bytes 1179656 | tf_op jit(solution)/shard_map/ppermute | solution.py:303
  21.8 0.0 copy-done.12
  21.8 0.0 copy-start
  21.9 0.0 copy-done.13
  21.9 0.0 copy-done.14
  21.9 0.0 copy-start.2
  21.9 0.1 copy.13.lists
  22.0 0.1 pad_add_fusion.places
  22.1 3.4 %collective-permute-done.1.halo_a = bf16[2,128,768]{2,1,0:T(8,128)(2,1)S(1)} collective-permute-done((bf16[2,128,768]{2,1,0:T(8,128)(2,1)S(1)}, bf16[2,128,768]{2,1,0:T(8,128)(2,1)S(1)}, u32[]{:S(2)}, u32[]{:S(2)}) %collective-permute-start.1) | collective-permute-done | bytes 393248 | tf_op jit(solution)/shard_map/ppermute | solution.py:313
  25.5 0.0 copy-start.8
  25.5 0.7 copy-done.8
  26.2 0.0 collective-permute-done.halo_n
  26.2 0.0 copy-start.10
  26.2 0.7 copy-done.10
  27.0 0.0 copy-start.9
  27.0 1.0 copy-done.9
  28.0 0.0 copy-start.11
  28.0 1.0 copy-done.11
  28.9 9.5 %attention.1 = (bf16[640,768]{1,0:T(8,128)(2,1)}, f32[640,768]{1,0:T(8,128)S(1)}, f32[1,1024]{1,0:T(1,128)}, f32[2,768]{1,0:T(2,128)}, bf16[2,128,768]{2,1,0:T(8...) custom-call(s32[5,4]{1,0:T(8,128)S(1)} %copy.13.lists, s32[2]{0:T(128)S(1)} %pad_add_fusion.places, ...), custom_call_target="tpu_custom_call" | custom-call | flops 2264924160 | bytes 4915200 | tf_op jit(solution)/shard_map/attention/pallas_call | solution.py:190
  38.5 0.0 copy-done
  38.5 0.0 copy-done.2
  38.5 8.5 %psum.43.inner = f32[1,1024]{1,0:T(1,128)S(1)} all-reduce(f32[1,1024]{1,0:T(1,128)} %get-tuple-element.26), channel_id=1, replica_groups=mesh['y'=4,'far'=4,'x'=4,'core'=2,'tp'=4] {'tp'}, use_global_device_ids=true, to_apply=%region_1.0 | all-reduce | flops 1024 | bytes 8192 | tf_op jit(solution)/shard_map/psum | solution.py:342
  47.0 1.9 %collective-permute-start.3 = (f32[1,1024]{1,0:T(1,128)S(1)}, f32[1,1024]{1,0:T(1,128)S(1)}, u32[]{:S(2)}, u32[]{:S(2)}) collective-permute-start(f32[1,1024]{1,0:T(1,128)S(1)} %psum.43.inner), channel_id=1, source_target_pairs={{0,4},{4,0},{1,5},{5,1},{2,6},{6,2},{3,7},{7,3},{8,12},{12,8},{9,1... | collective-permute-start | bytes 12296 | tf_op jit(solution)/shard_map/ppermute | solution.py:303
  48.9 1.9 %collective-permute-start.2 = (f32[1,1024]{1,0:T(1,128)S(1)}, f32[1,1024]{1,0:T(1,128)S(1)}, u32[]{:S(2)}, u32[]{:S(2)}) collective-permute-start(f32[1,1024]{1,0:T(1,128)S(1)} %psum.43.inner), channel_id=1, source_target_pairs={{4,8},{8,4},{12,16},{16,12},{20,24},{24,20},{28,32},{32,28},{36,40... | collective-permute-start | bytes 12296 | tf_op jit(solution)/shard_map/ppermute | solution.py:313
  50.9 4.5 %psum.44 = f32[2,768]{1,0:T(2,128)} all-reduce(f32[2,768]{1,0:T(2,128)} %get-tuple-element.29), channel_id=1, replica_groups=mesh['y'=4,'far'=4,'x'=4,'core'=2,'tp'=4] {'core'}, use_global_device_ids=true, to_apply=%region_2.0 | all-reduce | flops 1536 | bytes 12288 | tf_op jit(solution)/shard_map/psum | solution.py:346
  55.3 0.0 collective-permute-done.3.inner_n
  55.3 0.0 copy-start.4
  55.3 0.0 collective-permute-done.2.inner_a
  55.3 0.0 copy-start.6
  55.4 2.3 %collective-permute-start.4 = (bf16[2,128,768]{2,1,0:T(8,128)(2,1)}, bf16[2,128,768]{2,1,0:T(8,128)(2,1)S(1)}, u32[]{:S(2)}, u32[]{:S(2)}) collective-permute-start(bf16[2,128,768]{2,1,0:T(8,128)(2,1)} %get-tuple-element.37), channel_id=1, source_target_pairs={{0,4},{4,0},{1,5},{5,1},{2,6},{6,2},{3,7},{7,3},{8,12},{12,8},{9,1... | collective-permute-start | bytes 1179656 | tf_op jit(solution)/shard_map/ppermute | solution.py:303
  57.6 2.2 %collective-permute-start.5 = (bf16[2,128,768]{2,1,0:T(8,128)(2,1)}, bf16[2,128,768]{2,1,0:T(8,128)(2,1)S(1)}, u32[]{:S(2)}, u32[]{:S(2)}) collective-permute-start(bf16[2,128,768]{2,1,0:T(8,128)(2,1)} %get-tuple-element.38), channel_id=1, source_target_pairs={{4,8},{8,4},{12,16},{16,12},{20,24},{24,20},{28,32},{32,28},{36,40... | collective-permute-start | bytes 1179656 | tf_op jit(solution)/shard_map/ppermute | solution.py:313
  59.8 32.5 %psum.45 = f32[2,768]{1,0:T(2,128)} all-reduce(f32[2,768]{1,0:T(2,128)} %psum.44), channel_id=1, replica_groups=mesh['y'=4,'far'=4,'x'=4,'core'=2,'tp'=4] {'x'}, use_global_device_ids=true, to_apply=%region_3.0 | all-reduce | flops 1536 | bytes 12288 | tf_op jit(solution)/shard_map/psum | solution.py:353
  92.3 0.0 copy-done.4
  92.3 0.0 copy-done.6
  92.3 18.1 %psum.46 = f32[2,768]{1,0:T(2,128)} all-reduce(f32[2,768]{1,0:T(2,128)} %psum.45), channel_id=1, replica_groups=mesh['y'=4,'far'=4,'x'=4,'core'=2,'tp'=4] {'y'}, use_global_device_ids=true, to_apply=%region_4.0 | all-reduce | flops 1536 | bytes 12288 | tf_op jit(solution)/shard_map/psum | solution.py:353
  110.4 13.7 %psum.47.gains = f32[2,768]{1,0:T(2,128)S(1)} all-reduce(f32[2,768]{1,0:T(2,128)} %psum.46), channel_id=1, replica_groups=mesh['y'=4,'far'=4,'x'=4,'core'=2,'tp'=4] {'far'}, use_global_device_ids=true, to_apply=%region_5.0 | all-reduce | flops 1536 | bytes 12288 | tf_op jit(solution)/shard_map/psum | solution.py:353
  124.1 0.0 collective-permute-done.4.from_near
  124.1 0.0 collective-permute-done.5.from_across
  124.1 0.0 copy-start.1
  124.2 0.7 copy-done.1
  124.8 0.0 copy-start.3
  124.8 0.7 copy-done.3
  125.5 0.0 copy-start.5
  125.5 0.7 copy-done.5
  126.2 0.0 copy-start.7
  126.2 0.7 copy-done.7
  126.9 2.8 %norms_backward.1 = (bf16[640,768]{1,0:T(8,128)(2,1)}, bf16[128,768]{1,0:T(8,128)(2,1)}, bf16[128,768]{1,0:T(8,128)(2,1)}, f32[768]{0:T(1024)}, f32[768]{0:T(1024)}) custom-call(f32[1,768]{1,0:T(1,128)S(1)} %psum.42.totals, f32[1,1024]{1,0:T(1,128)S(1)} %psum.43.inner, f32[1,1024]{1,0:T(1,128)S(1)} %copy-done.5, f32[1,1024]{1,0:T(1,128)S(1)} %copy-done.7, ...), custom_call_target="tpu_custom_call" | custom-call | tf_op jit(solution)/shard_map/norms_backward/pallas_call | solution.py:280
  (2 shorter events, 0.0 us)
Async XLA Ops:
  0.6 21.2 %copy-start.12 = (f32[768]{0:T(1024)S(1)}, f32[768]{0:T(1024)}, u32[]{:S(2)}) copy-start(f32[768]{0:T(1024)} %gain.1) | copy-start | bytes 9220
  0.6 21.2 %copy-start.13 = (f32[768]{0:T(1024)S(1)}, f32[768]{0:T(1024)}, u32[]{:S(2)}) copy-start(f32[768]{0:T(1024)} %param.11) | copy-start | bytes 9220
  0.7 21.2 %copy-start.14 = (s32[5,4]{0,1:T(4,128)S(1)}, s32[5,4]{0,1:T(4,128)}, u32[]{:S(2)}) copy-start(s32[5,4]{0,1:T(4,128)} %param.13) | copy-start | bytes 244
  16.4 9.1 %collective-permute-start.1 = (bf16[2,128,768]{2,1,0:T(8,128)(2,1)S(1)}, bf16[2,128,768]{2,1,0:T(8,128)(2,1)S(1)}, u32[]{:S(2)}, u32[]{:S(2)}) collective-permute-start(bf16[2,128,768]{2,1,0:T(8,128)(2,1)S(1)} %norm_keys.1.held), channel_id=1, source_target_pairs={{4,8},{8,4},{12,16},{16,12},{20,24},{24,20},{28,32},{32,28},{36,40... | collective-permute-start | bytes 1179656 | tf_op jit(solution)/shard_map/ppermute | solution.py:313
  18.3 7.9 %collective-permute-start = (bf16[2,128,768]{2,1,0:T(8,128)(2,1)S(1)}, bf16[2,128,768]{2,1,0:T(8,128)(2,1)S(1)}, u32[]{:S(2)}, u32[]{:S(2)}) collective-permute-start(bf16[2,128,768]{2,1,0:T(8,128)(2,1)S(1)} %norm_keys.1.held), channel_id=1, source_target_pairs={{0,4},{4,0},{1,5},{5,1},{2,6},{6,2},{3,7},{7,3},{8,12},{12,8},{9,1... | collective-permute-start | bytes 1179656 | tf_op jit(solution)/shard_map/ppermute | solution.py:303
  21.8 16.7 %copy-start = (f32[1,768]{1,0:T(1,128)}, f32[1,768]{1,0:T(1,128)S(1)}, u32[]{:S(2)}) copy-start(f32[1,768]{1,0:T(1,128)S(1)} %broadcast_in_dim.7.key_gain) | copy-start | bytes 9220
  21.9 16.6 %copy-start.2 = (f32[1,768]{1,0:T(1,128)}, f32[1,768]{1,0:T(1,128)S(1)}, u32[]{:S(2)}) copy-start(f32[1,768]{1,0:T(1,128)S(1)} %broadcast_in_dim.6.gain.query_gain) | copy-start | bytes 9220
  25.5 0.7 copy-start.8
  26.2 0.7 copy-start.10
  27.0 1.0 copy-start.9
  28.0 1.0 copy-start.11
  47.0 8.3 %collective-permute-start.3 = (f32[1,1024]{1,0:T(1,128)S(1)}, f32[1,1024]{1,0:T(1,128)S(1)}, u32[]{:S(2)}, u32[]{:S(2)}) collective-permute-start(f32[1,1024]{1,0:T(1,128)S(1)} %psum.43.inner), channel_id=1, source_target_pairs={{0,4},{4,0},{1,5},{5,1},{2,6},{6,2},{3,7},{7,3},{8,12},{12,8},{9,1... | collective-permute-start | bytes 12296 | tf_op jit(solution)/shard_map/ppermute | solution.py:303
  48.9 6.4 %collective-permute-start.2 = (f32[1,1024]{1,0:T(1,128)S(1)}, f32[1,1024]{1,0:T(1,128)S(1)}, u32[]{:S(2)}, u32[]{:S(2)}) collective-permute-start(f32[1,1024]{1,0:T(1,128)S(1)} %psum.43.inner), channel_id=1, source_target_pairs={{4,8},{8,4},{12,16},{16,12},{20,24},{24,20},{28,32},{32,28},{36,40... | collective-permute-start | bytes 12296 | tf_op jit(solution)/shard_map/ppermute | solution.py:313
  55.3 37.0 %copy-start.4 = (f32[1,1024]{1,0:T(1,128)}, f32[1,1024]{1,0:T(1,128)S(1)}, u32[]{:S(2)}) copy-start(f32[1,1024]{1,0:T(1,128)S(1)} %collective-permute-done.3.inner_n) | copy-start | bytes 12292
  55.3 37.0 %copy-start.6 = (f32[1,1024]{1,0:T(1,128)}, f32[1,1024]{1,0:T(1,128)S(1)}, u32[]{:S(2)}) copy-start(f32[1,1024]{1,0:T(1,128)S(1)} %collective-permute-done.2.inner_a) | copy-start | bytes 12292
  55.4 68.8 %collective-permute-start.4 = (bf16[2,128,768]{2,1,0:T(8,128)(2,1)}, bf16[2,128,768]{2,1,0:T(8,128)(2,1)S(1)}, u32[]{:S(2)}, u32[]{:S(2)}) collective-permute-start(bf16[2,128,768]{2,1,0:T(8,128)(2,1)} %get-tuple-element.37), channel_id=1, source_target_pairs={{0,4},{4,0},{1,5},{5,1},{2,6},{6,2},{3,7},{7,3},{8,12},{12,8},{9,1... | collective-permute-start | bytes 1179656 | tf_op jit(solution)/shard_map/ppermute | solution.py:303
  57.6 66.5 %collective-permute-start.5 = (bf16[2,128,768]{2,1,0:T(8,128)(2,1)}, bf16[2,128,768]{2,1,0:T(8,128)(2,1)S(1)}, u32[]{:S(2)}, u32[]{:S(2)}) collective-permute-start(bf16[2,128,768]{2,1,0:T(8,128)(2,1)} %get-tuple-element.38), channel_id=1, source_target_pairs={{4,8},{8,4},{12,16},{16,12},{20,24},{24,20},{28,32},{32,28},{36,40... | collective-permute-start | bytes 1179656 | tf_op jit(solution)/shard_map/ppermute | solution.py:313
  124.1 0.7 copy-start.1
  124.8 0.7 copy-start.3
  125.5 0.7 copy-start.5
  126.2 0.7 copy-start.7

commit v7 on v5

--- a/solution.py
+++ b/solution.py
@@ -66,7 +66,7 @@
     scale = as_columns(inverse_rms(totals[:, first:]))
     for start in range(0, key.shape[1], HS):
         lanes = slice(start, start + HS)
-        held[0, :, lanes] = (key[:, lanes].astype(jnp.float32) * scale * gain[:, lanes]).astype(
+        held[0, :, lanes] = (key[:, lanes].astype(jnp.float32) * scale * gain[lanes][None]).astype(
             jnp.bfloat16
         )
     held[1] = value[...]
@@ -83,7 +83,7 @@
 
 def attention_kernel(
     lists, places, totals, query, cot, gain, key_gain, held, halo_n, halo_a,
-    attended, grad_query, inner, gains, near, across, own,
+    attended, grad_query, inner, gains, near, across_k, across_v, own_k, own_v,
     scale_cols, inner_sum, probs_low, grad_low,
 ):
     head = pl.program_id(0)
@@ -148,10 +148,10 @@
         )
         near[0, :, lanes] = grad_keys[:span].astype(jnp.bfloat16)
         near[1, :, lanes] = grad_values[:span].astype(jnp.bfloat16)
-        own[0, :, lanes] = grad_keys[span : 2 * span]
-        own[1, :, lanes] = grad_values[span : 2 * span]
-        across[0, :, lanes] = grad_keys[2 * span :].astype(jnp.bfloat16)
-        across[1, :, lanes] = grad_values[2 * span :].astype(jnp.bfloat16)
+        own_k[:, lanes] = grad_keys[span : 2 * span]
+        own_v[:, lanes] = grad_values[span : 2 * span]
+        across_k[:, lanes] = grad_keys[2 * span :].astype(jnp.bfloat16)
+        across_v[:, lanes] = grad_values[2 * span :].astype(jnp.bfloat16)
 
     total = rows // BLOCK
     groups = [list(range(i, min(i + 2, total))) for i in range(0, total, 2)]
@@ -200,17 +200,21 @@
             whole((1, rows)),
             of_head(2),
             of_head(2, span),
-            of_head(2, span),
-            of_head(2, span),
+            of_head(span),
+            of_head(span),
+            of_head(span),
+            of_head(span),
         ],
         out_shape=[
             shape((rows, width), bf16),
             shape((rows, width), f32),
-            shape((1, rows), f32),
-            shape((2, width), f32),
-            shape((2, span, width), bf16),
-            shape((2, span, width), bf16),
-            shape((2, span, width), f32),
+            pltpu.HBM((1, rows), f32),
+            pltpu.HBM((2, width), f32),
+            pltpu.HBM((2, span, width), bf16),
+            pltpu.HBM((span, width), bf16),
+            pltpu.HBM((span, width), bf16),
+            shape((span, width), f32),
+            shape((span, width), f32),
         ],
         scratch_shapes=[
             pltpu.VMEM((rows, HS), f32),
@@ -226,27 +230,26 @@
     )(lists, places, totals, query, cot, gain, key_gain, held, halo_n, halo_a)
 
 
-def combine_kernel(
-    own, from_near, from_across, key, key_gain, inner_query, grad_key, value_grad, inner
-):
-    total = own[0] + from_near[0].astype(jnp.float32) + from_across[0].astype(jnp.float32)
+def combine_kernel(own, from_near, from_across, key, key_gain, inner_query, grad_key, inner):
+    total = own[...] + from_near[0].astype(jnp.float32) + from_across[...].astype(jnp.float32)
     grad_key[...] = total
-    value_grad[...] = (
-        own[1] + from_near[1].astype(jnp.float32) + from_across[1].astype(jnp.float32)
-    ).astype(jnp.bfloat16)
     rows = inner_query.shape[1]
     inner[:, :rows] = inner_query[...]
     inner[:, rows:] = across_rows(key[...].astype(jnp.float32) * (total * key_gain[...]))
 
 
 def combine(own, from_near, from_across, key, key_gain, inner_query):
-    _, rows, width = own.shape
     shape = jax.ShapeDtypeStruct
+    rows, width = own.shape
+    whole = pl.BlockSpec(memory_space=pltpu.VMEM)
+    first = pl.BlockSpec((1, rows, width), lambda i: (0, 0, 0))
     return pl.pallas_call(
         combine_kernel,
+        grid=(1,),
+        in_specs=[whole, first] + [whole] * 4,
+        out_specs=[whole, whole],
         out_shape=[
             shape((rows, width), jnp.float32),
-            shape((rows, width), jnp.bfloat16),
             shape((1, inner_query.shape[1] + rows), jnp.float32),
         ],
         compiler_params=pltpu.CompilerParams(vmem_limit_bytes=VMEM_BYTES),
@@ -256,7 +259,8 @@
 
 def norms_backward_kernel(
     totals, inner_parts, gains, query, grad_query, query_gain, key, grad_key, key_gain,
-    query_out, key_out, query_gain_grad, key_gain_grad,
+    own, from_near, from_across,
+    query_out, key_out, value_out, query_gain_grad, key_gain_grad,
 ):
     rows = query.shape[0]
     inner = inner_parts[0]
@@ -280,6 +284,9 @@
     for start in range(0, rows, BLOCK):
         one(start, query_out, query, grad_query, query_gain)
     one(rows, key_out, key, grad_key, key_gain)
+    value_out[...] = (
+        own[...] + from_near[0].astype(jnp.float32) + from_across[...].astype(jnp.float32)
+    ).astype(jnp.bfloat16)
     query_gain_grad[...] = gains[0]
     key_gain_grad[...] = gains[1]
 
@@ -294,10 +301,16 @@
 
     shape = jax.ShapeDtypeStruct
     width = query.shape[1]
+    whole = pl.BlockSpec(memory_space=pltpu.VMEM)
+    second = pl.BlockSpec((1, *key.shape), lambda i: (1, 0, 0))
     return pl.pallas_call(
         kernel,
+        grid=(1,),
+        in_specs=[whole] * (count + 9) + [second, whole],
+        out_specs=[whole] * 5,
         out_shape=[
             shape(query.shape, jnp.bfloat16),
+            shape(key.shape, jnp.bfloat16),
             shape(key.shape, jnp.bfloat16),
             shape((width,), jnp.float32),
             shape((width,), jnp.float32),
@@ -305,6 +318,10 @@
         compiler_params=pltpu.CompilerParams(vmem_limit_bytes=VMEM_BYTES),
         name="norms_backward",
     )(totals, *inner_parts, gains, *rest)
+
+
+def in_hbm(value):
+    return pltpu.with_memory_space_constraint(value, pltpu.HBM)
 
 
 def swap_near(value):
@@ -325,17 +342,19 @@
     place = lax.axis_index(LINE)
     core = lax.axis_index("core")
     video_query, audio_key, audio_value, cotangent = (
-        pltpu.with_memory_space_constraint(argument, pltpu.HBM)
+        in_hbm(argument)
         for argument in (video_query, audio_key, audio_value, cotangent)
     )
     places = jnp.stack([place + 1 - 2 * core, place - 1 + 2 * core]).astype(jnp.int32)
+    totals = lax.psum(squares(video_query, audio_key), "tp")
+    held = norm_keys(totals, audio_key, audio_value, in_hbm(key_gain))
     query_gain = query_gain[None]
     key_gain = key_gain[None]
-    totals = lax.psum(squares(video_query, audio_key), "tp")
-    held = norm_keys(totals, audio_key, audio_value, key_gain)
-    halo_a = swap_across(held)
-    halo_n = swap_near(held)
-    (attended, grad_query, inner_query, gains, to_near, to_across, own) = attention(
+    halo_a = in_hbm(swap_across(held))
+    halo_n = in_hbm(swap_near(held))
+    (
+        attended, grad_query, inner_query, gains, to_near, to_across_k, to_across_v, own_k, own_v
+    ) = attention(
         time_lists,
         places,
         totals,
@@ -347,12 +366,15 @@
         halo_n,
         halo_a,
     )
-    from_across = swap_across(to_across)
+    from_across_k = swap_across(to_across_k)
     from_near = swap_near(to_near)
-    for axis in ("core", "x", "y"):
+    for axis in ("core", "x"):
         gains = lax.psum(gains, axis)
-    grad_key, audio_value_grad, inner = combine(
-        own, from_near, from_across, audio_key, key_gain, inner_query
+    gains, to_across_v = lax.optimization_barrier((gains, to_across_v))
+    from_across_v = swap_across(to_across_v)
+    gains = lax.psum(gains, "y")
+    grad_key, inner = combine(
+        own_k, from_near, in_hbm(from_across_k), audio_key, key_gain, in_hbm(inner_query)
     )
     inner, gains = lax.optimization_barrier((inner, gains))
     size = lax.axis_size("tp")
@@ -361,16 +383,21 @@
         for by in range(1, size)
     ]
     gains = lax.psum(gains, "far")
-    video_query_grad, audio_key_grad, query_gain_grad, key_gain_grad = norms_backward(
-        totals,
-        inner_parts,
-        gains,
-        video_query,
-        grad_query,
-        query_gain,
-        audio_key,
-        grad_key,
-        key_gain,
+    video_query_grad, audio_key_grad, audio_value_grad, query_gain_grad, key_gain_grad = (
+        norms_backward(
+            totals,
+            inner_parts,
+            gains,
+            video_query,
+            grad_query,
+            query_gain,
+            audio_key,
+            grad_key,
+            key_gain,
+            own_v,
+            from_near,
+            from_across_v,
+        )
     )
     return (
         attended,

time: 124 us -> 120 us (0.968)
  local copies, waits for them, and re-layouts: 6.14 us -> 0.79 us
  starting transfers between devices: 15.6 us -> 18.3 us
  blocking collectives: 82.9 us -> 81.3 us
    psum x3 -> x2, blocking collectives: 53.6 us -> 34.3 us  [on_device(): gains = lax.psum(gains, axis)]
    psum x0 -> x1, blocking collectives: none -> 18.5 us  [on_device(): gains = lax.psum(gains, 'y')]
    unnamed x19 -> x11, local copies, waits for them, and re-layouts: 5.44 us -> 0.79 us
    ppermute x2 -> x3, starting transfers between devices: 1.37 us -> 2.7 us  [swap_across(): return lax.ppermute(value, LINE, pairs)]
  transfers between devices with their start and end apart: 7 -> 8, of which waited for: 1 -> 1; matrix products, arithmetic and copies ran while one was open for 0% -> 0% of each run, Pallas kernels for 0% -> 1%
where the time goes in v7:
time: 120 us; the launch traced here: 119 us
  blocking collectives  81.3 us (68%)
  starting transfers between devices  18.3 us (15%)
  Pallas kernels  16.4 us (14%)
  waiting for transfers between devices  1.59 us (1%)
    psum x2, blocking collectives, on_device(): gains = lax.psum(gains, axis)  34.3 us
    psum x1, blocking collectives, on_device(): gains = lax.psum(gains, 'y')  18.5 us
    psum x1, blocking collectives, on_device(): gains = lax.psum(gains, 'far')  14.7 us
    psum x1, blocking collectives, on_device(): totals = lax.psum(squares(video_query, audio_key), 'tp')  13.8 us
    ppermute x3, starting transfers between devices, on_device(): lax.ppermute(inner, 'tp', [(i, (i + by) % size) for i in range(size)])  11 us
    pallas_call x1, Pallas kernels, attention(): pl.pallas_call(attention_kernel, grid=(heads,), in_specs=[scalars] * 2 +...  9.62 us
    ppermute x2, starting transfers between devices, swap_near(): return lax.ppermute(value, 'core', [(0, 1), (1, 0)])  4.64 us
    pallas_call x1, Pallas kernels, norms_backward(): pl.pallas_call(kernel, grid=(1,), in_specs=[whole] * (count + 9) + [secon...  2.88 us
  transfers between devices with their start and end apart: 8, of which 1 were waited for; matrix products, arithmetic and copies ran while one was open for 0% of the time, Pallas kernels for 1%

profile of v7, /device:TPU:32, one launch (start us, length us, event | category | flops | bytes accessed | tf_op | source)
XLA Modules:
  0.0 119.3 jit_solution(16453632177212528913)
XLA Ops:
  0.6 0.0 copy-start.1
  0.6 0.0 copy-start.2
  0.7 0.0 copy-start.3
  0.7 1.5 %squares.1 = f32[1,768]{1,0:T(1,128)S(1)} custom-call(bf16[640,768]{1,0:T(8,128)(2,1)} %refs_5_.1, bf16[128,768]{1,0:T(8,128)(2,1)} %refs_8_.1), custom_call_target="tpu_custom_call" | custom-call | tf_op jit(solution)/shard_map/squares/pallas_call | solution.py:56
  2.2 13.8 %psum.35.totals = f32[1,768]{1,0:T(1,128)S(1)} all-reduce(f32[1,768]{1,0:T(1,128)S(1)} %squares.1), channel_id=1, replica_groups=mesh['y'=4,'far'=4,'x'=4,'core'=2,'tp'=4] {'tp'}, use_global_device_ids=true, to_apply=%region_0.0 | all-reduce | flops 768 | bytes 6144 | tf_op jit(solution)/shard_map/psum | solution.py:349
  16.0 1.2 norm_keys.1.held
  17.2 0.7 collective-permute-start.1
  17.9 1.9 %collective-permute-start = (bf16[2,128,768]{2,1,0:T(8,128)(2,1)S(1)}, bf16[2,128,768]{2,1,0:T(8,128)(2,1)}, u32[]{:S(2)}, u32[]{:S(2)}) collective-permute-start(bf16[2,128,768]{2,1,0:T(8,128)(2,1)S(1)} %norm_keys.1.held), channel_id=1, source_target_pairs={{0,4},{4,0},{1,5},{5,1},{2,6},{6,2},{3,7},{7,3},{8,12},{12,8},{9,1... | collective-permute-start | bytes 1179656 | tf_op jit(solution)/shard_map/ppermute | solution.py:328
  19.8 0.0 copy-done.1
  19.8 0.0 copy-done.2
  19.9 0.0 copy-done.3
  19.9 0.1 copy.13.lists
  20.0 0.1 pad_add_fusion.places
  20.0 0.0 collective-permute-done.1.halo_a
  20.0 0.0 copy-start.4
  20.0 1.6 %collective-permute-done.halo_n = bf16[2,128,768]{2,1,0:T(8,128)(2,1)} collective-permute-done((bf16[2,128,768]{2,1,0:T(8,128)(2,1)S(1)}, bf16[2,128,768]{2,1,0:T(8,128)(2,1)}, u32[]{:S(2)}, u32[]{:S(2)}) %collective-permute-start) | collective-permute-done | bytes 393248 | tf_op jit(solution)/shard_map/ppermute | solution.py:328
  21.6 0.0 copy-done.4
  21.6 9.6 %attention.1 = (bf16[640,768]{1,0:T(8,128)(2,1)}, f32[640,768]{1,0:T(8,128)S(1)}, f32[1,640]{1,0:T(1,128)}, f32[2,768]{1,0:T(2,128)}, bf16[2,128,768]{2,1,0:T(8,...) custom-call(s32[5,4]{1,0:T(8,128)S(1)} %copy.13.lists, ...), custom_call_target="tpu_custom_call" | custom-call | flops 2264924160 | bytes 4915200 | tf_op jit(solution)/shard_map/attention/pallas_call | solution.py:189
  31.2 2.7 %collective-permute-start.2 = (bf16[2,128,768]{2,1,0:T(8,128)(2,1)}, bf16[2,128,768]{2,1,0:T(8,128)(2,1)S(1)}, u32[]{:S(2)}, u32[]{:S(2)}) collective-permute-start(bf16[2,128,768]{2,1,0:T(8,128)(2,1)} %get-tuple-element.28), channel_id=1, source_target_pairs={{0,4},{4,0},{1,5},{5,1},{2,6},{6,2},{3,7},{7,3},{8,12},{12,8},{9,1... | collective-permute-start | bytes 1179656 | tf_op jit(solution)/shard_map/ppermute | solution.py:328
  34.0 0.7 collective-permute-start.3
  34.6 5.4 %psum.36 = f32[2,768]{1,0:T(2,128)S(1)} all-reduce(f32[2,768]{1,0:T(2,128)} %get-tuple-element.32), channel_id=1, replica_groups=mesh['y'=4,'far'=4,'x'=4,'core'=2,'tp'=4] {'core'}, use_global_device_ids=true, to_apply=%region_1.0 | all-reduce | flops 1536 | bytes 12288 | tf_op jit(solution)/shard_map/psum | solution.py:372
  40.0 28.9 %psum.37 = f32[2,768]{1,0:T(2,128)S(1)} all-reduce(f32[2,768]{1,0:T(2,128)S(1)} %psum.36), channel_id=1, replica_groups=mesh['y'=4,'far'=4,'x'=4,'core'=2,'tp'=4] {'x'}, use_global_device_ids=true, to_apply=%region_2.0 | all-reduce | flops 1536 | bytes 12288 | tf_op jit(solution)/shard_map/psum | solution.py:372
  69.0 1.3 %collective-permute-start.7 = (bf16[128,768]{1,0:T(8,128)(2,1)}, bf16[128,768]{1,0:T(8,128)(2,1)}, u32[]{:S(2)}, u32[]{:S(2)}) collective-permute-start(bf16[128,768]{1,0:T(8,128)(2,1)} %get-tuple-element.40), channel_id=1, source_target_pairs={{4,8},{8,4},{12,16},{16,12},{20,24},{24,20},{28,32},{32,28},{36,40... | collective-permute-start | bytes 589832 | tf_op jit(solution)/shard_map/ppermute | solution.py:338
  70.3 18.5 %psum.38 = f32[2,768]{1,0:T(2,128)} all-reduce(f32[2,768]{1,0:T(2,128)S(1)} %psum.37), channel_id=1, replica_groups=mesh['y'=4,'far'=4,'x'=4,'core'=2,'tp'=4] {'y'}, use_global_device_ids=true, to_apply=%region_3.0 | all-reduce | flops 1536 | bytes 12288 | tf_op jit(solution)/shard_map/psum | solution.py:375
  88.8 0.0 collective-permute-done.3.from_across
  88.8 0.0 copy-start
  88.8 0.0 collective-permute-done.2.from_near.refs_12_
  88.8 0.7 copy-done
  89.5 1.2 %combine.1 = (f32[128,768]{1,0:T(8,128)S(1)}, f32[1,768]{1,0:T(1,128)S(1)}) custom-call(f32[128,768]{1,0:T(8,128)S(1)} %get-tuple-element.27.own, bf16[2,128,768]{2,1,0:T(8,128)(2,1)S(1)} %collective-permute-done.2.from_near.refs_12_, bf16[128,768]{1,0:T(8,128)(2,1)} %copy-done, bf16[128,768]{1,0:T(8,128)(2,1)} %refs_8_.1, ...), custom_call_target="tpu_custom_call" | custom-call | tf_op jit(solution)/shard_map/combine/pallas_call | solution.py:246
  90.7 4.9 %collective-permute-start.6 = (f32[1,768]{1,0:T(1,128)S(1)}, f32[1,768]{1,0:T(1,128)S(1)}, u32[]{:S(2)}, u32[]{:S(2)}) collective-permute-start(f32[1,768]{1,0:T(1,128)S(1)} %get-tuple-element.35.refs_0_), channel_id=1, source_target_pairs={{0,3},{1,0},{2,1},{3,2},{4,7},{5,4},{6,5},{7,6},{8,11},{9,8},{10,9... | collective-permute-start | bytes 9224 | tf_op jit(solution)/shard_map/ppermute | solution.py:382
  95.5 1.9 %collective-permute-start.5 = (f32[1,768]{1,0:T(1,128)S(1)}, f32[1,768]{1,0:T(1,128)S(1)}, u32[]{:S(2)}, u32[]{:S(2)}) collective-permute-start(f32[1,768]{1,0:T(1,128)S(1)} %get-tuple-element.35.refs_0_), channel_id=1, source_target_pairs={{0,2},{1,3},{2,0},{3,1},{4,6},{5,7},{6,4},{7,5},{8,10},{9,11},{10,... | collective-permute-start | bytes 9224 | tf_op jit(solution)/shard_map/ppermute | solution.py:382
  97.5 4.2 %collective-permute-start.4 = (f32[1,768]{1,0:T(1,128)S(1)}, f32[1,768]{1,0:T(1,128)S(1)}, u32[]{:S(2)}, u32[]{:S(2)}) collective-permute-start(f32[1,768]{1,0:T(1,128)S(1)} %get-tuple-element.35.refs_0_), channel_id=1, source_target_pairs={{0,1},{1,2},{2,3},{3,0},{4,5},{5,6},{6,7},{7,4},{8,9},{9,10},{10,1... | collective-permute-start | bytes 9224 | tf_op jit(solution)/shard_map/ppermute | solution.py:382
  101.7 14.7 %psum.39.refs_4_ = f32[2,768]{1,0:T(2,128)S(1)} all-reduce(f32[2,768]{1,0:T(2,128)} %psum.38), channel_id=1, replica_groups=mesh['y'=4,'far'=4,'x'=4,'core'=2,'tp'=4] {'far'}, use_global_device_ids=true, to_apply=%region_4.0 | all-reduce | flops 1536 | bytes 12288 | tf_op jit(solution)/shard_map/psum | solution.py:385
  116.4 0.0 collective-permute-done.7.refs_13_
  116.4 0.0 collective-permute-done.6.refs_3_
  116.4 0.0 collective-permute-done.5.refs_2_
  116.5 0.0 collective-permute-done.4.refs_1_
  116.5 2.9 %norms_backward.1 = (bf16[640,768]{1,0:T(8,128)(2,1)}, bf16[128,768]{1,0:T(8,128)(2,1)}, bf16[128,768]{1,0:T(8,128)(2,1)}, f32[768]{0:T(1024)}, f32[768]{0:T(1024)}) custom-call(f32[1,768]{1,0:T(1,128)S(1)} %psum.35.totals, f32[1,768]{1,0:T(1,128)S(1)} %get-tuple-element.35.refs_0_, f32[1,768]{1,0:T(1,128)S(1)} %collective-permute-done.4.refs_1_, ...), custom_call_target="tpu_custom_call" | custom-call | tf_op jit(solution)/shard_map/norms_backward/pallas_call | solution.py:306
  (2 shorter events, 0.0 us)
Async XLA Ops:
  0.6 19.2 %copy-start.1 = (f32[768]{0:T(1024)S(1)}, f32[768]{0:T(1024)}, u32[]{:S(2)}) copy-start(f32[768]{0:T(1024)} %gain.1) | copy-start | bytes 9220
  0.6 19.2 %copy-start.2 = (f32[768]{0:T(1024)S(1)}, f32[768]{0:T(1024)}, u32[]{:S(2)}) copy-start(f32[768]{0:T(1024)} %param.11) | copy-start | bytes 9220
  0.7 19.2 %copy-start.3 = (s32[5,4]{0,1:T(4,128)S(1)}, s32[5,4]{0,1:T(4,128)}, u32[]{:S(2)}) copy-start(s32[5,4]{0,1:T(4,128)} %param.13) | copy-start | bytes 244
  17.2 2.9 %collective-permute-start.1 = (bf16[2,128,768]{2,1,0:T(8,128)(2,1)S(1)}, bf16[2,128,768]{2,1,0:T(8,128)(2,1)S(1)}, u32[]{:S(2)}, u32[]{:S(2)}) collective-permute-start(bf16[2,128,768]{2,1,0:T(8,128)(2,1)S(1)} %norm_keys.1.held), channel_id=1, source_target_pairs={{4,8},{8,4},{12,16},{16,12},{20,24},{24,20},{28,32},{32,28},{36,40... | collective-permute-start | bytes 1179656 | tf_op jit(solution)/shard_map/ppermute | solution.py:338
  17.9 3.7 %collective-permute-start = (bf16[2,128,768]{2,1,0:T(8,128)(2,1)S(1)}, bf16[2,128,768]{2,1,0:T(8,128)(2,1)}, u32[]{:S(2)}, u32[]{:S(2)}) collective-permute-start(bf16[2,128,768]{2,1,0:T(8,128)(2,1)S(1)} %norm_keys.1.held), channel_id=1, source_target_pairs={{0,4},{4,0},{1,5},{5,1},{2,6},{6,2},{3,7},{7,3},{8,12},{12,8},{9,1... | collective-permute-start | bytes 1179656 | tf_op jit(solution)/shard_map/ppermute | solution.py:328
  20.0 1.6 %copy-start.4 = (bf16[2,128,768]{2,1,0:T(8,128)(2,1)}, bf16[2,128,768]{2,1,0:T(8,128)(2,1)S(1)}, u32[]{:S(2)}) copy-start(bf16[2,128,768]{2,1,0:T(8,128)(2,1)S(1)} %collective-permute-done.1.halo_a) | copy-start | bytes 1179652
  31.2 57.5 %collective-permute-start.2 = (bf16[2,128,768]{2,1,0:T(8,128)(2,1)}, bf16[2,128,768]{2,1,0:T(8,128)(2,1)S(1)}, u32[]{:S(2)}, u32[]{:S(2)}) collective-permute-start(bf16[2,128,768]{2,1,0:T(8,128)(2,1)} %get-tuple-element.28), channel_id=1, source_target_pairs={{0,4},{4,0},{1,5},{5,1},{2,6},{6,2},{3,7},{7,3},{8,12},{12,8},{9,1... | collective-permute-start | bytes 1179656 | tf_op jit(solution)/shard_map/ppermute | solution.py:328
  34.0 54.8 %collective-permute-start.3 = (bf16[128,768]{1,0:T(8,128)(2,1)}, bf16[128,768]{1,0:T(8,128)(2,1)S(1)}, u32[]{:S(2)}, u32[]{:S(2)}) collective-permute-start(bf16[128,768]{1,0:T(8,128)(2,1)} %get-tuple-element.29), channel_id=1, source_target_pairs={{4,8},{8,4},{12,16},{16,12},{20,24},{24,20},{28,32},{32,28},{36,40... | collective-permute-start | bytes 589832 | tf_op jit(solution)/shard_map/ppermute | solution.py:338
  69.0 47.5 %collective-permute-start.7 = (bf16[128,768]{1,0:T(8,128)(2,1)}, bf16[128,768]{1,0:T(8,128)(2,1)}, u32[]{:S(2)}, u32[]{:S(2)}) collective-permute-start(bf16[128,768]{1,0:T(8,128)(2,1)} %get-tuple-element.40), channel_id=1, source_target_pairs={{4,8},{8,4},{12,16},{16,12},{20,24},{24,20},{28,32},{32,28},{36,40... | collective-permute-start | bytes 589832 | tf_op jit(solution)/shard_map/ppermute | solution.py:338
  88.8 0.7 copy-start
  90.7 25.8 %collective-permute-start.6 = (f32[1,768]{1,0:T(1,128)S(1)}, f32[1,768]{1,0:T(1,128)S(1)}, u32[]{:S(2)}, u32[]{:S(2)}) collective-permute-start(f32[1,768]{1,0:T(1,128)S(1)} %get-tuple-element.35.refs_0_), channel_id=1, source_target_pairs={{0,3},{1,0},{2,1},{3,2},{4,7},{5,4},{6,5},{7,6},{8,11},{9,8},{10,9... | collective-permute-start | bytes 9224 | tf_op jit(solution)/shard_map/ppermute | solution.py:382
  95.5 20.9 %collective-permute-start.5 = (f32[1,768]{1,0:T(1,128)S(1)}, f32[1,768]{1,0:T(1,128)S(1)}, u32[]{:S(2)}, u32[]{:S(2)}) collective-permute-start(f32[1,768]{1,0:T(1,128)S(1)} %get-tuple-element.35.refs_0_), channel_id=1, source_target_pairs={{0,2},{1,3},{2,0},{3,1},{4,6},{5,7},{6,4},{7,5},{8,10},{9,11},{10,... | collective-permute-start | bytes 9224 | tf_op jit(solution)/shard_map/ppermute | solution.py:382
  97.5 19.0 %collective-permute-start.4 = (f32[1,768]{1,0:T(1,128)S(1)}, f32[1,768]{1,0:T(1,128)S(1)}, u32[]{:S(2)}, u32[]{:S(2)}) collective-permute-start(f32[1,768]{1,0:T(1,128)S(1)} %get-tuple-element.35.refs_0_), channel_id=1, source_target_pairs={{0,1},{1,2},{2,3},{3,0},{4,5},{5,6},{6,7},{7,4},{8,9},{9,10},{10,1... | collective-permute-start | bytes 9224 | tf_op jit(solution)/shard_map/ppermute | solution.py:382

commit v8 on v7

--- a/solution.py
+++ b/solution.py
@@ -366,13 +366,14 @@
         halo_n,
         halo_a,
     )
-    from_across_k = swap_across(to_across_k)
     from_near = swap_near(to_near)
     for axis in ("core", "x"):
         gains = lax.psum(gains, axis)
+    gains, to_across_k = lax.optimization_barrier((gains, to_across_k))
+    from_across_k = swap_across(to_across_k)
+    gains = lax.psum(gains, "y")
     gains, to_across_v = lax.optimization_barrier((gains, to_across_v))
     from_across_v = swap_across(to_across_v)
-    gains = lax.psum(gains, "y")
     grad_key, inner = combine(
         own_k, from_near, in_hbm(from_across_k), audio_key, key_gain, in_hbm(inner_query)
     )

time: 120 us -> 120 us (level)
    psum x2, blocking collectives: 34.3 us -> 27.4 us  [on_device(): gains = lax.psum(gains, axis)]
    psum x1, blocking collectives: 18.5 us -> 23 us  [on_device(): gains = lax.psum(gains, 'y')]
    psum x1, blocking collectives: 14.7 us -> 17.8 us  [on_device(): gains = lax.psum(gains, 'far')]
where the time goes in v8:
time: 120 us; the launch traced here: 119 us
  blocking collectives  82 us (68%)
  starting transfers between devices  17.4 us (14%)
  Pallas kernels  16.4 us (14%)
  waiting for transfers between devices  1.59 us (1%)
    psum x2, blocking collectives, on_device(): gains = lax.psum(gains, axis)  27.4 us
    psum x1, blocking collectives, on_device(): gains = lax.psum(gains, 'y')  23 us
    psum x1, blocking collectives, on_device(): gains = lax.psum(gains, 'far')  17.8 us
    psum x1, blocking collectives, on_device(): totals = lax.psum(squares(video_query, audio_key), 'tp')  13.8 us
    ppermute x3, starting transfers between devices, on_device(): lax.ppermute(inner, 'tp', [(i, (i + by) % size) for i in range(size)])  10 us
    pallas_call x1, Pallas kernels, attention(): pl.pallas_call(attention_kernel, grid=(heads,), in_specs=[scalars] * 2 +...  9.62 us
    ppermute x2, starting transfers between devices, swap_near(): return lax.ppermute(value, 'core', [(0, 1), (1, 0)])  4.64 us
    pallas_call x1, Pallas kernels, norms_backward(): pl.pallas_call(kernel, grid=(1,), in_specs=[whole] * (count + 9) + [secon...  2.88 us
  transfers between devices with their start and end apart: 8, of which 1 were waited for; matrix products, arithmetic and copies ran while one was open for 0% of the time, Pallas kernels for 1%

profile of v8, /device:TPU:32, one launch (start us, length us, event | category | flops | bytes accessed | tf_op | source)
XLA Modules:
  0.0 119.0 jit_solution(1292541250097996437)
XLA Ops:
  0.6 0.0 copy-start.1
  0.6 0.0 copy-start.2
  0.7 0.0 copy-start.3
  0.7 1.5 %squares.1 = f32[1,768]{1,0:T(1,128)S(1)} custom-call(bf16[640,768]{1,0:T(8,128)(2,1)} %refs_5_.1, bf16[128,768]{1,0:T(8,128)(2,1)} %refs_8_.1), custom_call_target="tpu_custom_call" | custom-call | tf_op jit(solution)/shard_map/squares/pallas_call | solution.py:56
  2.2 13.8 %psum.35.totals = f32[1,768]{1,0:T(1,128)S(1)} all-reduce(f32[1,768]{1,0:T(1,128)S(1)} %squares.1), channel_id=1, replica_groups=mesh['y'=4,'far'=4,'x'=4,'core'=2,'tp'=4] {'tp'}, use_global_device_ids=true, to_apply=%region_0.0 | all-reduce | flops 768 | bytes 6144 | tf_op jit(solution)/shard_map/psum | solution.py:349
  16.0 1.2 norm_keys.1.held
  17.2 0.7 collective-permute-start.1
  17.9 1.9 %collective-permute-start = (bf16[2,128,768]{2,1,0:T(8,128)(2,1)S(1)}, bf16[2,128,768]{2,1,0:T(8,128)(2,1)}, u32[]{:S(2)}, u32[]{:S(2)}) collective-permute-start(bf16[2,128,768]{2,1,0:T(8,128)(2,1)S(1)} %norm_keys.1.held), channel_id=1, source_target_pairs={{0,4},{4,0},{1,5},{5,1},{2,6},{6,2},{3,7},{7,3},{8,12},{12,8},{9,1... | collective-permute-start | bytes 1179656 | tf_op jit(solution)/shard_map/ppermute | solution.py:328
  19.8 0.0 copy-done.1
  19.8 0.0 copy-done.2
  19.9 0.0 copy-done.3
  19.9 0.1 copy.13.lists
  20.0 0.1 pad_add_fusion.places
  20.0 0.0 collective-permute-done.1.halo_a
  20.0 0.0 copy-start.4
  20.0 1.6 %collective-permute-done.halo_n = bf16[2,128,768]{2,1,0:T(8,128)(2,1)} collective-permute-done((bf16[2,128,768]{2,1,0:T(8,128)(2,1)S(1)}, bf16[2,128,768]{2,1,0:T(8,128)(2,1)}, u32[]{:S(2)}, u32[]{:S(2)}) %collective-permute-start) | collective-permute-done | bytes 393248 | tf_op jit(solution)/shard_map/ppermute | solution.py:328
  21.6 0.0 copy-done.4
  21.6 9.6 %attention.1 = (bf16[640,768]{1,0:T(8,128)(2,1)}, f32[640,768]{1,0:T(8,128)S(1)}, f32[1,640]{1,0:T(1,128)}, f32[2,768]{1,0:T(2,128)}, bf16[2,128,768]{2,1,0:T(8,...) custom-call(s32[5,4]{1,0:T(8,128)S(1)} %copy.13.lists, ...), custom_call_target="tpu_custom_call" | custom-call | flops 2264924160 | bytes 4915200 | tf_op jit(solution)/shard_map/attention/pallas_call | solution.py:189
  31.2 2.7 %collective-permute-start.2 = (bf16[2,128,768]{2,1,0:T(8,128)(2,1)}, bf16[2,128,768]{2,1,0:T(8,128)(2,1)S(1)}, u32[]{:S(2)}, u32[]{:S(2)}) collective-permute-start(bf16[2,128,768]{2,1,0:T(8,128)(2,1)} %get-tuple-element.30), channel_id=1, source_target_pairs={{0,4},{4,0},{1,5},{5,1},{2,6},{6,2},{3,7},{7,3},{8,12},{12,8},{9,1... | collective-permute-start | bytes 1179656 | tf_op jit(solution)/shard_map/ppermute | solution.py:328
  34.0 2.6 %psum.36 = f32[2,768]{1,0:T(2,128)S(1)} all-reduce(f32[2,768]{1,0:T(2,128)} %get-tuple-element.31), channel_id=1, replica_groups=mesh['y'=4,'far'=4,'x'=4,'core'=2,'tp'=4] {'core'}, use_global_device_ids=true, to_apply=%region_1.0 | all-reduce | flops 1536 | bytes 12288 | tf_op jit(solution)/shard_map/psum | solution.py:371
  36.6 24.8 %psum.37 = f32[2,768]{1,0:T(2,128)S(1)} all-reduce(f32[2,768]{1,0:T(2,128)S(1)} %psum.36), channel_id=1, replica_groups=mesh['y'=4,'far'=4,'x'=4,'core'=2,'tp'=4] {'x'}, use_global_device_ids=true, to_apply=%region_2.0 | all-reduce | flops 1536 | bytes 12288 | tf_op jit(solution)/shard_map/psum | solution.py:371
  61.4 0.7 collective-permute-start.3
  62.0 23.0 %psum.38 = f32[2,768]{1,0:T(2,128)} all-reduce(f32[2,768]{1,0:T(2,128)S(1)} %psum.37), channel_id=1, replica_groups=mesh['y'=4,'far'=4,'x'=4,'core'=2,'tp'=4] {'y'}, use_global_device_ids=true, to_apply=%region_3.0 | all-reduce | flops 1536 | bytes 12288 | tf_op jit(solution)/shard_map/psum | solution.py:374
  85.0 1.3 %collective-permute-start.7 = (bf16[128,768]{1,0:T(8,128)(2,1)}, bf16[128,768]{1,0:T(8,128)(2,1)}, u32[]{:S(2)}, u32[]{:S(2)}) collective-permute-start(bf16[128,768]{1,0:T(8,128)(2,1)} %get-tuple-element.44), channel_id=1, source_target_pairs={{4,8},{8,4},{12,16},{16,12},{20,24},{24,20},{28,32},{32,28},{36,40... | collective-permute-start | bytes 589832 | tf_op jit(solution)/shard_map/ppermute | solution.py:338
  86.3 0.0 collective-permute-done.3.from_across
  86.3 0.0 copy-start
  86.3 0.0 collective-permute-done.2.from_near.refs_12_
  86.3 0.7 copy-done
  87.0 1.2 %combine.1 = (f32[128,768]{1,0:T(8,128)S(1)}, f32[1,768]{1,0:T(1,128)S(1)}) custom-call(f32[128,768]{1,0:T(8,128)S(1)} %get-tuple-element.29.own, bf16[2,128,768]{2,1,0:T(8,128)(2,1)S(1)} %collective-permute-done.2.from_near.refs_12_, bf16[128,768]{1,0:T(8,128)(2,1)} %copy-done, bf16[128,768]{1,0:T(8,128)(2,1)} %refs_8_.1, ...), custom_call_target="tpu_custom_call" | custom-call | tf_op jit(solution)/shard_map/combine/pallas_call | solution.py:246
  88.2 4.7 %collective-permute-start.6 = (f32[1,768]{1,0:T(1,128)S(1)}, f32[1,768]{1,0:T(1,128)S(1)}, u32[]{:S(2)}, u32[]{:S(2)}) collective-permute-start(f32[1,768]{1,0:T(1,128)S(1)} %get-tuple-element.39.refs_0_), channel_id=1, source_target_pairs={{0,3},{1,0},{2,1},{3,2},{4,7},{5,4},{6,5},{7,6},{8,11},{9,8},{10,9... | collective-permute-start | bytes 9224 | tf_op jit(solution)/shard_map/ppermute | solution.py:383
  93.0 1.9 %collective-permute-start.5 = (f32[1,768]{1,0:T(1,128)S(1)}, f32[1,768]{1,0:T(1,128)S(1)}, u32[]{:S(2)}, u32[]{:S(2)}) collective-permute-start(f32[1,768]{1,0:T(1,128)S(1)} %get-tuple-element.39.refs_0_), channel_id=1, source_target_pairs={{0,2},{1,3},{2,0},{3,1},{4,6},{5,7},{6,4},{7,5},{8,10},{9,11},{10,... | collective-permute-start | bytes 9224 | tf_op jit(solution)/shard_map/ppermute | solution.py:383
  94.9 3.4 %collective-permute-start.4 = (f32[1,768]{1,0:T(1,128)S(1)}, f32[1,768]{1,0:T(1,128)S(1)}, u32[]{:S(2)}, u32[]{:S(2)}) collective-permute-start(f32[1,768]{1,0:T(1,128)S(1)} %get-tuple-element.39.refs_0_), channel_id=1, source_target_pairs={{0,1},{1,2},{2,3},{3,0},{4,5},{5,6},{6,7},{7,4},{8,9},{9,10},{10,1... | collective-permute-start | bytes 9224 | tf_op jit(solution)/shard_map/ppermute | solution.py:383
  98.3 17.8 %psum.39.refs_4_ = f32[2,768]{1,0:T(2,128)S(1)} all-reduce(f32[2,768]{1,0:T(2,128)} %psum.38), channel_id=1, replica_groups=mesh['y'=4,'far'=4,'x'=4,'core'=2,'tp'=4] {'far'}, use_global_device_ids=true, to_apply=%region_4.0 | all-reduce | flops 1536 | bytes 12288 | tf_op jit(solution)/shard_map/psum | solution.py:386
  116.1 0.0 collective-permute-done.7.refs_13_
  116.1 0.0 collective-permute-done.6.refs_3_
  116.1 0.0 collective-permute-done.5.refs_2_
  116.2 0.0 collective-permute-done.4.refs_1_
  116.2 2.9 %norms_backward.1 = (bf16[640,768]{1,0:T(8,128)(2,1)}, bf16[128,768]{1,0:T(8,128)(2,1)}, bf16[128,768]{1,0:T(8,128)(2,1)}, f32[768]{0:T(1024)}, f32[768]{0:T(1024)}) custom-call(f32[1,768]{1,0:T(1,128)S(1)} %psum.35.totals, f32[1,768]{1,0:T(1,128)S(1)} %get-tuple-element.39.refs_0_, f32[1,768]{1,0:T(1,128)S(1)} %collective-permute-done.4.refs_1_, ...), custom_call_target="tpu_custom_call" | custom-call | tf_op jit(solution)/shard_map/norms_backward/pallas_call | solution.py:306
  (2 shorter events, 0.0 us)
Async XLA Ops:
  0.6 19.2 %copy-start.1 = (f32[768]{0:T(1024)S(1)}, f32[768]{0:T(1024)}, u32[]{:S(2)}) copy-start(f32[768]{0:T(1024)} %gain.1) | copy-start | bytes 9220
  0.6 19.2 %copy-start.2 = (f32[768]{0:T(1024)S(1)}, f32[768]{0:T(1024)}, u32[]{:S(2)}) copy-start(f32[768]{0:T(1024)} %param.11) | copy-start | bytes 9220
  0.7 19.2 %copy-start.3 = (s32[5,4]{0,1:T(4,128)S(1)}, s32[5,4]{0,1:T(4,128)}, u32[]{:S(2)}) copy-start(s32[5,4]{0,1:T(4,128)} %param.13) | copy-start | bytes 244
  17.2 2.9 %collective-permute-start.1 = (bf16[2,128,768]{2,1,0:T(8,128)(2,1)S(1)}, bf16[2,128,768]{2,1,0:T(8,128)(2,1)S(1)}, u32[]{:S(2)}, u32[]{:S(2)}) collective-permute-start(bf16[2,128,768]{2,1,0:T(8,128)(2,1)S(1)} %norm_keys.1.held), channel_id=1, source_target_pairs={{4,8},{8,4},{12,16},{16,12},{20,24},{24,20},{28,32},{32,28},{36,40... | collective-permute-start | bytes 1179656 | tf_op jit(solution)/shard_map/ppermute | solution.py:338
  17.9 3.7 %collective-permute-start = (bf16[2,128,768]{2,1,0:T(8,128)(2,1)S(1)}, bf16[2,128,768]{2,1,0:T(8,128)(2,1)}, u32[]{:S(2)}, u32[]{:S(2)}) collective-permute-start(bf16[2,128,768]{2,1,0:T(8,128)(2,1)S(1)} %norm_keys.1.held), channel_id=1, source_target_pairs={{0,4},{4,0},{1,5},{5,1},{2,6},{6,2},{3,7},{7,3},{8,12},{12,8},{9,1... | collective-permute-start | bytes 1179656 | tf_op jit(solution)/shard_map/ppermute | solution.py:328
  20.0 1.6 %copy-start.4 = (bf16[2,128,768]{2,1,0:T(8,128)(2,1)}, bf16[2,128,768]{2,1,0:T(8,128)(2,1)S(1)}, u32[]{:S(2)}) copy-start(bf16[2,128,768]{2,1,0:T(8,128)(2,1)S(1)} %collective-permute-done.1.halo_a) | copy-start | bytes 1179652
  31.2 55.1 %collective-permute-start.2 = (bf16[2,128,768]{2,1,0:T(8,128)(2,1)}, bf16[2,128,768]{2,1,0:T(8,128)(2,1)S(1)}, u32[]{:S(2)}, u32[]{:S(2)}) collective-permute-start(bf16[2,128,768]{2,1,0:T(8,128)(2,1)} %get-tuple-element.30), channel_id=1, source_target_pairs={{0,4},{4,0},{1,5},{5,1},{2,6},{6,2},{3,7},{7,3},{8,12},{12,8},{9,1... | collective-permute-start | bytes 1179656 | tf_op jit(solution)/shard_map/ppermute | solution.py:328
  61.4 25.0 %collective-permute-start.3 = (bf16[128,768]{1,0:T(8,128)(2,1)}, bf16[128,768]{1,0:T(8,128)(2,1)S(1)}, u32[]{:S(2)}, u32[]{:S(2)}) collective-permute-start(bf16[128,768]{1,0:T(8,128)(2,1)} %get-tuple-element.33), channel_id=1, source_target_pairs={{4,8},{8,4},{12,16},{16,12},{20,24},{24,20},{28,32},{32,28},{36,40... | collective-permute-start | bytes 589832 | tf_op jit(solution)/shard_map/ppermute | solution.py:338
  85.0 31.1 %collective-permute-start.7 = (bf16[128,768]{1,0:T(8,128)(2,1)}, bf16[128,768]{1,0:T(8,128)(2,1)}, u32[]{:S(2)}, u32[]{:S(2)}) collective-permute-start(bf16[128,768]{1,0:T(8,128)(2,1)} %get-tuple-element.44), channel_id=1, source_target_pairs={{4,8},{8,4},{12,16},{16,12},{20,24},{24,20},{28,32},{32,28},{36,40... | collective-permute-start | bytes 589832 | tf_op jit(solution)/shard_map/ppermute | solution.py:338
  86.3 0.7 copy-start
  88.2 27.9 %collective-permute-start.6 = (f32[1,768]{1,0:T(1,128)S(1)}, f32[1,768]{1,0:T(1,128)S(1)}, u32[]{:S(2)}, u32[]{:S(2)}) collective-permute-start(f32[1,768]{1,0:T(1,128)S(1)} %get-tuple-element.39.refs_0_), channel_id=1, source_target_pairs={{0,3},{1,0},{2,1},{3,2},{4,7},{5,4},{6,5},{7,6},{8,11},{9,8},{10,9... | collective-permute-start | bytes 9224 | tf_op jit(solution)/shard_map/ppermute | solution.py:383
  93.0 23.2 %collective-permute-start.5 = (f32[1,768]{1,0:T(1,128)S(1)}, f32[1,768]{1,0:T(1,128)S(1)}, u32[]{:S(2)}, u32[]{:S(2)}) collective-permute-start(f32[1,768]{1,0:T(1,128)S(1)} %get-tuple-element.39.refs_0_), channel_id=1, source_target_pairs={{0,2},{1,3},{2,0},{3,1},{4,6},{5,7},{6,4},{7,5},{8,10},{9,11},{10,... | collective-permute-start | bytes 9224 | tf_op jit(solution)/shard_map/ppermute | solution.py:383
  94.9 21.3 %collective-permute-start.4 = (f32[1,768]{1,0:T(1,128)S(1)}, f32[1,768]{1,0:T(1,128)S(1)}, u32[]{:S(2)}, u32[]{:S(2)}) collective-permute-start(f32[1,768]{1,0:T(1,128)S(1)} %get-tuple-element.39.refs_0_), channel_id=1, source_target_pairs={{0,1},{1,2},{2,3},{3,0},{4,5},{5,6},{6,7},{7,4},{8,9},{9,10},{10,1... | collective-permute-start | bytes 9224 | tf_op jit(solution)/shard_map/ppermute | solution.py:383

commit v9 on v7

--- a/solution.py
+++ b/solution.py
@@ -366,11 +366,13 @@
         halo_n,
         halo_a,
     )
-    from_across_k = swap_across(to_across_k)
     from_near = swap_near(to_near)
     for axis in ("core", "x"):
         gains = lax.psum(gains, axis)
-    gains, to_across_v = lax.optimization_barrier((gains, to_across_v))
+    gains, to_across_k, to_across_v = lax.optimization_barrier(
+        (gains, to_across_k, to_across_v)
+    )
+    from_across_k = swap_across(to_across_k)
     from_across_v = swap_across(to_across_v)
     gains = lax.psum(gains, "y")
     grad_key, inner = combine(

time: 120 us -> 123 us (1.025)
  the two profiles are of different devices: /device:TPU:32 before, /device:TPU:16 now
where the time goes in v9:
time: 123 us; the launch traced here: 122 us
  blocking collectives  53.7 us (44%)
  starting transfers between devices  33.6 us (27%)
  Pallas kernels  16.4 us (13%)
  waiting for transfers between devices  15.9 us (13%)
  local copies, waits for them, and re-layouts  1.53 us (1%)
    ppermute x3, starting transfers between devices, swap_across(): return lax.ppermute(value, LINE, pairs)  22 us
    psum x1, blocking collectives, on_device(): gains = lax.psum(gains, 'far')  17.9 us
    ppermute x3, waiting for transfers between devices, swap_across(): return lax.ppermute(value, LINE, pairs)  15.8 us
    psum x2, blocking collectives, on_device(): gains = lax.psum(gains, axis)  13.7 us
    psum x1, blocking collectives, on_device(): totals = lax.psum(squares(video_query, audio_key), 'tp')  13 us
    pallas_call x1, Pallas kernels, attention(): pl.pallas_call(attention_kernel, grid=(heads,), in_specs=[scalars] * 2 +...  9.63 us
    psum x1, blocking collectives, on_device(): gains = lax.psum(gains, 'y')  9.08 us
    ppermute x3, starting transfers between devices, on_device(): lax.ppermute(inner, 'tp', [(i, (i + by) % size) for i in range(size)])  7.76 us
  transfers between devices with their start and end apart: 8, of which 2 were waited for; matrix products, arithmetic and copies ran while one was open for 0% of the time, Pallas kernels for 1%

profile of v9, /device:TPU:16, one launch (start us, length us, event | category | flops | bytes accessed | tf_op | source)
XLA Modules:
  0.0 122.1 jit_solution(9403985394882989173)
XLA Ops:
  0.6 0.0 copy-start.1
  0.6 0.0 copy-start.2
  0.7 0.0 copy-start.3
  0.7 1.5 %squares.1 = f32[1,768]{1,0:T(1,128)S(1)} custom-call(bf16[640,768]{1,0:T(8,128)(2,1)} %refs_5_.1, bf16[128,768]{1,0:T(8,128)(2,1)} %refs_8_.1), custom_call_target="tpu_custom_call" | custom-call | tf_op jit(solution)/shard_map/squares/pallas_call | solution.py:56
  2.2 13.0 %psum.35.totals = f32[1,768]{1,0:T(1,128)S(1)} all-reduce(f32[1,768]{1,0:T(1,128)S(1)} %squares.1), channel_id=1, replica_groups=mesh['y'=4,'far'=4,'x'=4,'core'=2,'tp'=4] {'tp'}, use_global_device_ids=true, to_apply=%region_0.0 | all-reduce | flops 768 | bytes 6144 | tf_op jit(solution)/shard_map/psum | solution.py:349
  15.2 1.2 norm_keys.1.held
  16.4 9.5 %collective-permute-start.1 = (bf16[2,128,768]{2,1,0:T(8,128)(2,1)S(1)}, bf16[2,128,768]{2,1,0:T(8,128)(2,1)S(1)}, u32[]{:S(2)}, u32[]{:S(2)}) collective-permute-start(bf16[2,128,768]{2,1,0:T(8,128)(2,1)S(1)} %norm_keys.1.held), channel_id=1, source_target_pairs={{4,8},{8,4},{12,16},{16,12},{20,24},{24,20},{28,32},{32,28},{36,40... | collective-permute-start | bytes 1179656 | tf_op jit(solution)/shard_map/ppermute | solution.py:338
  25.9 1.9 %collective-permute-start = (bf16[2,128,768]{2,1,0:T(8,128)(2,1)S(1)}, bf16[2,128,768]{2,1,0:T(8,128)(2,1)}, u32[]{:S(2)}, u32[]{:S(2)}) collective-permute-start(bf16[2,128,768]{2,1,0:T(8,128)(2,1)S(1)} %norm_keys.1.held), channel_id=1, source_target_pairs={{0,4},{4,0},{1,5},{5,1},{2,6},{6,2},{3,7},{7,3},{8,12},{12,8},{9,1... | collective-permute-start | bytes 1179656 | tf_op jit(solution)/shard_map/ppermute | solution.py:328
  27.8 0.0 copy-done.1
  27.9 0.0 copy-done.2
  27.9 0.0 copy-done.3
  27.9 0.1 copy.13.lists
  28.0 0.1 pad_add_fusion.places
  28.1 12.9 %collective-permute-done.1.halo_a = bf16[2,128,768]{2,1,0:T(8,128)(2,1)S(1)} collective-permute-done((bf16[2,128,768]{2,1,0:T(8,128)(2,1)S(1)}, bf16[2,128,768]{2,1,0:T(8,128)(2,1)S(1)}, u32[]{:S(2)}, u32[]{:S(2)}) %collective-permute-start.1) | collective-permute-done | bytes 393248 | tf_op jit(solution)/shard_map/ppermute | solution.py:338
  41.0 0.0 copy-start.4
  41.0 0.0 collective-permute-done.halo_n
  41.0 0.7 copy-done.4
  41.7 9.6 %attention.1 = (bf16[640,768]{1,0:T(8,128)(2,1)}, f32[640,768]{1,0:T(8,128)S(1)}, f32[1,640]{1,0:T(1,128)}, f32[2,768]{1,0:T(2,128)}, bf16[2,128,768]{2,1,0:T(8,...) custom-call(s32[5,4]{1,0:T(8,128)S(1)} %copy.13.lists, ...), custom_call_target="tpu_custom_call" | custom-call | flops 2264924160 | bytes 4915200 | tf_op jit(solution)/shard_map/attention/pallas_call | solution.py:189
  51.3 1.9 %collective-permute-start.2 = (bf16[2,128,768]{2,1,0:T(8,128)(2,1)}, bf16[2,128,768]{2,1,0:T(8,128)(2,1)S(1)}, u32[]{:S(2)}, u32[]{:S(2)}) collective-permute-start(bf16[2,128,768]{2,1,0:T(8,128)(2,1)} %get-tuple-element.29), channel_id=1, source_target_pairs={{0,4},{4,0},{1,5},{5,1},{2,6},{6,2},{3,7},{7,3},{8,12},{12,8},{9,1... | collective-permute-start | bytes 1179656 | tf_op jit(solution)/shard_map/ppermute | solution.py:328
  53.3 2.8 %psum.36 = f32[2,768]{1,0:T(2,128)S(1)} all-reduce(f32[2,768]{1,0:T(2,128)} %get-tuple-element.30), channel_id=1, replica_groups=mesh['y'=4,'far'=4,'x'=4,'core'=2,'tp'=4] {'core'}, use_global_device_ids=true, to_apply=%region_1.0 | all-reduce | flops 1536 | bytes 12288 | tf_op jit(solution)/shard_map/psum | solution.py:371
  56.0 10.9 %psum.37 = f32[2,768]{1,0:T(2,128)S(1)} all-reduce(f32[2,768]{1,0:T(2,128)S(1)} %psum.36), channel_id=1, replica_groups=mesh['y'=4,'far'=4,'x'=4,'core'=2,'tp'=4] {'x'}, use_global_device_ids=true, to_apply=%region_2.0 | all-reduce | flops 1536 | bytes 12288 | tf_op jit(solution)/shard_map/psum | solution.py:371
  67.0 9.0 %collective-permute-start.3 = (bf16[128,768]{1,0:T(8,128)(2,1)}, bf16[128,768]{1,0:T(8,128)(2,1)S(1)}, u32[]{:S(2)}, u32[]{:S(2)}) collective-permute-start(bf16[128,768]{1,0:T(8,128)(2,1)} %get-tuple-element.33), channel_id=1, source_target_pairs={{4,8},{8,4},{12,16},{16,12},{20,24},{24,20},{28,32},{32,28},{36,40... | collective-permute-start | bytes 589832 | tf_op jit(solution)/shard_map/ppermute | solution.py:338
  76.0 3.5 %collective-permute-start.7 = (bf16[128,768]{1,0:T(8,128)(2,1)}, bf16[128,768]{1,0:T(8,128)(2,1)}, u32[]{:S(2)}, u32[]{:S(2)}) collective-permute-start(bf16[128,768]{1,0:T(8,128)(2,1)} %get-tuple-element.42), channel_id=1, source_target_pairs={{4,8},{8,4},{12,16},{16,12},{20,24},{24,20},{28,32},{32,28},{36,40... | collective-permute-start | bytes 589832 | tf_op jit(solution)/shard_map/ppermute | solution.py:338
  79.5 9.1 %psum.38 = f32[2,768]{1,0:T(2,128)} all-reduce(f32[2,768]{1,0:T(2,128)S(1)} %psum.37), channel_id=1, replica_groups=mesh['y'=4,'far'=4,'x'=4,'core'=2,'tp'=4] {'y'}, use_global_device_ids=true, to_apply=%region_3.0 | all-reduce | flops 1536 | bytes 12288 | tf_op jit(solution)/shard_map/psum | solution.py:377
  88.6 3.0 %collective-permute-done.3.from_across = bf16[128,768]{1,0:T(8,128)(2,1)S(1)} collective-permute-done((bf16[128,768]{1,0:T(8,128)(2,1)}, bf16[128,768]{1,0:T(8,128)(2,1)S(1)}, u32[]{:S(2)}, u32[]{:S(2)}) %collective-permute-start.3) | collective-permute-done | bytes 196640 | tf_op jit(solution)/shard_map/ppermute | solution.py:338
  91.5 0.0 copy-start
  91.5 0.0 collective-permute-done.2.from_near.refs_12_
  91.5 0.7 copy-done
  92.2 1.2 combine.1
  93.4 1.9 %collective-permute-start.6 = (f32[1,768]{1,0:T(1,128)S(1)}, f32[1,768]{1,0:T(1,128)S(1)}, u32[]{:S(2)}, u32[]{:S(2)}) collective-permute-start(f32[1,768]{1,0:T(1,128)S(1)} %get-tuple-element.37.refs_0_), channel_id=1, source_target_pairs={{0,3},{1,0},{2,1},{3,2},{4,7},{5,4},{6,5},{7,6},{8,11},{9,8},{10,9... | collective-permute-start | bytes 9224 | tf_op jit(solution)/shard_map/ppermute | solution.py:384
  95.3 1.9 %collective-permute-start.5 = (f32[1,768]{1,0:T(1,128)S(1)}, f32[1,768]{1,0:T(1,128)S(1)}, u32[]{:S(2)}, u32[]{:S(2)}) collective-permute-start(f32[1,768]{1,0:T(1,128)S(1)} %get-tuple-element.37.refs_0_), channel_id=1, source_target_pairs={{0,2},{1,3},{2,0},{3,1},{4,6},{5,7},{6,4},{7,5},{8,10},{9,11},{10,... | collective-permute-start | bytes 9224 | tf_op jit(solution)/shard_map/ppermute | solution.py:384
  97.3 3.9 %collective-permute-start.4 = (f32[1,768]{1,0:T(1,128)S(1)}, f32[1,768]{1,0:T(1,128)S(1)}, u32[]{:S(2)}, u32[]{:S(2)}) collective-permute-start(f32[1,768]{1,0:T(1,128)S(1)} %get-tuple-element.37.refs_0_), channel_id=1, source_target_pairs={{0,1},{1,2},{2,3},{3,0},{4,5},{5,6},{6,7},{7,4},{8,9},{9,10},{10,1... | collective-permute-start | bytes 9224 | tf_op jit(solution)/shard_map/ppermute | solution.py:384
  101.2 17.9 %psum.39.refs_4_ = f32[2,768]{1,0:T(2,128)S(1)} all-reduce(f32[2,768]{1,0:T(2,128)} %psum.38), channel_id=1, replica_groups=mesh['y'=4,'far'=4,'x'=4,'core'=2,'tp'=4] {'far'}, use_global_device_ids=true, to_apply=%region_4.0 | all-reduce | flops 1536 | bytes 12288 | tf_op jit(solution)/shard_map/psum | solution.py:387
  119.2 0.0 collective-permute-done.7.refs_13_
  119.2 0.0 collective-permute-done.6.refs_3_
  119.2 0.0 collective-permute-done.5.refs_2_
  119.2 0.0 collective-permute-done.4.refs_1_
  119.2 2.9 %norms_backward.1 = (bf16[640,768]{1,0:T(8,128)(2,1)}, bf16[128,768]{1,0:T(8,128)(2,1)}, bf16[128,768]{1,0:T(8,128)(2,1)}, f32[768]{0:T(1024)}, f32[768]{0:T(1024)}) custom-call(f32[1,768]{1,0:T(1,128)S(1)} %psum.35.totals, f32[1,768]{1,0:T(1,128)S(1)} %get-tuple-element.37.refs_0_, f32[1,768]{1,0:T(1,128)S(1)} %collective-permute-done.4.refs_1_, ...), custom_call_target="tpu_custom_call" | custom-call | tf_op jit(solution)/shard_map/norms_backward/pallas_call | solution.py:306
  (2 shorter events, 0.0 us)
Async XLA Ops:
  0.6 27.2 %copy-start.1 = (f32[768]{0:T(1024)S(1)}, f32[768]{0:T(1024)}, u32[]{:S(2)}) copy-start(f32[768]{0:T(1024)} %gain.1) | copy-start | bytes 9220
  0.6 27.2 %copy-start.2 = (f32[768]{0:T(1024)S(1)}, f32[768]{0:T(1024)}, u32[]{:S(2)}) copy-start(f32[768]{0:T(1024)} %param.11) | copy-start | bytes 9220
  0.7 27.3 %copy-start.3 = (s32[5,4]{0,1:T(4,128)S(1)}, s32[5,4]{0,1:T(4,128)}, u32[]{:S(2)}) copy-start(s32[5,4]{0,1:T(4,128)} %param.13) | copy-start | bytes 244
  16.4 24.6 %collective-permute-start.1 = (bf16[2,128,768]{2,1,0:T(8,128)(2,1)S(1)}, bf16[2,128,768]{2,1,0:T(8,128)(2,1)S(1)}, u32[]{:S(2)}, u32[]{:S(2)}) collective-permute-start(bf16[2,128,768]{2,1,0:T(8,128)(2,1)S(1)} %norm_keys.1.held), channel_id=1, source_target_pairs={{4,8},{8,4},{12,16},{16,12},{20,24},{24,20},{28,32},{32,28},{36,40... | collective-permute-start | bytes 1179656 | tf_op jit(solution)/shard_map/ppermute | solution.py:338
  25.9 15.0 %collective-permute-start = (bf16[2,128,768]{2,1,0:T(8,128)(2,1)S(1)}, bf16[2,128,768]{2,1,0:T(8,128)(2,1)}, u32[]{:S(2)}, u32[]{:S(2)}) collective-permute-start(bf16[2,128,768]{2,1,0:T(8,128)(2,1)S(1)} %norm_keys.1.held), channel_id=1, source_target_pairs={{0,4},{4,0},{1,5},{5,1},{2,6},{6,2},{3,7},{7,3},{8,12},{12,8},{9,1... | collective-permute-start | bytes 1179656 | tf_op jit(solution)/shard_map/ppermute | solution.py:328
  41.0 0.7 copy-start.4
  51.3 40.2 %collective-permute-start.2 = (bf16[2,128,768]{2,1,0:T(8,128)(2,1)}, bf16[2,128,768]{2,1,0:T(8,128)(2,1)S(1)}, u32[]{:S(2)}, u32[]{:S(2)}) collective-permute-start(bf16[2,128,768]{2,1,0:T(8,128)(2,1)} %get-tuple-element.29), channel_id=1, source_target_pairs={{0,4},{4,0},{1,5},{5,1},{2,6},{6,2},{3,7},{7,3},{8,12},{12,8},{9,1... | collective-permute-start | bytes 1179656 | tf_op jit(solution)/shard_map/ppermute | solution.py:328
  67.0 24.5 %collective-permute-start.3 = (bf16[128,768]{1,0:T(8,128)(2,1)}, bf16[128,768]{1,0:T(8,128)(2,1)S(1)}, u32[]{:S(2)}, u32[]{:S(2)}) collective-permute-start(bf16[128,768]{1,0:T(8,128)(2,1)} %get-tuple-element.33), channel_id=1, source_target_pairs={{4,8},{8,4},{12,16},{16,12},{20,24},{24,20},{28,32},{32,28},{36,40... | collective-permute-start | bytes 589832 | tf_op jit(solution)/shard_map/ppermute | solution.py:338
  76.0 43.2 %collective-permute-start.7 = (bf16[128,768]{1,0:T(8,128)(2,1)}, bf16[128,768]{1,0:T(8,128)(2,1)}, u32[]{:S(2)}, u32[]{:S(2)}) collective-permute-start(bf16[128,768]{1,0:T(8,128)(2,1)} %get-tuple-element.42), channel_id=1, source_target_pairs={{4,8},{8,4},{12,16},{16,12},{20,24},{24,20},{28,32},{32,28},{36,40... | collective-permute-start | bytes 589832 | tf_op jit(solution)/shard_map/ppermute | solution.py:338
  91.5 0.7 copy-start
  93.4 25.7 %collective-permute-start.6 = (f32[1,768]{1,0:T(1,128)S(1)}, f32[1,768]{1,0:T(1,128)S(1)}, u32[]{:S(2)}, u32[]{:S(2)}) collective-permute-start(f32[1,768]{1,0:T(1,128)S(1)} %get-tuple-element.37.refs_0_), channel_id=1, source_target_pairs={{0,3},{1,0},{2,1},{3,2},{4,7},{5,4},{6,5},{7,6},{8,11},{9,8},{10,9... | collective-permute-start | bytes 9224 | tf_op jit(solution)/shard_map/ppermute | solution.py:384
  95.3 23.8 %collective-permute-start.5 = (f32[1,768]{1,0:T(1,128)S(1)}, f32[1,768]{1,0:T(1,128)S(1)}, u32[]{:S(2)}, u32[]{:S(2)}) collective-permute-start(f32[1,768]{1,0:T(1,128)S(1)} %get-tuple-element.37.refs_0_), channel_id=1, source_target_pairs={{0,2},{1,3},{2,0},{3,1},{4,6},{5,7},{6,4},{7,5},{8,10},{9,11},{10,... | collective-permute-start | bytes 9224 | tf_op jit(solution)/shard_map/ppermute | solution.py:384
  97.3 21.9 %collective-permute-start.4 = (f32[1,768]{1,0:T(1,128)S(1)}, f32[1,768]{1,0:T(1,128)S(1)}, u32[]{:S(2)}, u32[]{:S(2)}) collective-permute-start(f32[1,768]{1,0:T(1,128)S(1)} %get-tuple-element.37.refs_0_), channel_id=1, source_target_pairs={{0,1},{1,2},{2,3},{3,0},{4,5},{5,6},{6,7},{7,4},{8,9},{9,10},{10,1... | collective-permute-start | bytes 9224 | tf_op jit(solution)/shard_map/ppermute | solution.py:384
